TPU v7x, 1024 devices: a whole 4x4x32 slice. The times are simulated.
1024 devices in a mesh: row: 16 (over z_hi, y), col: 64 (over z_lo, x, core).
Axes of the slice: x: 4, y: 4, z: 32 (z_hi: 4, z_lo: 8; z = z_hi * 8 + z_lo), core: 2. Of those that a mesh axis runs over, the one named last changes fastest.
Arguments:
- inputs: bfloat16 [512, 8192], P('col', 'row'), may hold values from -6 to 6
- cotangent: bfloat16 [512, 8192], P('col', 'row'), may hold values from -6 to 6
- gate_weight: bfloat16 [8192, 28672], P('row', 'col'), may hold values from -0.09375 to 0.09375
- up_weight: bfloat16 [8192, 28672], P('row', 'col'), may hold values from -0.09375 to 0.09375
- down_weight: bfloat16 [28672, 8192], P('col', 'row'), may hold values from -0.046875 to 0.046875
- gate_pattern: int32 [2048, 28672], P('row', 'col'), may hold values from 0 to 5
- up_pattern: int32 [2048, 28672], P('row', 'col'), may hold values from 0 to 5
- down_pattern: int32 [7168, 8192], P('col', 'row'), may hold values from 0 to 5
Outputs:
- grad_inputs: bfloat16 [512, 8192], P('col', 'row')
- grad_gate_weight: bfloat16 [8192, 28672], P('row', 'col')
- grad_up_weight: bfloat16 [8192, 28672], P('row', 'col')
- grad_down_weight: bfloat16 [28672, 8192], P('col', 'row')
All inputs are finite; a program needn't handle non-finite values.
Results may differ from a plain program's by a relative error of at most 0.0049.
Values may be sent and summed in bfloat16 or wider, within the bound.
No kernel may reach another device: no remote copies, remote signals or barrier semaphores. Data moves between devices by JAX's collectives and lax.ppermute only.
A program may use at most 32 MiB of HBM per device.

v0:
```python
import functools

import jax
import jax.numpy as jnp
from jax import lax
from jax.sharding import PartitionSpec as P

keep_sets = ((0, 1, 2), (0, 3, 4), (1, 3, 5), (2, 4, 5))


def expand_keep(pattern):
    planes = [
        functools.reduce(jnp.logical_or, [pattern == member for member in group_set])
        for group_set in keep_sets
    ]
    return jnp.stack(planes, axis=1).reshape(pattern.shape[0] * 4, pattern.shape[1])


def swiglu_back(gate_pre, up_pre, hidden_grad):
    sigmoid_gate = jax.nn.sigmoid(gate_pre)
    silu_gate = gate_pre * sigmoid_gate
    hidden = (silu_gate * up_pre).astype(jnp.bfloat16)
    up_grad = (hidden_grad * silu_gate).astype(jnp.bfloat16)
    gate_grad = (
        hidden_grad * up_pre * sigmoid_gate * (1.0 + gate_pre * (1.0 - sigmoid_gate))
    ).astype(jnp.bfloat16)
    return (hidden, gate_grad, up_grad)


def contract_rows(left_mat, right_mat):
    return lax.dot_general(
        left_mat, right_mat, (((0,), (0,)), ((), ())), preferred_element_type=jnp.float32
    )


def contract_cols(left_mat, right_mat):
    return lax.dot_general(
        left_mat, right_mat, (((1,), (1,)), ((), ())), preferred_element_type=jnp.float32
    )


def body(
    inputs, cotangent, gate_weight, up_weight, down_weight, gate_pattern, up_pattern, down_pattern
):
    gate_keep = expand_keep(gate_pattern)
    up_keep = expand_keep(up_pattern)
    down_keep = expand_keep(down_pattern)
    gate_eff = jnp.where(gate_keep, gate_weight, jnp.zeros_like(gate_weight))
    up_eff = jnp.where(up_keep, up_weight, jnp.zeros_like(up_weight))
    down_eff = jnp.where(down_keep, down_weight, jnp.zeros_like(down_weight))
    tokens, grad_out = (
        lax.all_gather(inputs, "col", axis=0, tiled=True),
        lax.all_gather(cotangent, "col", axis=0, tiled=True),
    )
    hidden_cols = gate_weight.shape[1]
    gate_pre = jnp.dot(tokens, gate_eff, preferred_element_type=jnp.float32)
    up_pre = jnp.dot(tokens, up_eff, preferred_element_type=jnp.float32)
    hidden_grad = contract_cols(grad_out, down_eff)
    summed = lax.psum(jnp.concatenate([gate_pre, up_pre, hidden_grad], axis=1), "row")
    hidden, gate_grad, up_grad = swiglu_back(
        summed[:, :hidden_cols],
        summed[:, hidden_cols : 2 * hidden_cols],
        summed[:, 2 * hidden_cols :],
    )
    grad_gate_weight = jnp.where(gate_keep, contract_rows(tokens, gate_grad), 0.0).astype(
        jnp.bfloat16
    )
    grad_up_weight = jnp.where(up_keep, contract_rows(tokens, up_grad), 0.0).astype(jnp.bfloat16)
    grad_down_weight = jnp.where(down_keep, contract_rows(hidden, grad_out), 0.0).astype(
        jnp.bfloat16
    )
    grad_inputs = lax.psum_scatter(
        contract_cols(gate_grad, gate_eff) + contract_cols(up_grad, up_eff),
        "col",
        scatter_dimension=0,
        tiled=True,
    ).astype(jnp.bfloat16)
    return (grad_inputs, grad_gate_weight, grad_up_weight, grad_down_weight)


def solution(mesh):
    return jax.shard_map(
        body,
        mesh=mesh,
        in_specs=(
            P("col", "row"),
            P("col", "row"),
            P("row", "col"),
            P("row", "col"),
            P("col", "row"),
            P("row", "col"),
            P("row", "col"),
            P("col", "row"),
        ),
        out_specs=(P("col", "row"), P("row", "col"), P("row", "col"), P("col", "row")),
        check_vma=False,
    )
```

profile of v0, /device:TPU:8, one launch (start us, length us, event | category | flops | bytes accessed | tf_op | source)
XLA Modules:
  0.0 1299.3 jit_solution(15686132151767270608)
XLA Ops:
  7.2 0.0 copy-start.7
  7.2 0.0 all-reduce.2.cloned.1.call-start
  7.2 1.1 or_bitcast_fusion.7
  8.4 1.0 or_bitcast_fusion.6
  9.4 1.0 or_bitcast_fusion.5
  10.4 0.1 or_bitcast_fusion.4
  10.5 0.0 copy-start.5
  10.5 0.5 copy.17
  11.0 0.3 reshape.18
  11.4 0.0 copy-start.1
  11.4 127.1 %all_gather.6 = bf16[512,512]{1,0:T(8,128)(2,1)S(1)} all-gather(bf16[8,512]{1,0:T(8,128)(2,1)S(1)} %copy-done.7), channel_id=1, replica_groups=mesh['row'=16,'col'=64] {'col'}, dimensions={0}, use_global_device_ids=true | all-gather | bytes 532480 | tf_op jit(solution)/shard_map/all_gather | solution.py:52
  138.5 0.2 copy.18
  138.7 0.1 or_bitcast_fusion.11
  138.8 0.1 or_bitcast_fusion.10
  138.9 0.1 or_bitcast_fusion.9
  139.0 0.1 or_bitcast_fusion.8
  139.1 0.0 copy-start.8
  139.1 0.5 copy.15
  139.6 0.3 reshape.17
  140.0 0.2 copy.16
  140.2 0.1 or_bitcast_fusion.3
  140.3 0.1 or_bitcast_fusion.2
  140.4 0.1 or_bitcast_fusion.1
  140.5 0.1 or_bitcast_fusion
  140.6 0.2 copy.19
  140.8 0.0 copy-start.6
  140.8 0.2 reshape.19
  141.1 0.0 copy-done.8
  141.1 0.0 copy-start.2
  141.1 113.8 %all_gather.7 = bf16[512,512]{1,0:T(8,128)(2,1)S(1)} all-gather(bf16[8,512]{1,0:T(8,128)(2,1)S(1)} %copy-done.8), channel_id=1, replica_groups=mesh['row'=16,'col'=64] {'col'}, dimensions={0}, use_global_device_ids=true | all-gather | bytes 532480 | tf_op jit(solution)/shard_map/all_gather | solution.py:53
  254.9 0.5 convolution_bitcast_fusion.3
  255.4 0.5 convolution_bitcast_fusion.4
  255.9 0.4 convolution_bitcast_fusion.2
  256.4 1.8 pad_maximum_fusion
  258.2 0.0 all-reduce.2.cloned.1.call-update
  258.2 0.0 reduce-scatter.2.cloned.1.call-start
  258.3 569.9 %all-reduce.2.cloned.1.call-done = f32[512,1344]{0,1:T(8,128)} async-done(((f32[512,1344]{0,1:T(8,128)}), f32[512,1344]{0,1:T(8,128)}) %all-reduce.2.cloned.1.call-update) | async-done | bytes 2752528 | tf_op jit(solution)/shard_map/psum | solution.py:59
  828.2 2.3 multiply_convert_fusion.1
  830.5 0.5 fusion.7
  831.0 1.5 convolution_add_fusion
  832.5 0.0 reduce-scatter.2.cloned.1.call-update
  832.5 0.3 copy.21
  832.8 0.3 copy.20
  833.2 1.2 fusion.3
  834.3 1.2 fusion.2
  835.5 2.6 fusion.4
  838.2 453.0 %reduce-scatter.2.cloned.1.call-done = f32[8,512]{1,0:T(8,128)} async-done(((f32[512,512]{1,0:T(8,128)}), f32[8,512]{1,0:T(8,128)}) %reduce-scatter.2.cloned.1.call-update) | async-done | bytes 16400 | tf_op jit(solution)/shard_map/reduce_scatter | solution.py:72
  1291.1 1.3 convert_element_type.23
  (14 shorter events, 0.1 us)
Async XLA Ops:
  7.2 4.2 copy-start.7
  7.2 131.3 %copy-start.4 = (bf16[512,448]{0,1:T(8,128)(2,1)S(1)}, bf16[512,448]{0,1:T(8,128)(2,1)}, u32[]{:S(2)}) copy-start(bf16[512,448]{0,1:T(8,128)(2,1)} %param.11) | copy-start | bytes 1376260
  7.2 131.5 %copy-start = (s32[128,448]{0,1:T(8,128)S(1)}, s32[128,448]{0,1:T(8,128)}, u32[]{:S(2)}) copy-start(s32[128,448]{0,1:T(8,128)} %param.13) | copy-start | bytes 688132
  7.2 821.0 %all-reduce.2.cloned.1.call-start = ((), (), s32[]{:S(2)}) async-start(), calls=%async_computation.1 | async-start | bytes 5505024 | tf_op jit(solution)/shard_map/psum | solution.py:59
  10.5 129.4 %copy-start.5 = (bf16[512,448]{0,1:T(8,128)(2,1)S(1)}, bf16[512,448]{0,1:T(8,128)(2,1)}, u32[]{:S(2)}) copy-start(bf16[512,448]{0,1:T(8,128)(2,1)} %param.10) | copy-start | bytes 1376260
  11.4 128.8 %copy-start.1 = (s32[112,512]{1,0:T(8,128)S(1)}, s32[112,512]{1,0:T(8,128)}, u32[]{:S(2)}) copy-start(s32[112,512]{1,0:T(8,128)} %param.15) | copy-start | bytes 688132
  139.1 2.0 copy-start.8
  140.8 115.1 %copy-start.6 = (bf16[448,512]{1,0:T(8,128)(2,1)S(1)}, bf16[448,512]{1,0:T(8,128)(2,1)}, u32[]{:S(2)}) copy-start(bf16[448,512]{1,0:T(8,128)(2,1)} %param.12) | copy-start | bytes 1376260
  141.1 115.3 %copy-start.2 = (pred[448,512]{1,0:T(32,128)(4,1)}, pred[448,512]{1,0:T(32,128)(4,1)S(1)}, u32[]{:S(2)}) copy-start(pred[448,512]{1,0:T(32,128)(4,1)S(1)} %reshape.19) | copy-start | bytes 688132
  258.2 1032.9 %reduce-scatter.2.cloned.1.call-start = ((), (), s32[]{:S(2)}) async-start(), calls=%async_computation.2 | async-start | bytes 1064960 | tf_op jit(solution)/shard_map/reduce_scatter | solution.py:72
  832.5 3.0 copy-start.3
Sparse Core Ops, SparseCore 0:
  258.4 569.8 all-reduce.1
  832.6 458.4 reduce-scatter.1
where the time goes:
time: 1300 us
  waiting for transfers between devices  1020 us (78%)
  blocking collectives  241 us (19%)
  between operations  14.3 us (1%)
    psum x1, waiting for transfers between devices, body(): lax.psum(jnp.concatenate([gate_pre, up_pre, hidden_grad], axis=1), 'row')  570 us
    reduce_scatter x1, waiting for transfers between devices, body(): lax.psum_scatter(contract_cols(gate_grad, gate_eff) + contract_cols(up_gr...  453 us
    all_gather x1, blocking collectives, body(): lax.all_gather(inputs, 'col', axis=0, tiled=True)  127 us
    all_gather x1, blocking collectives, body(): lax.all_gather(cotangent, 'col', axis=0, tiled=True)  114 us
  transfers between devices with their start and end apart: 2, of which 2 were waited for; matrix products, arithmetic and copies ran while one was open for 0% of the time, Pallas kernels for 0%

commit v1 on v0

v1 whole, which is shorter than its diff:
```python
import jax
import jax.numpy as jnp
import numpy as np
from jax import lax
from jax.sharding import Mesh, PartitionSpec as P

bf16 = jnp.bfloat16
f32 = jnp.float32
keep_sets = ((0, 1, 2), (0, 3, 4), (1, 3, 5), (2, 4, 5))


def keep_planes(pattern):
    planes = []
    for members in keep_sets:
        kept = pattern == members[0]
        for member in members[1:]:
            kept = kept | (pattern == member)
        planes.append(kept.astype(bf16))
    return planes


def spread_matrix(groups):
    row = lax.broadcasted_iota(jnp.int32, (4 * groups, 4 * groups), 0)
    col = lax.broadcasted_iota(jnp.int32, (4 * groups, 4 * groups), 1)
    return ((row % groups) * 4 + row // groups == col).astype(bf16)


def dot(a, b, dims):
    return lax.dot_general(a, b, (dims, ((), ())), preferred_element_type=f32)


def gather_by_exchange(block, axis, size):
    return lax.all_to_all(jnp.broadcast_to(block[None], (size, *block.shape)), axis, 0, 0)


def swiglu_back(gate_pre, up_pre, hidden_grad):
    sigmoid_gate = jax.nn.sigmoid(gate_pre)
    silu_gate = gate_pre * sigmoid_gate
    hidden = (silu_gate * up_pre).astype(bf16)
    up_grad = (hidden_grad * silu_gate).astype(bf16)
    gate_grad = (
        hidden_grad * up_pre * sigmoid_gate * (1.0 + gate_pre * (1.0 - sigmoid_gate))
    ).astype(bf16)
    return jnp.stack([hidden, gate_grad, up_grad])


def body(inputs, cotangent, gate_weight, up_weight, down_weight, gate_pattern, up_pattern, down_pattern):
    sizes = {"zhi": 4, "y": 4, "zlo": 8, "x": 4, "core": 2}
    rows, width = inputs.shape
    hidden_units = down_weight.shape[0]
    tokens_all = rows * sizes["zlo"] * sizes["x"] * sizes["core"]

    both = jnp.stack([inputs, cotangent])
    both = gather_by_exchange(both, "zlo", sizes["zlo"])
    both = gather_by_exchange(both, "x", sizes["x"])
    both = both.transpose(2, 0, 1, 3, 4).reshape(2, tokens_all // 2, width)
    tokens = lax.all_gather(both[0], "core", axis=0, tiled=True)
    grad_out = lax.all_gather(both[1], "core", axis=0, tiled=True)

    spread_width = spread_matrix(width // 4)
    spread_units = spread_matrix(hidden_units // 4)
    gate_keep = dot(jnp.concatenate(keep_planes(gate_pattern.T), axis=1), spread_width, ((1,), (0,))) > 0.5
    up_keep = dot(jnp.concatenate(keep_planes(up_pattern.T), axis=1), spread_width, ((1,), (0,))) > 0.5
    down_keep = dot(spread_units, jnp.concatenate(keep_planes(down_pattern), axis=0), ((0,), (0,))) > 0.5
    zero = jnp.zeros((), bf16)
    gate_eff = jnp.where(gate_keep, gate_weight.T, zero)
    up_eff = jnp.where(up_keep, up_weight.T, zero)
    down_eff = jnp.where(down_keep, down_weight, zero)

    ny, nz = sizes["y"], sizes["zhi"]
    quarter, strip = hidden_units // ny, tokens_all // nz
    partial = jnp.stack(
        [
            dot(gate_eff, tokens, ((1,), (1,))).reshape(ny, quarter, tokens_all),
            dot(up_eff, tokens, ((1,), (1,))).reshape(ny, quarter, tokens_all),
            dot(down_eff, grad_out, ((1,), (1,))).reshape(ny, quarter, tokens_all),
        ],
        axis=1,
    )
    summed = lax.all_to_all(partial, "y", 0, 0).sum(axis=0)
    strips = summed.astype(bf16).reshape(3, quarter, nz, strip).transpose(2, 0, 1, 3)
    summed = lax.all_to_all(strips, "zhi", 0, 0).astype(f32).sum(axis=0)
    triple = swiglu_back(summed[0], summed[1], summed[2])
    triple = gather_by_exchange(triple, "zhi", nz)
    triple = gather_by_exchange(triple, "y", ny)
    triple = triple.transpose(2, 0, 3, 1, 4).reshape(3, hidden_units, tokens_all)
    hidden, gate_grad, up_grad = triple[0], triple[1], triple[2]

    half = tokens_all // 2
    back = dot(gate_grad, gate_eff, ((0,), (0,))) + dot(up_grad, up_eff, ((0,), (0,)))
    back = back.reshape(2, half, width)
    core = lax.axis_index("core")
    kept = jnp.where(core == 0, back[0], back[1])
    sent = jnp.where(core == 0, back[1], back[0])
    back = kept + lax.ppermute(sent, "core", [(0, 1), (1, 0)])
    back = lax.all_to_all(back.reshape(sizes["x"], half // sizes["x"], width), "x", 0, 0).sum(axis=0)
    back = lax.all_to_all(back.reshape(sizes["zlo"], rows, width), "zlo", 0, 0).sum(axis=0)

    grad_gate = jnp.where(gate_keep, dot(gate_grad, tokens, ((1,), (0,))), 0.0).astype(bf16)
    grad_up = jnp.where(up_keep, dot(up_grad, tokens, ((1,), (0,))), 0.0).astype(bf16)
    grad_down = jnp.where(down_keep, dot(hidden, grad_out, ((1,), (0,))), 0.0).astype(bf16)
    return (back.astype(bf16), grad_gate.T, grad_up.T, grad_down)


def solution(mesh):
    fine = Mesh(
        np.asarray(mesh.devices).reshape(4, 4, 8, 4, 2), ("zhi", "y", "zlo", "x", "core")
    )
    row, col = ("zhi", "y"), ("zlo", "x", "core")
    return jax.shard_map(
        body,
        mesh=fine,
        in_specs=(
            P(col, row),
            P(col, row),
            P(row, col),
            P(row, col),
            P(col, row),
            P(row, col),
            P(row, col),
            P(col, row),
        ),
        out_specs=(P(col, row), P(row, col), P(row, col), P(col, row)),
        check_vma=False,
    )
```

time: 1300 us -> 260 us (0.20)
  the two profiles are of different devices: /device:TPU:8 before, /device:TPU:6 now
where the time goes in v1:
time: 260 us; the launch traced here: 259 us
  blocking collectives  163 us (63%)
  starting transfers between devices  35.4 us (14%)
  waiting for transfers between devices  34.6 us (13%)
  other arithmetic  9.6 us (4%)
  matrix products  9.23 us (4%)
  local copies, waits for them, and re-layouts  5.77 us (2%)
    all_to_all x1, blocking collectives, body(): summed = lax.all_to_all(strips, 'zhi', 0, 0).astype(f32).sum(axis=0)  56.4 us
    all_to_all x1, blocking collectives, gather_by_exchange(): lax.all_to_all(jnp.broadcast_to(block[None], (size, *block.shape)), axis,...  53.1 us
    all_to_all x1, blocking collectives, body(): summed = lax.all_to_all(partial, 'y', 0, 0).sum(axis=0)  36.4 us
    all_to_all x3, waiting for transfers between devices, gather_by_exchange(): lax.all_to_all(jnp.broadcast_to(block[None], (size, *block.shape)), axis,...  24.7 us
    all_to_all x3, starting transfers between devices, gather_by_exchange(): lax.all_to_all(jnp.broadcast_to(block[None], (size, *block.shape)), axis,...  23 us
    all_to_all x1, blocking collectives, body(): lax.all_to_all(back.reshape(sizes['x'], half // sizes['x'], width), 'x',...  12.5 us
    all_to_all x1, starting transfers between devices, body(): lax.all_to_all(back.reshape(sizes['zlo'], rows, width), 'zlo', 0, 0)  10.4 us
    dot_general x11, matrix products, dot(): return lax.dot_general(a, b, (dims, ((), ())), preferred_element_type=f32)  9.23 us
  transfers between devices with their start and end apart: 5, of which 5 were waited for; matrix products, arithmetic and copies ran while one was open for 5% of the time, Pallas kernels for 0%

profile of v1, /device:TPU:6, one launch (start us, length us, event | category | flops | bytes accessed | tf_op | source)
XLA Modules:
  0.0 258.5 jit_solution(12973947186396006714)
XLA Ops:
  0.7 0.8 pad_maximum_fusion.2
  1.5 0.7 broadcast_in_dim.39
  2.1 12.5 %all-to-all-start = ((bf16[8,2,8,512]{3,2,1,0:T(8,128)(2,1)}), bf16[8,2,8,512]{3,2,1,0:T(8,128)(2,1)S(1)}, u32[]{:S(2)}, u32[]{:S(2)}) async-start(bf16[8,2,8,512]{3,2,1,0:T(8,128)(2,1)} %broadcast_in_dim.39), calls=%async_computation | async-start | bytes 262144 | tf_op jit(solution)/shard_map/all_to_all | solution.py:33
  14.7 1.1 or_bitcast_fusion.7
  15.8 1.0 or_bitcast_fusion.6
  16.8 1.1 or_bitcast_fusion.3
  17.9 1.1 or_or_fusion.3
  19.0 1.0 or_or_fusion.2
  20.0 0.1 or_bitcast_fusion.5
  20.1 0.1 or_or_fusion.1
  20.3 0.1 or_bitcast_fusion.2
  20.5 0.9 convolution_compare_fusion
  21.4 0.8 convolution_compare_fusion.2
  22.2 4.4 %all-to-all-done = bf16[8,2,8,512]{3,2,1,0:T(8,128)(2,1)S(1)} async-done(((bf16[8,2,8,512]{3,2,1,0:T(8,128)(2,1)}), bf16[8,2,8,512]{3,2,1,0:T(8,128)(2,1)S(1)}, u32[]{:S(2)}, u32[]{:S(2)}) %all-to-all-start) | async-done | bytes 131104 | tf_op jit(solution)/shard_map/all_to_all | solution.py:33
  26.6 0.9 broadcast_in_dim.40
  27.5 6.8 %all-to-all-start.1 = ((bf16[4,8,2,8,512]{4,3,2,1,0:T(8,128)(2,1)}), bf16[4,8,2,8,512]{4,3,2,1,0:T(8,128)(2,1)S(1)}, u32[]{:S(2)}, u32[]{:S(2)}) async-start(bf16[4,8,2,8,512]{4,3,2,1,0:T(8,128)(2,1)} %broadcast_in_dim.40), calls=%async_computation.1 | async-start | bytes 1048576 | tf_op jit(solution)/shard_map/all_to_all | solution.py:33
  34.5 0.8 convolution_compare_fusion.1
  35.3 5.1 %all-to-all-done.1 = bf16[4,8,2,8,512]{4,3,2,1,0:T(8,128)(2,1)S(1)} async-done(((bf16[4,8,2,8,512]{4,3,2,1,0:T(8,128)(2,1)}), bf16[4,8,2,8,512]{4,3,2,1,0:T(8,128)(2,1)S(1)}, u32[]{:S(2)}, u32[]{:S(2)}) %all-to-all-start.1) | async-done | bytes 524320 | tf_op jit(solution)/shard_map/all_to_all | solution.py:33
  40.4 2.3 all_gather.6
  42.7 2.2 all_gather.7
  44.9 0.4 fusion.44
  45.3 0.4 fusion.45
  45.8 0.4 fusion.31
  46.2 0.3 pad_maximum_fusion
  46.5 36.4 %all_to_all.40 = f32[4,3,112,512]{3,2,1,0:T(8,128)S(1)} all-to-all(f32[4,3,112,512]{3,2,1,0:T(8,128)S(1)} %pad_maximum_fusion), channel_id=1, replica_groups=mesh['zhi'=4,'y'=4,'zlo'=8,'x'=4,'core'=2] {'y'}, dimensions={0} | all-to-all | bytes 5505024 | tf_op jit(solution)/shard_map/all_to_all | solution.py:80
  82.9 1.1 reduce_sum.36
  84.0 1.1 convert_element_type.67
  85.2 56.4 %all_to_all.41 = bf16[4,3,112,128]{3,2,1,0:T(8,128)(2,1)S(1)} all-to-all(bf16[4,3,112,128]{3,2,1,0:T(8,128)(2,1)S(1)} %copy.24), channel_id=1, replica_groups=mesh['zhi'=4,'y'=4,'zlo'=8,'x'=4,'core'=2] {'zhi'}, dimensions={0} | all-to-all | bytes 688128 | tf_op jit(solution)/shard_map/all_to_all | solution.py:82
  141.7 53.1 %all_to_all.42 = bf16[4,3,112,128]{3,2,1,0:T(8,128)(2,1)S(1)} all-to-all(bf16[4,3,112,128]{3,2,1,0:T(8,128)(2,1)S(1)} %broadcast_in_dim.41), channel_id=1, replica_groups=mesh['zhi'=4,'y'=4,'zlo'=8,'x'=4,'core'=2] {'zhi'}, dimensions={0} | all-to-all | bytes 688128 | tf_op jit(solution)/shard_map/all_to_all | solution.py:33
  194.8 0.1 copy.25
  195.0 1.6 broadcast_in_dim.42
  196.5 3.7 %all-to-all-start.5 = ((bf16[4,4,3,112,128]{4,1,3,2,0:T(4,128)(2,1)}), bf16[4,4,3,112,128]{4,1,3,2,0:T(4,128)(2,1)S(1)}, u32[]{:S(2)}, u32[]{:S(2)}) async-start(bf16[4,4,3,112,128]{4,1,3,2,0:T(4,128)(2,1)} %broadcast_in_dim.42), calls=%async_computation.5 | async-start | bytes 2752512 | tf_op jit(solution)/shard_map/all_to_all | solution.py:33
  200.2 15.2 %all-to-all-done.5 = bf16[4,4,3,112,128]{4,1,3,2,0:T(4,128)(2,1)S(1)} async-done(((bf16[4,4,3,112,128]{4,1,3,2,0:T(4,128)(2,1)}), bf16[4,4,3,112,128]{4,1,3,2,0:T(4,128)(2,1)S(1)}, u32[]{:S(2)}, u32[]{:S(2)}) %all-to-all-start.5) | async-done | bytes 1376288 | tf_op jit(solution)/shard_map/all_to_all | solution.py:33
  215.5 1.2 fusion.73
  216.7 0.5 fusion.29
  217.2 1.4 convolution_add_fusion
  218.7 0.1 slice_select_fusion
  218.8 1.9 collective-permute-start
  220.7 1.9 collective-permute-done
  222.6 0.1 select_add_fusion
  222.8 12.5 %all_to_all.43 = f32[4,64,512]{2,1,0:T(8,128)S(1)} all-to-all(f32[4,64,512]{2,1,0:T(8,128)S(1)} %bitcast.78), channel_id=1, replica_groups=mesh['zhi'=4,'y'=4,'zlo'=8,'x'=4,'core'=2] {'x'}, dimensions={0} | all-to-all | bytes 1048576 | tf_op jit(solution)/shard_map/all_to_all | solution.py:96
  235.2 0.7 reduce_sum.38
  235.9 10.4 %all-to-all-start.7 = ((f32[8,8,512]{2,1,0:T(8,128)}), f32[8,8,512]{2,1,0:T(8,128)S(1)}, u32[]{:S(2)}, u32[]{:S(2)}) async-start(f32[8,8,512]{2,1,0:T(8,128)} %bitcast.24), calls=%async_computation.7 | async-start | bytes 262144 | tf_op jit(solution)/shard_map/all_to_all | solution.py:97
  246.4 1.2 fusion.2
  247.6 1.2 fusion.1
  248.7 1.2 fusion
  249.9 8.0 %all-to-all-done.7 = f32[8,8,512]{2,1,0:T(8,128)S(1)} async-done(((f32[8,8,512]{2,1,0:T(8,128)}), f32[8,8,512]{2,1,0:T(8,128)S(1)}, u32[]{:S(2)}, u32[]{:S(2)}) %all-to-all-start.7) | async-done | bytes 131104 | tf_op jit(solution)/shard_map/all_to_all | solution.py:97
  257.9 0.6 reduce_sum.39
  (50 shorter events, 0.6 us)
Async XLA Ops:
  0.6 19.4 %copy-start.2 = (s32[128,448]{0,1:T(8,128)S(1)}, s32[128,448]{0,1:T(8,128)}, u32[]{:S(2)}) copy-start(s32[128,448]{0,1:T(8,128)} %param.13) | copy-start | bytes 688132
  0.6 19.7 %copy-start.4 = (s32[128,448]{0,1:T(8,128)S(1)}, s32[128,448]{0,1:T(8,128)}, u32[]{:S(2)}) copy-start(s32[128,448]{0,1:T(8,128)} %param.14) | copy-start | bytes 688132
  0.7 19.5 %copy-start.3 = (s32[112,512]{1,0:T(8,128)S(1)}, s32[112,512]{1,0:T(8,128)}, u32[]{:S(2)}) copy-start(s32[112,512]{1,0:T(8,128)} %param.15) | copy-start | bytes 688132
  2.1 24.5 %all-to-all-start = ((bf16[8,2,8,512]{3,2,1,0:T(8,128)(2,1)}), bf16[8,2,8,512]{3,2,1,0:T(8,128)(2,1)S(1)}, u32[]{:S(2)}, u32[]{:S(2)}) async-start(bf16[8,2,8,512]{3,2,1,0:T(8,128)(2,1)} %broadcast_in_dim.39), calls=%async_computation | async-start | bytes 262144 | tf_op jit(solution)/shard_map/all_to_all | solution.py:33
  21.4 24.4 %copy-start.15 = (pred[448,512]{1,0:T(32,128)(4,1)}, pred[448,512]{1,0:T(32,128)(4,1)S(1)}, u32[]{:S(2)}) copy-start(pred[448,512]{1,0:T(32,128)(4,1)S(1)} %convolution_compare_fusion) | copy-start | bytes 688132
  27.5 12.9 %all-to-all-start.1 = ((bf16[4,8,2,8,512]{4,3,2,1,0:T(8,128)(2,1)}), bf16[4,8,2,8,512]{4,3,2,1,0:T(8,128)(2,1)S(1)}, u32[]{:S(2)}, u32[]{:S(2)}) async-start(bf16[4,8,2,8,512]{4,3,2,1,0:T(8,128)(2,1)} %broadcast_in_dim.40), calls=%async_computation.1 | async-start | bytes 1048576 | tf_op jit(solution)/shard_map/all_to_all | solution.py:33
  34.4 10.4 %copy-start.5 = (bf16[512,448]{0,1:T(8,128)(2,1)S(1)}, bf16[512,448]{0,1:T(8,128)(2,1)}, u32[]{:S(2)}) copy-start(bf16[512,448]{0,1:T(8,128)(2,1)} %param.10) | copy-start | bytes 1376260
  35.2 10.5 %copy-start.11 = (pred[448,512]{1,0:T(32,128)(4,1)}, pred[448,512]{1,0:T(32,128)(4,1)S(1)}, u32[]{:S(2)}) copy-start(pred[448,512]{1,0:T(32,128)(4,1)S(1)} %convolution_compare_fusion.1) | copy-start | bytes 688132
  35.2 10.1 %copy-start.7 = (bf16[512,448]{0,1:T(8,128)(2,1)S(1)}, bf16[512,448]{0,1:T(8,128)(2,1)}, u32[]{:S(2)}) copy-start(bf16[512,448]{0,1:T(8,128)(2,1)} %param.11) | copy-start | bytes 1376260
  40.4 5.4 %copy-start.13 = (bf16[448,512]{1,0:T(8,128)(2,1)S(1)}, bf16[448,512]{1,0:T(8,128)(2,1)}, u32[]{:S(2)}) copy-start(bf16[448,512]{1,0:T(8,128)(2,1)} %param.12) | copy-start | bytes 1376260
  44.9 1.4 copy-start
  196.5 20.2 %copy-start.6 = (bf16[512,448]{0,1:T(8,128)(2,1)S(1)}, bf16[512,448]{0,1:T(8,128)(2,1)}, u32[]{:S(2)}) copy-start(bf16[512,448]{0,1:T(8,128)(2,1)} %param.10) | copy-start | bytes 1376260
  196.5 18.9 %all-to-all-start.5 = ((bf16[4,4,3,112,128]{4,1,3,2,0:T(4,128)(2,1)}), bf16[4,4,3,112,128]{4,1,3,2,0:T(4,128)(2,1)S(1)}, u32[]{:S(2)}, u32[]{:S(2)}) async-start(bf16[4,4,3,112,128]{4,1,3,2,0:T(4,128)(2,1)} %broadcast_in_dim.42), calls=%async_computation.5 | async-start | bytes 2752512 | tf_op jit(solution)/shard_map/all_to_all | solution.py:33
  200.2 17.0 %copy-start.8 = (bf16[512,448]{0,1:T(8,128)(2,1)S(1)}, bf16[512,448]{0,1:T(8,128)(2,1)}, u32[]{:S(2)}) copy-start(bf16[512,448]{0,1:T(8,128)(2,1)} %param.11) | copy-start | bytes 1376260
  216.7 2.1 copy-start.9
  218.7 27.7 %copy-start.12 = (pred[448,512]{1,0:T(32,128)(4,1)S(1)}, pred[448,512]{1,0:T(32,128)(4,1)}, u32[]{:S(2)}) copy-start(pred[448,512]{1,0:T(32,128)(4,1)} %copy-done.11) | copy-start | bytes 688132
  218.8 3.8 %collective-permute-start = (f32[256,512]{1,0:T(8,128)S(1)}, f32[256,512]{1,0:T(8,128)S(1)}, u32[]{:S(2)}, u32[]{:S(2)}) collective-permute-start(f32[256,512]{1,0:T(8,128)S(1)} %slice_select_fusion), channel_id=1, source_target_pairs={{0,1},{1,0},{2,3},{3,2},{4,5},{5,4},{6,7},{7,6},{8,9},{9,8},{10,11... | collective-permute-start | bytes 1572872 | tf_op jit(solution)/shard_map/ppermute | solution.py:95
  220.7 25.7 %copy-start.10 = (bf16[1,4,112,4,128]{4,3,2,0,1:T(4,128)(2,1)S(1)}, bf16[1,4,112,4,128]{4,3,2,0,1:T(4,128)(2,1)}, u32[]{:S(2)}) copy-start(bf16[1,4,112,4,128]{4,3,2,0,1:T(4,128)(2,1)} %copy-done.9) | copy-start | bytes 1376260
  222.8 26.0 %copy-start.1 = (bf16[512,512]{1,0:T(8,128)(2,1)S(1)}, bf16[512,512]{1,0:T(8,128)(2,1)}, u32[]{:S(2)}) copy-start(bf16[512,512]{1,0:T(8,128)(2,1)} %copy-done) | copy-start | bytes 1572868
  222.8 26.0 %copy-start.14 = (bf16[1,4,112,4,128]{4,3,2,0,1:T(4,128)(2,1)S(1)}, bf16[1,4,112,4,128]{4,3,2,0,1:T(4,128)(2,1)}, u32[]{:S(2)}) copy-start(bf16[1,4,112,4,128]{4,3,2,0,1:T(4,128)(2,1)} %get-tuple-element.31) | copy-start | bytes 1376260
  235.9 12.8 %copy-start.16 = (pred[448,512]{1,0:T(32,128)(4,1)S(1)}, pred[448,512]{1,0:T(32,128)(4,1)}, u32[]{:S(2)}) copy-start(pred[448,512]{1,0:T(32,128)(4,1)} %copy-done.15) | copy-start | bytes 688132
  235.9 22.0 %all-to-all-start.7 = ((f32[8,8,512]{2,1,0:T(8,128)}), f32[8,8,512]{2,1,0:T(8,128)S(1)}, u32[]{:S(2)}, u32[]{:S(2)}) async-start(f32[8,8,512]{2,1,0:T(8,128)} %bitcast.24), calls=%async_computation.7 | async-start | bytes 262144 | tf_op jit(solution)/shard_map/all_to_all | solution.py:97

commit v2 on v1

--- a/solution.py
+++ b/solution.py
@@ -31,6 +31,13 @@
 
 def gather_by_exchange(block, axis, size):
     return lax.all_to_all(jnp.broadcast_to(block[None], (size, *block.shape)), axis, 0, 0)
+
+
+def zhi_exchange(block, flip0, flip1):
+    pairs = [
+        (z * 2 + c, (z ^ (flip0, flip1)[c]) * 2 + c) for z in range(4) for c in range(2)
+    ]
+    return lax.ppermute(block, ("zhi", "core"), pairs)
 
 
 def swiglu_back(gate_pre, up_pre, hidden_grad):
@@ -67,8 +74,8 @@
     up_eff = jnp.where(up_keep, up_weight.T, zero)
     down_eff = jnp.where(down_keep, down_weight, zero)
 
-    ny, nz = sizes["y"], sizes["zhi"]
-    quarter, strip = hidden_units // ny, tokens_all // nz
+    ny = sizes["y"]
+    quarter = hidden_units // ny
     partial = jnp.stack(
         [
             dot(gate_eff, tokens, ((1,), (1,))).reshape(ny, quarter, tokens_all),
@@ -78,18 +85,26 @@
         axis=1,
     )
     summed = lax.all_to_all(partial, "y", 0, 0).sum(axis=0)
-    strips = summed.astype(bf16).reshape(3, quarter, nz, strip).transpose(2, 0, 1, 3)
-    summed = lax.all_to_all(strips, "zhi", 0, 0).astype(f32).sum(axis=0)
-    triple = swiglu_back(summed[0], summed[1], summed[2])
-    triple = gather_by_exchange(triple, "zhi", nz)
+
+    zhi, core = lax.axis_index("zhi"), lax.axis_index("core")
+    first = jnp.where(core == 0, (zhi ^ (zhi >> 1)) & 1, zhi >> 1) == 0
+    front, back = summed[:, :, : tokens_all // 2], summed[:, :, tokens_all // 2 :]
+    kept = jnp.where(first, front, back)
+    sent = jnp.where(first, back, front).astype(bf16)
+    kept = kept + zhi_exchange(sent, 1, 3).astype(f32)
+    kept = kept + zhi_exchange(kept.astype(bf16), 3, 1).astype(f32)
+    mine = swiglu_back(kept[0], kept[1], kept[2])
+    other = zhi_exchange(mine, 1, 3)
+    triple = jnp.concatenate(
+        [jnp.where(first, mine, other), jnp.where(first, other, mine)], axis=2
+    )
     triple = gather_by_exchange(triple, "y", ny)
-    triple = triple.transpose(2, 0, 3, 1, 4).reshape(3, hidden_units, tokens_all)
+    triple = triple.transpose(1, 0, 2, 3).reshape(3, hidden_units, tokens_all)
     hidden, gate_grad, up_grad = triple[0], triple[1], triple[2]
 
     half = tokens_all // 2
     back = dot(gate_grad, gate_eff, ((0,), (0,))) + dot(up_grad, up_eff, ((0,), (0,)))
     back = back.reshape(2, half, width)
-    core = lax.axis_index("core")
     kept = jnp.where(core == 0, back[0], back[1])
     sent = jnp.where(core == 0, back[1], back[0])
     back = kept + lax.ppermute(sent, "core", [(0, 1), (1, 0)])

time: 260 us -> 223 us (0.86)
  blocking collectives: 163 us -> 32.6 us
  waiting for transfers between devices: 34.6 us -> 107 us
  starting transfers between devices: 35.4 us -> 59.8 us
  local copies, waits for them, and re-layouts: 5.77 us -> 2.32 us
    all_to_all x2 -> x0, blocking collectives: 92.9 us -> none  [the longest x1 56.4 us: body(): summed = lax.all_to_all(strips, 'zhi', 0, 0).astype(f32).sum(axis=0)]
    ppermute x0 -> x3, waiting for transfers between devices: none -> 54.1 us  [zhi_exchange(): return lax.ppermute(block, ('zhi', 'core'), pairs)]
    all_to_all x1, blocking collectives: 53.1 us -> 15.2 us  [gather_by_exchange(): lax.all_to_all(jnp.broadcast_to(block[None], (size, *block.shape)), axis,...]
    all_to_all x0 -> x1, waiting for transfers between devices: none -> 33.9 us  [body(): summed = lax.all_to_all(partial, 'y', 0, 0).sum(axis=0)]
    ppermute x0 -> x3, starting transfers between devices: none -> 25.1 us  [zhi_exchange(): return lax.ppermute(block, ('zhi', 'core'), pairs)]
    all_to_all x3 -> x2, waiting for transfers between devices: 24.7 us -> 9.45 us  [gather_by_exchange(): lax.all_to_all(jnp.broadcast_to(block[None], (size, *block.shape)), axis,...]
    all_to_all x3 -> x2, starting transfers between devices: 23 us -> 19.4 us  [gather_by_exchange(): lax.all_to_all(jnp.broadcast_to(block[None], (size, *block.shape)), axis,...]
    all_to_all x0 -> x1, starting transfers between devices: none -> 3.66 us  [body(): summed = lax.all_to_all(partial, 'y', 0, 0).sum(axis=0)]
  transfers between devices with their start and end apart: 5 -> 8, of which waited for: 5 -> 8; matrix products, arithmetic and copies ran while one was open for 5% -> 5% of each run, Pallas kernels for 0% -> 0%
where the time goes in v2:
time: 223 us; the launch traced here: 222 us
  waiting for transfers between devices  107 us (48%)
  starting transfers between devices  59.8 us (27%)
  blocking collectives  32.6 us (15%)
  other arithmetic  10.6 us (5%)
  matrix products  8.29 us (4%)
  local copies, waits for them, and re-layouts  2.32 us (1%)
    ppermute x3, waiting for transfers between devices, zhi_exchange(): return lax.ppermute(block, ('zhi', 'core'), pairs)  54.1 us
    all_to_all x1, waiting for transfers between devices, body(): summed = lax.all_to_all(partial, 'y', 0, 0).sum(axis=0)  33.9 us
    ppermute x3, starting transfers between devices, zhi_exchange(): return lax.ppermute(block, ('zhi', 'core'), pairs)  25.1 us
    all_to_all x2, starting transfers between devices, gather_by_exchange(): lax.all_to_all(jnp.broadcast_to(block[None], (size, *block.shape)), axis,...  19.4 us
    all_to_all x1, blocking collectives, gather_by_exchange(): lax.all_to_all(jnp.broadcast_to(block[None], (size, *block.shape)), axis,...  15.2 us
    all_to_all x1, blocking collectives, body(): lax.all_to_all(back.reshape(sizes['x'], half // sizes['x'], width), 'x',...  12.9 us
    all_to_all x1, starting transfers between devices, body(): lax.all_to_all(back.reshape(sizes['zlo'], rows, width), 'zlo', 0, 0)  9.58 us
    all_to_all x2, waiting for transfers between devices, gather_by_exchange(): lax.all_to_all(jnp.broadcast_to(block[None], (size, *block.shape)), axis,...  9.45 us
  transfers between devices with their start and end apart: 8, of which 8 were waited for; matrix products, arithmetic and copies ran while one was open for 5% of the time, Pallas kernels for 0%

profile of v2, /device:TPU:6, one launch (start us, length us, event | category | flops | bytes accessed | tf_op | source)
XLA Modules:
  0.0 221.9 jit_solution(14372047272425582124)
XLA Ops:
  0.7 0.8 pad_maximum_fusion.3
  1.5 0.7 broadcast_in_dim.33
  2.1 12.5 %all-to-all-start = ((bf16[8,2,8,512]{3,2,1,0:T(8,128)(2,1)}), bf16[8,2,8,512]{3,2,1,0:T(8,128)(2,1)S(1)}, u32[]{:S(2)}, u32[]{:S(2)}) async-start(bf16[8,2,8,512]{3,2,1,0:T(8,128)(2,1)} %broadcast_in_dim.33), calls=%async_computation | async-start | bytes 262144 | tf_op jit(solution)/shard_map/all_to_all | solution.py:33
  14.7 1.1 or_bitcast_fusion.7
  15.8 1.0 or_bitcast_fusion.6
  16.8 1.1 or_bitcast_fusion.3
  17.9 1.1 or_or_fusion.3
  19.0 1.0 or_or_fusion.2
  20.3 0.1 or_bitcast_fusion.2
  20.5 0.9 convolution_compare_fusion
  21.4 0.8 convolution_compare_fusion.2
  22.2 4.4 %all-to-all-done = bf16[8,2,8,512]{3,2,1,0:T(8,128)(2,1)S(1)} async-done(((bf16[8,2,8,512]{3,2,1,0:T(8,128)(2,1)}), bf16[8,2,8,512]{3,2,1,0:T(8,128)(2,1)S(1)}, u32[]{:S(2)}, u32[]{:S(2)}) %all-to-all-start) | async-done | bytes 131104 | tf_op jit(solution)/shard_map/all_to_all | solution.py:33
  26.6 0.9 broadcast_in_dim.34
  27.4 6.8 %all-to-all-start.1 = ((bf16[4,8,2,8,512]{4,3,2,1,0:T(8,128)(2,1)}), bf16[4,8,2,8,512]{4,3,2,1,0:T(8,128)(2,1)S(1)}, u32[]{:S(2)}, u32[]{:S(2)}) async-start(bf16[4,8,2,8,512]{4,3,2,1,0:T(8,128)(2,1)} %broadcast_in_dim.34), calls=%async_computation.1 | async-start | bytes 1048576 | tf_op jit(solution)/shard_map/all_to_all | solution.py:33
  34.5 0.8 convolution_compare_fusion.1
  35.2 5.1 %all-to-all-done.1 = bf16[4,8,2,8,512]{4,3,2,1,0:T(8,128)(2,1)S(1)} async-done(((bf16[4,8,2,8,512]{4,3,2,1,0:T(8,128)(2,1)}), bf16[4,8,2,8,512]{4,3,2,1,0:T(8,128)(2,1)S(1)}, u32[]{:S(2)}, u32[]{:S(2)}) %all-to-all-start.1) | async-done | bytes 524320 | tf_op jit(solution)/shard_map/all_to_all | solution.py:33
  40.4 2.3 %all_gather.6 = bf16[512,512]{1,0:T(8,128)(2,1)S(1)} all-gather(bf16[256,512]{1,0:T(8,128)(2,1)S(1)} %bitcast.70), channel_id=1, replica_groups=mesh['zhi'=4,'y'=4,'zlo'=8,'x'=4,'core'=2] {'core'}, dimensions={0}, use_global_device_ids=true | all-gather | bytes 786432 | tf_op jit(solution)/shard_map/all_gather | solution.py:64
  42.7 2.2 all_gather.7
  44.9 0.4 fusion.34
  45.3 0.4 fusion.35
  45.8 0.4 fusion.24
  46.3 1.8 pad_maximum_fusion
  48.1 3.7 %all-to-all-start.2 = ((f32[4,3,112,512]{3,2,1,0:T(8,128)}), f32[4,3,112,512]{3,2,1,0:T(8,128)S(1)}, u32[]{:S(2)}, u32[]{:S(2)}) async-start(f32[4,3,112,512]{3,2,1,0:T(8,128)} %pad_maximum_fusion), calls=%async_computation.2 | async-start | bytes 5505024 | tf_op jit(solution)/shard_map/all_to_all | solution.py:87
  51.7 33.9 %all-to-all-done.2 = f32[4,3,112,512]{3,2,1,0:T(8,128)S(1)} async-done(((f32[4,3,112,512]{3,2,1,0:T(8,128)}), f32[4,3,112,512]{3,2,1,0:T(8,128)S(1)}, u32[]{:S(2)}, u32[]{:S(2)}) %all-to-all-start.2) | async-done | bytes 2752544 | tf_op jit(solution)/shard_map/all_to_all | solution.py:87
  85.6 0.3 reduce_sum.27
  86.0 14.2 %collective-permute-start = (bf16[3,112,256]{2,1,0:T(8,128)(2,1)S(1)}, bf16[3,112,256]{2,1,0:T(8,128)(2,1)S(1)}, u32[]{:S(2)}, u32[]{:S(2)}) collective-permute-start(bf16[3,112,256]{2,1,0:T(8,128)(2,1)S(1)} %select_convert_fusion), channel_id=1, source_target_pairs={{0,256},{1,769},{256,0},{257,513},{512,768},{513,257},{768,512},{7... | collective-permute-start | bytes 516104 | tf_op jit(solution)/shard_map/ppermute | solution.py:40
  100.2 16.4 %collective-permute-done = bf16[3,112,256]{2,1,0:T(8,128)(2,1)S(1)} collective-permute-done((bf16[3,112,256]{2,1,0:T(8,128)(2,1)S(1)}, bf16[3,112,256]{2,1,0:T(8,128)(2,1)S(1)}, u32[]{:S(2)}, u32[]{:S(2)}) %collective-permute-start) | collective-permute-done | bytes 172064 | tf_op jit(solution)/shard_map/ppermute | solution.py:40
  116.7 7.0 %collective-permute-start.1 = (bf16[3,112,256]{2,1,0:T(8,128)(2,1)S(1)}, bf16[3,112,256]{2,1,0:T(8,128)(2,1)S(1)}, u32[]{:S(2)}, u32[]{:S(2)}) collective-permute-start(bf16[3,112,256]{2,1,0:T(8,128)(2,1)S(1)} %fusion.42), channel_id=1, source_target_pairs={{0,768},{1,257},{256,512},{257,1},{512,256},{513,769},{768,0},{769... | collective-permute-start | bytes 516104 | tf_op jit(solution)/shard_map/ppermute | solution.py:40
  123.6 18.4 %collective-permute-done.1 = bf16[3,112,256]{2,1,0:T(8,128)(2,1)S(1)} collective-permute-done((bf16[3,112,256]{2,1,0:T(8,128)(2,1)S(1)}, bf16[3,112,256]{2,1,0:T(8,128)(2,1)S(1)}, u32[]{:S(2)}, u32[]{:S(2)}) %collective-permute-start.1) | collective-permute-done | bytes 172064 | tf_op jit(solution)/shard_map/ppermute | solution.py:40
  142.2 3.9 %collective-permute-start.2 = (bf16[3,112,256]{2,1,0:T(8,128)(2,1)S(1)}, bf16[3,112,256]{2,1,0:T(8,128)(2,1)S(1)}, u32[]{:S(2)}, u32[]{:S(2)}) collective-permute-start(bf16[3,112,256]{2,1,0:T(8,128)(2,1)S(1)} %pad_maximum_fusion.2), channel_id=1, source_target_pairs={{0,256},{1,769},{256,0},{257,513},{512,768},{513,257},{768,512},{7... | collective-permute-start | bytes 516104 | tf_op jit(solution)/shard_map/ppermute | solution.py:40
  146.1 19.3 %collective-permute-done.2 = bf16[3,112,256]{2,1,0:T(8,128)(2,1)S(1)} collective-permute-done((bf16[3,112,256]{2,1,0:T(8,128)(2,1)S(1)}, bf16[3,112,256]{2,1,0:T(8,128)(2,1)S(1)}, u32[]{:S(2)}, u32[]{:S(2)}) %collective-permute-start.2) | collective-permute-done | bytes 172064 | tf_op jit(solution)/shard_map/ppermute | solution.py:40
  165.6 0.1 broadcast_in_dim.35
  165.7 15.2 %all_to_all.30 = bf16[4,3,112,512]{3,2,1,0:T(8,128)(2,1)S(1)} all-to-all(bf16[4,3,112,512]{3,2,1,0:T(8,128)(2,1)S(1)} %broadcast_in_dim.35), channel_id=1, replica_groups=mesh['zhi'=4,'y'=4,'zlo'=8,'x'=4,'core'=2] {'y'}, dimensions={0} | all-to-all | bytes 2752512 | tf_op jit(solution)/shard_map/all_to_all | solution.py:33
  180.9 0.1 fusion.64
  181.0 0.5 fusion.33
  181.5 0.4 copy-done.10
  182.0 0.5 convolution_add_fusion
  182.6 2.1 collective-permute-start.3
  184.6 1.9 collective-permute-done.3
  186.5 0.1 select_add_fusion
  186.7 12.9 %all_to_all.31 = f32[4,64,512]{2,1,0:T(8,128)S(1)} all-to-all(f32[4,64,512]{2,1,0:T(8,128)S(1)} %bitcast.63), channel_id=1, replica_groups=mesh['zhi'=4,'y'=4,'zlo'=8,'x'=4,'core'=2] {'x'}, dimensions={0} | all-to-all | bytes 1048576 | tf_op jit(solution)/shard_map/all_to_all | solution.py:111
  199.6 0.7 reduce_sum.28
  200.2 9.6 %all-to-all-start.5 = ((f32[8,8,512]{2,1,0:T(8,128)}), f32[8,8,512]{2,1,0:T(8,128)S(1)}, u32[]{:S(2)}, u32[]{:S(2)}) async-start(f32[8,8,512]{2,1,0:T(8,128)} %bitcast.25), calls=%async_computation.5 | async-start | bytes 262144 | tf_op jit(solution)/shard_map/all_to_all | solution.py:112
  209.8 1.2 fusion.2
  211.0 1.2 fusion.1
  212.2 1.2 fusion
  213.4 7.9 %all-to-all-done.5 = f32[8,8,512]{2,1,0:T(8,128)S(1)} async-done(((f32[8,8,512]{2,1,0:T(8,128)}), f32[8,8,512]{2,1,0:T(8,128)S(1)}, u32[]{:S(2)}, u32[]{:S(2)}) %all-to-all-start.5) | async-done | bytes 131104 | tf_op jit(solution)/shard_map/all_to_all | solution.py:112
  221.3 0.6 reduce_sum.29
  (56 shorter events, 1.1 us)
Async XLA Ops:
  0.6 19.4 %copy-start.4 = (s32[128,448]{0,1:T(8,128)S(1)}, s32[128,448]{0,1:T(8,128)}, u32[]{:S(2)}) copy-start(s32[128,448]{0,1:T(8,128)} %param.13) | copy-start | bytes 688132
  0.6 19.7 %copy-start.6 = (s32[128,448]{0,1:T(8,128)S(1)}, s32[128,448]{0,1:T(8,128)}, u32[]{:S(2)}) copy-start(s32[128,448]{0,1:T(8,128)} %param.14) | copy-start | bytes 688132
  0.7 19.5 %copy-start.5 = (s32[112,512]{1,0:T(8,128)S(1)}, s32[112,512]{1,0:T(8,128)}, u32[]{:S(2)}) copy-start(s32[112,512]{1,0:T(8,128)} %param.15) | copy-start | bytes 688132
  2.1 24.5 %all-to-all-start = ((bf16[8,2,8,512]{3,2,1,0:T(8,128)(2,1)}), bf16[8,2,8,512]{3,2,1,0:T(8,128)(2,1)S(1)}, u32[]{:S(2)}, u32[]{:S(2)}) async-start(bf16[8,2,8,512]{3,2,1,0:T(8,128)(2,1)} %broadcast_in_dim.33), calls=%async_computation | async-start | bytes 262144 | tf_op jit(solution)/shard_map/all_to_all | solution.py:33
  21.4 24.4 %copy-start.16 = (pred[448,512]{1,0:T(32,128)(4,1)}, pred[448,512]{1,0:T(32,128)(4,1)S(1)}, u32[]{:S(2)}) copy-start(pred[448,512]{1,0:T(32,128)(4,1)S(1)} %convolution_compare_fusion) | copy-start | bytes 688132
  22.2 22.7 %copy-start.11 = (pred[448,512]{1,0:T(32,128)(4,1)}, pred[448,512]{1,0:T(32,128)(4,1)S(1)}, u32[]{:S(2)}) copy-start(pred[448,512]{1,0:T(32,128)(4,1)S(1)} %convolution_compare_fusion.2) | copy-start | bytes 688132
  27.4 12.9 %all-to-all-start.1 = ((bf16[4,8,2,8,512]{4,3,2,1,0:T(8,128)(2,1)}), bf16[4,8,2,8,512]{4,3,2,1,0:T(8,128)(2,1)S(1)}, u32[]{:S(2)}, u32[]{:S(2)}) async-start(bf16[4,8,2,8,512]{4,3,2,1,0:T(8,128)(2,1)} %broadcast_in_dim.34), calls=%async_computation.1 | async-start | bytes 1048576 | tf_op jit(solution)/shard_map/all_to_all | solution.py:33
  34.4 10.4 %copy-start.7 = (bf16[512,448]{0,1:T(8,128)(2,1)S(1)}, bf16[512,448]{0,1:T(8,128)(2,1)}, u32[]{:S(2)}) copy-start(bf16[512,448]{0,1:T(8,128)(2,1)} %param.10) | copy-start | bytes 1376260
  35.2 10.5 %copy-start.13 = (pred[448,512]{1,0:T(32,128)(4,1)}, pred[448,512]{1,0:T(32,128)(4,1)S(1)}, u32[]{:S(2)}) copy-start(pred[448,512]{1,0:T(32,128)(4,1)S(1)} %convolution_compare_fusion.1) | copy-start | bytes 688132
  35.2 10.1 %copy-start.9 = (bf16[512,448]{0,1:T(8,128)(2,1)S(1)}, bf16[512,448]{0,1:T(8,128)(2,1)}, u32[]{:S(2)}) copy-start(bf16[512,448]{0,1:T(8,128)(2,1)} %param.11) | copy-start | bytes 1376260
  40.4 5.4 %copy-start.15 = (bf16[448,512]{1,0:T(8,128)(2,1)S(1)}, bf16[448,512]{1,0:T(8,128)(2,1)}, u32[]{:S(2)}) copy-start(bf16[448,512]{1,0:T(8,128)(2,1)} %param.12) | copy-start | bytes 1376260
  42.7 3.6 %copy-start = (bf16[512,512]{1,0:T(8,128)(2,1)}, bf16[512,512]{1,0:T(8,128)(2,1)S(1)}, u32[]{:S(2)}) copy-start(bf16[512,512]{1,0:T(8,128)(2,1)S(1)} %all_gather.6) | copy-start | bytes 1572868
  44.9 1.4 copy-start.2
  48.1 37.6 %all-to-all-start.2 = ((f32[4,3,112,512]{3,2,1,0:T(8,128)}), f32[4,3,112,512]{3,2,1,0:T(8,128)S(1)}, u32[]{:S(2)}, u32[]{:S(2)}) async-start(f32[4,3,112,512]{3,2,1,0:T(8,128)} %pad_maximum_fusion), calls=%async_computation.2 | async-start | bytes 5505024 | tf_op jit(solution)/shard_map/all_to_all | solution.py:87
  86.0 30.6 %collective-permute-start = (bf16[3,112,256]{2,1,0:T(8,128)(2,1)S(1)}, bf16[3,112,256]{2,1,0:T(8,128)(2,1)S(1)}, u32[]{:S(2)}, u32[]{:S(2)}) collective-permute-start(bf16[3,112,256]{2,1,0:T(8,128)(2,1)S(1)} %select_convert_fusion), channel_id=1, source_target_pairs={{0,256},{1,769},{256,0},{257,513},{512,768},{513,257},{768,512},{7... | collective-permute-start | bytes 516104 | tf_op jit(solution)/shard_map/ppermute | solution.py:40
  116.7 25.3 %collective-permute-start.1 = (bf16[3,112,256]{2,1,0:T(8,128)(2,1)S(1)}, bf16[3,112,256]{2,1,0:T(8,128)(2,1)S(1)}, u32[]{:S(2)}, u32[]{:S(2)}) collective-permute-start(bf16[3,112,256]{2,1,0:T(8,128)(2,1)S(1)} %fusion.42), channel_id=1, source_target_pairs={{0,768},{1,257},{256,512},{257,1},{512,256},{513,769},{768,0},{769... | collective-permute-start | bytes 516104 | tf_op jit(solution)/shard_map/ppermute | solution.py:40
  142.2 23.3 %collective-permute-start.2 = (bf16[3,112,256]{2,1,0:T(8,128)(2,1)S(1)}, bf16[3,112,256]{2,1,0:T(8,128)(2,1)S(1)}, u32[]{:S(2)}, u32[]{:S(2)}) collective-permute-start(bf16[3,112,256]{2,1,0:T(8,128)(2,1)S(1)} %pad_maximum_fusion.2), channel_id=1, source_target_pairs={{0,256},{1,769},{256,0},{257,513},{512,768},{513,257},{768,512},{7... | collective-permute-start | bytes 516104 | tf_op jit(solution)/shard_map/ppermute | solution.py:40
  165.7 15.3 %copy-start.8 = (bf16[512,448]{0,1:T(8,128)(2,1)S(1)}, bf16[512,448]{0,1:T(8,128)(2,1)}, u32[]{:S(2)}) copy-start(bf16[512,448]{0,1:T(8,128)(2,1)} %param.10) | copy-start | bytes 1376260
  165.7 15.3 %copy-start.12 = (pred[448,512]{1,0:T(32,128)(4,1)S(1)}, pred[448,512]{1,0:T(32,128)(4,1)}, u32[]{:S(2)}) copy-start(pred[448,512]{1,0:T(32,128)(4,1)} %copy-done.11) | copy-start | bytes 688132
  180.9 1.0 copy-start.10
  180.9 1.1 copy-start.14
  182.5 27.3 %copy-start.1 = (bf16[512,512]{1,0:T(8,128)(2,1)S(1)}, bf16[512,512]{1,0:T(8,128)(2,1)}, u32[]{:S(2)}) copy-start(bf16[512,512]{1,0:T(8,128)(2,1)} %copy-done) | copy-start | bytes 1572868
  182.6 3.9 %collective-permute-start.3 = (f32[256,512]{1,0:T(8,128)S(1)}, f32[256,512]{1,0:T(8,128)S(1)}, u32[]{:S(2)}, u32[]{:S(2)}) collective-permute-start(f32[256,512]{1,0:T(8,128)S(1)} %slice_select_fusion), channel_id=1, source_target_pairs={{0,1},{1,0},{2,3},{3,2},{4,5},{5,4},{6,7},{7,6},{8,9},{9,8},{10,11... | collective-permute-start | bytes 1572872 | tf_op jit(solution)/shard_map/ppermute | solution.py:110
  186.7 25.5 %copy-start.3 = (bf16[512,512]{1,0:T(8,128)(2,1)S(1)}, bf16[512,512]{1,0:T(8,128)(2,1)}, u32[]{:S(2)}) copy-start(bf16[512,512]{1,0:T(8,128)(2,1)} %copy-done.2) | copy-start | bytes 1572868
  200.2 11.9 %copy-start.17 = (pred[448,512]{1,0:T(32,128)(4,1)S(1)}, pred[448,512]{1,0:T(32,128)(4,1)}, u32[]{:S(2)}) copy-start(pred[448,512]{1,0:T(32,128)(4,1)} %copy-done.16) | copy-start | bytes 688132
  200.2 21.0 %all-to-all-start.5 = ((f32[8,8,512]{2,1,0:T(8,128)}), f32[8,8,512]{2,1,0:T(8,128)S(1)}, u32[]{:S(2)}, u32[]{:S(2)}) async-start(f32[8,8,512]{2,1,0:T(8,128)} %bitcast.25), calls=%async_computation.5 | async-start | bytes 262144 | tf_op jit(solution)/shard_map/all_to_all | solution.py:112

commit v3 on v2

v3 whole, which is shorter than its diff:
```python
import jax
import jax.numpy as jnp
import numpy as np
from jax import lax
from jax.sharding import Mesh, PartitionSpec as P

bf16 = jnp.bfloat16
f32 = jnp.float32
keep_sets = ((0, 1, 2), (0, 3, 4), (1, 3, 5), (2, 4, 5))


def keep_planes(pattern):
    planes = []
    for members in keep_sets:
        kept = pattern == members[0]
        for member in members[1:]:
            kept = kept | (pattern == member)
        planes.append(kept.astype(bf16))
    return planes


def spread_matrix(groups):
    row = lax.broadcasted_iota(jnp.int32, (4 * groups, 4 * groups), 0)
    col = lax.broadcasted_iota(jnp.int32, (4 * groups, 4 * groups), 1)
    return ((row % groups) * 4 + row // groups == col).astype(bf16)


def dot(a, b, dims):
    return lax.dot_general(a, b, (dims, ((), ())), preferred_element_type=f32)


def gather_by_exchange(block, axis, size):
    return lax.all_to_all(jnp.broadcast_to(block[None], (size, *block.shape)), axis, 0, 0)


def zhi_exchange(block, flip0, flip1):
    pairs = [
        (z * 2 + c, (z ^ (flip0, flip1)[c]) * 2 + c) for z in range(4) for c in range(2)
    ]
    return lax.ppermute(block, ("zhi", "core"), pairs)


f16 = jnp.float16
PAD = 8


def to_link(values, power):
    scaled = values * jnp.exp2(-power)
    shape = (*values.shape[:-2], PAD, values.shape[-1])
    return jnp.concatenate([scaled, jnp.broadcast_to(power, shape)], axis=-2).astype(f16)


def from_link(block):
    wide = block.astype(f32)
    power = wide[..., -PAD : 1 - PAD, :1]
    return wide[..., :-PAD, :] * jnp.exp2(power), power


def top(values):
    return jnp.max(jnp.abs(values)).astype(f32)


def power_of(bound):
    return jnp.ceil(jnp.log2(jnp.maximum(bound, 1e-30))) - 15.0


def swiglu_back(gate_pre, up_pre, hidden_grad):
    sigmoid_gate = jax.nn.sigmoid(gate_pre)
    silu_gate = gate_pre * sigmoid_gate
    hidden = (silu_gate * up_pre).astype(bf16)
    up_grad = (hidden_grad * silu_gate).astype(bf16)
    gate_grad = (
        hidden_grad * up_pre * sigmoid_gate * (1.0 + gate_pre * (1.0 - sigmoid_gate))
    ).astype(bf16)
    return jnp.stack([hidden, gate_grad, up_grad])


def body(inputs, cotangent, gate_weight, up_weight, down_weight, gate_pattern, up_pattern, down_pattern):
    sizes = {"zhi": 4, "y": 4, "zlo": 8, "x": 4, "core": 2}
    rows, width = inputs.shape
    hidden_units = down_weight.shape[0]
    half = rows * sizes["zlo"] * sizes["x"]
    ny = sizes["y"]
    quarter = hidden_units // ny
    zhi, core = lax.axis_index("zhi"), lax.axis_index("core")

    keep = jnp.where(core == 0, (zhi ^ (zhi >> 1)) & 1, zhi >> 1)
    own_first = keep == core

    spread_width = spread_matrix(width // 4)
    spread_units = spread_matrix(hidden_units // 4)
    gate_keep = dot(jnp.concatenate(keep_planes(gate_pattern.T), axis=1), spread_width, ((1,), (0,))) > 0.5
    up_keep = dot(jnp.concatenate(keep_planes(up_pattern.T), axis=1), spread_width, ((1,), (0,))) > 0.5
    down_keep = dot(spread_units, jnp.concatenate(keep_planes(down_pattern), axis=0), ((0,), (0,))) > 0.5
    zero = jnp.zeros((), bf16)
    gate_eff = jnp.where(gate_keep, gate_weight.T, zero)
    up_eff = jnp.where(up_keep, up_weight.T, zero)
    down_eff = jnp.where(down_keep, down_weight, zero)
    weight_tops = jnp.stack([top(gate_weight), top(up_weight), top(down_weight)])

    both = jnp.stack([inputs, cotangent])
    both = gather_by_exchange(both, "zlo", sizes["zlo"])
    both = gather_by_exchange(both, "x", sizes["x"])
    own = both.transpose(2, 0, 1, 3, 4).reshape(2, half, width)
    other = lax.ppermute(own, "core", [(0, 1), (1, 0)])
    kept_side = jnp.where(own_first, own, other)
    sent_side = jnp.where(own_first, other, own)
    token_tops = jnp.maximum(
        jnp.max(jnp.abs(own), axis=(1, 2)), jnp.max(jnp.abs(other), axis=(1, 2))
    ).astype(f32)
    bounds = weight_tops * jnp.stack([token_tops[0], token_tops[0], token_tops[1]])
    power = power_of(bounds * (width / 2))[:, None, None]

    def summed_over_y(side):
        partial = jnp.stack(
            [
                dot(gate_eff, side[0], ((1,), (1,))).reshape(ny, quarter, half),
                dot(up_eff, side[0], ((1,), (1,))).reshape(ny, quarter, half),
                dot(down_eff, side[1], ((1,), (1,))).reshape(ny, quarter, half),
            ],
            axis=1,
        )
        values, powers = from_link(lax.all_to_all(to_link(partial, power), "y", 0, 0))
        return values.sum(axis=0), powers.max(axis=0) + 2.0

    sent, sent_power = summed_over_y(sent_side)
    values, _ = from_link(zhi_exchange(to_link(sent, sent_power), 1, 3))
    kept, kept_power = summed_over_y(kept_side)
    kept = kept + values
    values, _ = from_link(zhi_exchange(to_link(kept, kept_power + 4.0), 3, 1))
    kept = kept + values

    mine = swiglu_back(kept[0], kept[1], kept[2])
    theirs = zhi_exchange(mine, 1, 3)

    def units(block):
        block = gather_by_exchange(block, "y", ny)
        return block.transpose(1, 0, 2, 3).reshape(3, hidden_units, half)

    first, second = units(mine), units(theirs)

    def back_of(side):
        return dot(side[1], gate_eff, ((0,), (0,))) + dot(side[2], up_eff, ((0,), (0,)))

    back_first, back_second = back_of(first), back_of(second)
    stays = jnp.where(own_first, back_first, back_second)
    leaves = jnp.where(own_first, back_second, back_first)
    back = stays + lax.ppermute(leaves, "core", [(0, 1), (1, 0)])
    back = lax.all_to_all(back.reshape(sizes["x"], half // sizes["x"], width), "x", 0, 0).sum(axis=0)
    back = lax.all_to_all(back.reshape(sizes["zlo"], rows, width), "zlo", 0, 0).sum(axis=0)

    def weight_grad(member, side):
        return dot(first[member], kept_side[side], ((1,), (0,))) + dot(
            second[member], sent_side[side], ((1,), (0,))
        )

    grad_gate = jnp.where(gate_keep, weight_grad(1, 0), 0.0).astype(bf16)
    grad_up = jnp.where(up_keep, weight_grad(2, 0), 0.0).astype(bf16)
    grad_down = jnp.where(down_keep, weight_grad(0, 1), 0.0).astype(bf16)
    return (back.astype(bf16), grad_gate.T, grad_up.T, grad_down)


def solution(mesh):
    fine = Mesh(
        np.asarray(mesh.devices).reshape(4, 4, 8, 4, 2), ("zhi", "y", "zlo", "x", "core")
    )
    row, col = ("zhi", "y"), ("zlo", "x", "core")
    return jax.shard_map(
        body,
        mesh=fine,
        in_specs=(
            P(col, row),
            P(col, row),
            P(row, col),
            P(row, col),
            P(col, row),
            P(row, col),
            P(row, col),
            P(col, row),
        ),
        out_specs=(P(col, row), P(row, col), P(row, col), P(col, row)),
        check_vma=False,
    )
```

time: 223 us -> 215 us (0.964)
  blocking collectives: 32.6 us -> 0 us
  starting transfers between devices: 59.8 us -> 87.9 us
  waiting for transfers between devices: 107 us -> 89.4 us
  local copies, waits for them, and re-layouts: 2.32 us -> 8.92 us
  matrix products: 8.29 us -> 12.5 us
  other arithmetic: 10.6 us -> 13.4 us
    all_to_all x2 -> x0, blocking collectives: 28.1 us -> none  [the longest x1 15.2 us: gather_by_exchange(): lax.all_to_all(jnp.broadcast_to(block[None], (size, *block.shape)), axis,...]
    all_to_all x1 -> x3, waiting for transfers between devices: 33.9 us -> 19.2 us  [the longest x2 11.6 us: summed_over_y(): lax.all_to_all(to_link(partial, power), 'y', 0, 0)]
    ppermute x3, waiting for transfers between devices: 54.1 us -> 43.7 us  [zhi_exchange(): return lax.ppermute(block, ('zhi', 'core'), pairs)]
    all_to_all x1 -> x3, starting transfers between devices: 3.66 us -> 13.7 us  [the longest x2 6.98 us: summed_over_y(): lax.all_to_all(to_link(partial, power), 'y', 0, 0)]
    all_to_all x2 -> x4, starting transfers between devices: 19.4 us -> 28.4 us  [gather_by_exchange(): lax.all_to_all(jnp.broadcast_to(block[None], (size, *block.shape)), axis,...]
    all_to_all x2 -> x4, waiting for transfers between devices: 9.45 us -> 17.3 us  [gather_by_exchange(): lax.all_to_all(jnp.broadcast_to(block[None], (size, *block.shape)), axis,...]
    all_gather x2 -> x0, blocking collectives: 4.48 us -> none  [the longest x1 2.31 us: body(): tokens = lax.all_gather(both[0], 'core', axis=0, tiled=True)]
    dot_general x11 -> x19, matrix products: 8.29 us -> 12.5 us  [dot(): return lax.dot_general(a, b, (dims, ((), ())), preferred_element_type=f32)]
  transfers between devices with their start and end apart: 8 -> 13, of which waited for: 8 -> 10; matrix products, arithmetic and copies ran while one was open for 5% -> 8% of each run, Pallas kernels for 0% -> 0%
where the time goes in v3:
time: 215 us; the launch traced here: 213 us
  waiting for transfers between devices  89.4 us (42%)
  starting transfers between devices  87.9 us (41%)
  other arithmetic  13.4 us (6%)
  matrix products  12.5 us (6%)
  local copies, waits for them, and re-layouts  8.92 us (4%)
    ppermute x3, waiting for transfers between devices, zhi_exchange(): return lax.ppermute(block, ('zhi', 'core'), pairs)  43.7 us
    ppermute x3, starting transfers between devices, zhi_exchange(): return lax.ppermute(block, ('zhi', 'core'), pairs)  28.7 us
    all_to_all x4, starting transfers between devices, gather_by_exchange(): lax.all_to_all(jnp.broadcast_to(block[None], (size, *block.shape)), axis,...  28.4 us
    all_to_all x4, waiting for transfers between devices, gather_by_exchange(): lax.all_to_all(jnp.broadcast_to(block[None], (size, *block.shape)), axis,...  17.3 us
    all_to_all x1, starting transfers between devices, body(): lax.all_to_all(back.reshape(sizes['zlo'], rows, width), 'zlo', 0, 0)  13.3 us
    dot_general x19, matrix products, dot(): return lax.dot_general(a, b, (dims, ((), ())), preferred_element_type=f32)  12.5 us
    all_to_all x2, waiting for transfers between devices, summed_over_y(): lax.all_to_all(to_link(partial, power), 'y', 0, 0)  11.6 us
    all_to_all x1, waiting for transfers between devices, body(): lax.all_to_all(back.reshape(sizes['x'], half // sizes['x'], width), 'x',...  7.51 us
  transfers between devices with their start and end apart: 13, of which 10 were waited for; matrix products, arithmetic and copies ran while one was open for 8% of the time, Pallas kernels for 0%

profile of v3, /device:TPU:6, one launch (start us, length us, event | category | flops | bytes accessed | tf_op | source)
XLA Modules:
  0.0 213.3 jit_solution(14534628108193415767)
XLA Ops:
  0.7 0.8 pad_maximum_fusion.5
  1.5 0.7 broadcast_in_dim.28
  2.1 12.5 %all-to-all-start = ((bf16[8,2,8,512]{3,2,1,0:T(8,128)(2,1)}), bf16[8,2,8,512]{3,2,1,0:T(8,128)(2,1)S(1)}, u32[]{:S(2)}, u32[]{:S(2)}) async-start(bf16[8,2,8,512]{3,2,1,0:T(8,128)(2,1)} %broadcast_in_dim.28), calls=%async_computation | async-start | bytes 262144 | tf_op jit(solution)/shard_map/all_to_all | solution.py:33
  14.7 1.1 or_or_fusion.3
  15.7 1.0 or_or_fusion.2
  16.8 0.7 abs_reduce_fusion.4
  18.6 0.7 abs_reduce_fusion.3
  19.5 1.5 bitcast_select_fusion.1
  21.0 5.5 %all-to-all-done = bf16[8,2,8,512]{3,2,1,0:T(8,128)(2,1)S(1)} async-done(((bf16[8,2,8,512]{3,2,1,0:T(8,128)(2,1)}), bf16[8,2,8,512]{3,2,1,0:T(8,128)(2,1)S(1)}, u32[]{:S(2)}, u32[]{:S(2)}) %all-to-all-start) | async-done | bytes 131104 | tf_op jit(solution)/shard_map/all_to_all | solution.py:33
  26.6 0.8 broadcast_in_dim.29
  27.5 6.8 %all-to-all-start.1 = ((bf16[4,8,2,8,512]{4,3,1,2,0:T(8,128)(2,1)}), bf16[4,8,2,8,512]{4,3,1,2,0:T(8,128)(2,1)S(1)}, u32[]{:S(2)}, u32[]{:S(2)}) async-start(bf16[4,8,2,8,512]{4,3,1,2,0:T(8,128)(2,1)} %broadcast_in_dim.29), calls=%async_computation.1 | async-start | bytes 1048576 | tf_op jit(solution)/shard_map/all_to_all | solution.py:33
  34.3 1.5 bitcast_select_fusion
  35.8 4.5 %all-to-all-done.1 = bf16[4,8,2,8,512]{4,3,1,2,0:T(8,128)(2,1)S(1)} async-done(((bf16[4,8,2,8,512]{4,3,1,2,0:T(8,128)(2,1)}), bf16[4,8,2,8,512]{4,3,1,2,0:T(8,128)(2,1)S(1)}, u32[]{:S(2)}, u32[]{:S(2)}) %all-to-all-start.1) | async-done | bytes 524320 | tf_op jit(solution)/shard_map/all_to_all | solution.py:33
  40.3 1.9 collective-permute-start
  42.3 2.3 %broadcast_select_fusion.3 = (bf16[448,512]{1,0:T(8,128)(2,1)S(1)}, bf16[]{:T(256)}, pred[448,512]{1,0:T(32,128)(4,1)}) fusion(bf16[448,512]{1,0:T(8,128)(2,1)S(1)} %copy-done.18, pred[112,512]{1,0:T(8,128)(4,1)S(1)} %or_or_fusion, pred[112,512]{1,0:T(8,128)(4,1)S(1)} %get-tuple-element.35, pred[112,512]{1,0:T(8,128)(4,1)S(1)} %get-tuple-element.32, ...), kind=kOutput, calls=%fused_computation.96 | convolution fusion | flops 208130048 | bytes 1384322 | tf_op jit(solution)/shard_map/dot_general | solution.py:29
  47.0 2.0 multiply_exponential_fusion.2
  49.0 0.4 fusion.3
  49.9 1.1 copy.34
  50.9 3.5 %all-to-all-start.3 = ((f16[4,3,120,256]{3,2,1,0:T(8,128)(2,1)}), f16[4,3,120,256]{3,2,1,0:T(8,128)(2,1)S(1)}, u32[]{:S(2)}, u32[]{:S(2)}) async-start(f16[4,3,120,256]{3,2,1,0:T(8,128)(2,1)} %copy.34), calls=%async_computation.3 | async-start | bytes 1474560 | tf_op jit(solution)/shard_map/all_to_all | solution.py:123
  54.4 1.0 copy.32
  55.5 11.6 %all-to-all-done.3 = f16[4,3,120,256]{3,2,1,0:T(8,128)(2,1)S(1)} async-done(((f16[4,3,120,256]{3,2,1,0:T(8,128)(2,1)}), f16[4,3,120,256]{3,2,1,0:T(8,128)(2,1)S(1)}, u32[]{:S(2)}, u32[]{:S(2)}) %all-to-all-start.3) | async-done | bytes 737312 | tf_op jit(solution)/shard_map/all_to_all | solution.py:123
  67.1 3.5 %all-to-all-start.2 = ((f16[4,3,120,256]{3,2,1,0:T(8,128)(2,1)}), f16[4,3,120,256]{3,2,1,0:T(8,128)(2,1)S(1)}, u32[]{:S(2)}, u32[]{:S(2)}) async-start(f16[4,3,120,256]{3,2,1,0:T(8,128)(2,1)} %copy.32), calls=%async_computation.2 | async-start | bytes 1474560 | tf_op jit(solution)/shard_map/all_to_all | solution.py:123
  71.3 14.4 %collective-permute-start.1 = (f16[3,120,256]{2,1,0:T(8,128)(2,1)S(1)}, f16[3,120,256]{2,1,0:T(8,128)(2,1)S(1)}, u32[]{:S(2)}, u32[]{:S(2)}) collective-permute-start(f16[3,120,256]{2,1,0:T(8,128)(2,1)S(1)} %pad_maximum_fusion.2), channel_id=1, source_target_pairs={{0,256},{1,769},{256,0},{257,513},{512,768},{513,257},{768,512},{7... | collective-permute-start | bytes 552968 | tf_op jit(solution)/shard_map/ppermute | solution.py:40
  86.1 17.0 %collective-permute-done.1 = f16[3,120,256]{2,1,0:T(8,128)(2,1)S(1)} collective-permute-done((f16[3,120,256]{2,1,0:T(8,128)(2,1)S(1)}, f16[3,120,256]{2,1,0:T(8,128)(2,1)S(1)}, u32[]{:S(2)}, u32[]{:S(2)}) %collective-permute-start.1) | collective-permute-done | bytes 184352 | tf_op jit(solution)/shard_map/ppermute | solution.py:40
  103.5 7.7 %collective-permute-start.2 = (f16[3,120,256]{2,1,0:T(8,128)(2,1)S(1)}, f16[3,120,256]{2,1,0:T(8,128)(2,1)S(1)}, u32[]{:S(2)}, u32[]{:S(2)}) collective-permute-start(f16[3,120,256]{2,1,0:T(8,128)(2,1)S(1)} %pad_maximum_fusion.3), channel_id=1, source_target_pairs={{0,768},{1,257},{256,512},{257,1},{512,256},{513,769},{768,0},{769... | collective-permute-start | bytes 552968 | tf_op jit(solution)/shard_map/ppermute | solution.py:40
  111.1 16.0 %collective-permute-done.2 = f16[3,120,256]{2,1,0:T(8,128)(2,1)S(1)} collective-permute-done((f16[3,120,256]{2,1,0:T(8,128)(2,1)S(1)}, f16[3,120,256]{2,1,0:T(8,128)(2,1)S(1)}, u32[]{:S(2)}, u32[]{:S(2)}) %collective-permute-start.2) | collective-permute-done | bytes 184352 | tf_op jit(solution)/shard_map/ppermute | solution.py:40
  127.5 0.9 broadcast_in_dim.33
  128.4 4.6 %all-to-all-start.4 = ((bf16[4,3,112,256]{3,2,1,0:T(8,128)(2,1)}), bf16[4,3,112,256]{3,2,1,0:T(8,128)(2,1)S(1)}, u32[]{:S(2)}, u32[]{:S(2)}) async-start(bf16[4,3,112,256]{3,2,1,0:T(8,128)(2,1)} %broadcast_in_dim.33), calls=%async_computation.4 | async-start | bytes 1376256 | tf_op jit(solution)/shard_map/all_to_all | solution.py:33
  133.0 6.6 %collective-permute-start.3 = (bf16[3,112,256]{2,1,0:T(8,128)(2,1)S(1)}, bf16[3,112,256]{2,1,0:T(8,128)(2,1)S(1)}, u32[]{:S(2)}, u32[]{:S(2)}) collective-permute-start(bf16[3,112,256]{2,1,0:T(8,128)(2,1)S(1)} %pad_maximum_fusion.4), channel_id=1, source_target_pairs={{0,256},{1,769},{256,0},{257,513},{512,768},{513,257},{768,512},{7... | collective-permute-start | bytes 516104 | tf_op jit(solution)/shard_map/ppermute | solution.py:40
  139.6 10.7 %collective-permute-done.3 = bf16[3,112,256]{2,1,0:T(8,128)(2,1)S(1)} collective-permute-done((bf16[3,112,256]{2,1,0:T(8,128)(2,1)S(1)}, bf16[3,112,256]{2,1,0:T(8,128)(2,1)S(1)}, u32[]{:S(2)}, u32[]{:S(2)}) %collective-permute-start.3) | collective-permute-done | bytes 172064 | tf_op jit(solution)/shard_map/ppermute | solution.py:40
  150.3 0.9 broadcast_in_dim.66
  151.2 4.5 %all-to-all-start.5 = ((bf16[4,3,112,256]{3,2,1,0:T(8,128)(2,1)}), bf16[4,3,112,256]{3,2,1,0:T(8,128)(2,1)S(1)}, u32[]{:S(2)}, u32[]{:S(2)}) async-start(bf16[4,3,112,256]{3,2,1,0:T(8,128)(2,1)} %broadcast_in_dim.66), calls=%async_computation.5 | async-start | bytes 1376256 | tf_op jit(solution)/shard_map/all_to_all | solution.py:33
  155.7 0.7 fusion.90
  157.5 7.3 %all-to-all-done.5 = bf16[4,3,112,256]{3,2,1,0:T(8,128)(2,1)S(1)} async-done(((bf16[4,3,112,256]{3,2,1,0:T(8,128)(2,1)}), bf16[4,3,112,256]{3,2,1,0:T(8,128)(2,1)S(1)}, u32[]{:S(2)}, u32[]{:S(2)}) %all-to-all-start.5) | async-done | bytes 688160 | tf_op jit(solution)/shard_map/all_to_all | solution.py:33
  164.9 0.7 fusion.91
  166.6 1.9 collective-permute-start.4
  168.6 1.9 collective-permute-done.4
  170.4 0.9 select_add_fusion
  171.4 6.7 %all-to-all-start.6 = ((f32[4,64,512]{2,1,0:T(8,128)}), f32[4,64,512]{2,1,0:T(8,128)}, u32[]{:S(2)}, u32[]{:S(2)}) async-start(f32[4,64,512]{2,1,0:T(8,128)} %bitcast.40), calls=%async_computation.6 | async-start | bytes 1048576 | tf_op jit(solution)/shard_map/all_to_all | solution.py:149
  178.7 7.5 %all-to-all-done.6 = f32[4,64,512]{2,1,0:T(8,128)} async-done(((f32[4,64,512]{2,1,0:T(8,128)}), f32[4,64,512]{2,1,0:T(8,128)}, u32[]{:S(2)}, u32[]{:S(2)}) %all-to-all-start.6) | async-done | bytes 524320 | tf_op jit(solution)/shard_map/all_to_all | solution.py:149
  186.2 1.7 reduce_sum.38
  187.9 13.3 %all-to-all-start.7 = ((f32[8,8,512]{2,1,0:T(8,128)}), f32[8,8,512]{2,1,0:T(8,128)S(1)}, u32[]{:S(2)}, u32[]{:S(2)}) async-start(f32[8,8,512]{2,1,0:T(8,128)} %bitcast.132), calls=%async_computation.7 | async-start | bytes 262144 | tf_op jit(solution)/shard_map/all_to_all | solution.py:150
  201.5 0.6 copy-done.16
  202.1 1.1 fusion.9
  203.2 1.1 fusion.8
  204.3 1.1 fusion.7
  205.3 7.4 %all-to-all-done.7 = f32[8,8,512]{2,1,0:T(8,128)S(1)} async-done(((f32[8,8,512]{2,1,0:T(8,128)}), f32[8,8,512]{2,1,0:T(8,128)S(1)}, u32[]{:S(2)}, u32[]{:S(2)}) %all-to-all-start.7) | async-done | bytes 131104 | tf_op jit(solution)/shard_map/all_to_all | solution.py:150
  212.7 0.6 reduce_sum.39
  (98 shorter events, 8.8 us)
Async XLA Ops:
  0.6 16.2 %copy-start.13 = (bf16[512,448]{0,1:T(8,128)(2,1)S(1)}, bf16[512,448]{0,1:T(8,128)(2,1)}, u32[]{:S(2)}) copy-start(bf16[512,448]{0,1:T(8,128)(2,1)} %param.10) | copy-start | bytes 1376260
  0.6 16.8 %copy-start = (s32[128,448]{0,1:T(8,128)S(1)}, s32[128,448]{0,1:T(8,128)}, u32[]{:S(2)}) copy-start(s32[128,448]{0,1:T(8,128)} %param.13) | copy-start | bytes 688132
  0.7 17.1 %copy-start.1 = (s32[128,448]{0,1:T(8,128)S(1)}, s32[128,448]{0,1:T(8,128)}, u32[]{:S(2)}) copy-start(s32[128,448]{0,1:T(8,128)} %param.14) | copy-start | bytes 688132
  2.1 24.5 %all-to-all-start = ((bf16[8,2,8,512]{3,2,1,0:T(8,128)(2,1)}), bf16[8,2,8,512]{3,2,1,0:T(8,128)(2,1)S(1)}, u32[]{:S(2)}, u32[]{:S(2)}) async-start(bf16[8,2,8,512]{3,2,1,0:T(8,128)(2,1)} %broadcast_in_dim.28), calls=%async_computation | async-start | bytes 262144 | tf_op jit(solution)/shard_map/all_to_all | solution.py:33
  17.6 1.0 copy-start.14
  17.7 1.6 copy-start.2
  27.5 12.9 %all-to-all-start.1 = ((bf16[4,8,2,8,512]{4,3,1,2,0:T(8,128)(2,1)}), bf16[4,8,2,8,512]{4,3,1,2,0:T(8,128)(2,1)S(1)}, u32[]{:S(2)}, u32[]{:S(2)}) async-start(bf16[4,8,2,8,512]{4,3,1,2,0:T(8,128)(2,1)} %broadcast_in_dim.29), calls=%async_computation.1 | async-start | bytes 1048576 | tf_op jit(solution)/shard_map/all_to_all | solution.py:33
  34.3 8.0 %copy-start.18 = (bf16[448,512]{1,0:T(8,128)(2,1)S(1)}, bf16[448,512]{1,0:T(8,128)(2,1)}, u32[]{:S(2)}) copy-start(bf16[448,512]{1,0:T(8,128)(2,1)} %param.12) | copy-start | bytes 1376260
  40.3 4.4 %collective-permute-start = (bf16[2,256,512]{2,1,0:T(8,128)(2,1)S(1)}, bf16[2,256,512]{2,1,0:T(8,128)(2,1)S(1)}, u32[]{:S(2)}, u32[]{:S(2)}) collective-permute-start(bf16[2,256,512]{2,1,0:T(8,128)(2,1)S(1)} %bitcast.119), channel_id=1, source_target_pairs={{0,1},{1,0},{2,3},{3,2},{4,5},{5,4},{6,7},{7,6},{8,9},{9,8},{10,11... | collective-permute-start | bytes 1572872 | tf_op jit(solution)/shard_map/ppermute | solution.py:105
  50.9 16.2 %all-to-all-start.3 = ((f16[4,3,120,256]{3,2,1,0:T(8,128)(2,1)}), f16[4,3,120,256]{3,2,1,0:T(8,128)(2,1)S(1)}, u32[]{:S(2)}, u32[]{:S(2)}) async-start(f16[4,3,120,256]{3,2,1,0:T(8,128)(2,1)} %copy.34), calls=%async_computation.3 | async-start | bytes 1474560 | tf_op jit(solution)/shard_map/all_to_all | solution.py:123
  67.1 18.5 %all-to-all-start.2 = ((f16[4,3,120,256]{3,2,1,0:T(8,128)(2,1)}), f16[4,3,120,256]{3,2,1,0:T(8,128)(2,1)S(1)}, u32[]{:S(2)}, u32[]{:S(2)}) async-start(f16[4,3,120,256]{3,2,1,0:T(8,128)(2,1)} %copy.32), calls=%async_computation.2 | async-start | bytes 1474560 | tf_op jit(solution)/shard_map/all_to_all | solution.py:123
  71.3 31.8 %collective-permute-start.1 = (f16[3,120,256]{2,1,0:T(8,128)(2,1)S(1)}, f16[3,120,256]{2,1,0:T(8,128)(2,1)S(1)}, u32[]{:S(2)}, u32[]{:S(2)}) collective-permute-start(f16[3,120,256]{2,1,0:T(8,128)(2,1)S(1)} %pad_maximum_fusion.2), channel_id=1, source_target_pairs={{0,256},{1,769},{256,0},{257,513},{512,768},{513,257},{768,512},{7... | collective-permute-start | bytes 552968 | tf_op jit(solution)/shard_map/ppermute | solution.py:40
  103.5 23.6 %collective-permute-start.2 = (f16[3,120,256]{2,1,0:T(8,128)(2,1)S(1)}, f16[3,120,256]{2,1,0:T(8,128)(2,1)S(1)}, u32[]{:S(2)}, u32[]{:S(2)}) collective-permute-start(f16[3,120,256]{2,1,0:T(8,128)(2,1)S(1)} %pad_maximum_fusion.3), channel_id=1, source_target_pairs={{0,768},{1,257},{256,512},{257,1},{512,256},{513,769},{768,0},{769... | collective-permute-start | bytes 552968 | tf_op jit(solution)/shard_map/ppermute | solution.py:40
  128.4 21.9 %all-to-all-start.4 = ((bf16[4,3,112,256]{3,2,1,0:T(8,128)(2,1)}), bf16[4,3,112,256]{3,2,1,0:T(8,128)(2,1)S(1)}, u32[]{:S(2)}, u32[]{:S(2)}) async-start(bf16[4,3,112,256]{3,2,1,0:T(8,128)(2,1)} %broadcast_in_dim.33), calls=%async_computation.4 | async-start | bytes 1376256 | tf_op jit(solution)/shard_map/all_to_all | solution.py:33
  133.0 17.3 %collective-permute-start.3 = (bf16[3,112,256]{2,1,0:T(8,128)(2,1)S(1)}, bf16[3,112,256]{2,1,0:T(8,128)(2,1)S(1)}, u32[]{:S(2)}, u32[]{:S(2)}) collective-permute-start(bf16[3,112,256]{2,1,0:T(8,128)(2,1)S(1)} %pad_maximum_fusion.4), channel_id=1, source_target_pairs={{0,256},{1,769},{256,0},{257,513},{512,768},{513,257},{768,512},{7... | collective-permute-start | bytes 516104 | tf_op jit(solution)/shard_map/ppermute | solution.py:40
  151.2 13.6 %all-to-all-start.5 = ((bf16[4,3,112,256]{3,2,1,0:T(8,128)(2,1)}), bf16[4,3,112,256]{3,2,1,0:T(8,128)(2,1)S(1)}, u32[]{:S(2)}, u32[]{:S(2)}) async-start(bf16[4,3,112,256]{3,2,1,0:T(8,128)(2,1)} %broadcast_in_dim.66), calls=%async_computation.5 | async-start | bytes 1376256 | tf_op jit(solution)/shard_map/all_to_all | solution.py:33
  156.4 0.7 copy-start.5
  156.4 0.8 copy-start.9
  165.6 0.7 copy-start.7
  165.6 1.0 copy-start.3
  166.6 3.8 %collective-permute-start.4 = (f32[256,512]{1,0:T(8,128)S(1)}, f32[256,512]{1,0:T(8,128)S(1)}, u32[]{:S(2)}, u32[]{:S(2)}) collective-permute-start(f32[256,512]{1,0:T(8,128)S(1)} %get-tuple-element.64), channel_id=1, source_target_pairs={{0,1},{1,0},{2,3},{3,2},{4,5},{5,4},{6,7},{7,6},{8,9},{9,8},{10,11... | collective-permute-start | bytes 1572872 | tf_op jit(solution)/shard_map/ppermute | solution.py:148
  170.4 7.6 %copy-start.4 = (bf16[1,4,112,256]{3,2,0,1:T(8,128)(2,1)S(1)}, bf16[1,4,112,256]{3,2,0,1:T(8,128)(2,1)}, u32[]{:S(2)}) copy-start(bf16[1,4,112,256]{3,2,0,1:T(8,128)(2,1)} %copy-done.3) | copy-start | bytes 688132
  171.4 7.0 %copy-start.8 = (bf16[1,4,112,256]{3,2,0,1:T(8,128)(2,1)S(1)}, bf16[1,4,112,256]{3,2,0,1:T(8,128)(2,1)}, u32[]{:S(2)}) copy-start(bf16[1,4,112,256]{3,2,0,1:T(8,128)(2,1)} %copy-done.7) | copy-start | bytes 688132
  171.4 14.8 %all-to-all-start.6 = ((f32[4,64,512]{2,1,0:T(8,128)}), f32[4,64,512]{2,1,0:T(8,128)}, u32[]{:S(2)}, u32[]{:S(2)}) async-start(f32[4,64,512]{2,1,0:T(8,128)} %bitcast.40), calls=%async_computation.6 | async-start | bytes 1048576 | tf_op jit(solution)/shard_map/all_to_all | solution.py:149
  178.4 22.8 %copy-start.12 = (bf16[1,4,112,256]{3,2,0,1:T(8,128)(2,1)S(1)}, bf16[1,4,112,256]{3,2,0,1:T(8,128)(2,1)}, u32[]{:S(2)}) copy-start(bf16[1,4,112,256]{3,2,0,1:T(8,128)(2,1)} %get-tuple-element.42) | copy-start | bytes 688132
  178.7 22.9 %copy-start.10 = (bf16[1,4,112,256]{3,2,0,1:T(8,128)(2,1)S(1)}, bf16[1,4,112,256]{3,2,0,1:T(8,128)(2,1)}, u32[]{:S(2)}) copy-start(bf16[1,4,112,256]{3,2,0,1:T(8,128)(2,1)} %copy-done.9) | copy-start | bytes 688132
  187.9 24.8 %all-to-all-start.7 = ((f32[8,8,512]{2,1,0:T(8,128)}), f32[8,8,512]{2,1,0:T(8,128)S(1)}, u32[]{:S(2)}, u32[]{:S(2)}) async-start(f32[8,8,512]{2,1,0:T(8,128)} %bitcast.132), calls=%async_computation.7 | async-start | bytes 262144 | tf_op jit(solution)/shard_map/all_to_all | solution.py:150
  201.2 0.9 copy-start.16
  201.5 1.7 copy-start.6
  201.5 1.7 copy-start.15
  203.2 1.1 copy-start.11
  203.2 1.1 copy-start.17

commit v4 on v3

v4 whole, which is shorter than its diff:
```python
import jax
import jax.numpy as jnp
import numpy as np
from jax import lax
from jax.experimental import pallas as pl
from jax.experimental.pallas import tpu as pltpu
from jax.sharding import Mesh, PartitionSpec as P

bf16 = jnp.bfloat16
f32 = jnp.float32
keep_sets = ((0, 1, 2), (0, 3, 4), (1, 3, 5), (2, 4, 5))


def keep_planes(pattern):
    planes = []
    for members in keep_sets:
        kept = pattern == members[0]
        for member in members[1:]:
            kept = kept | (pattern == member)
        planes.append(kept.astype(bf16))
    return planes


def spread_matrix(groups):
    row = lax.broadcasted_iota(jnp.int32, (4 * groups, 4 * groups), 0)
    col = lax.broadcasted_iota(jnp.int32, (4 * groups, 4 * groups), 1)
    return ((row % groups) * 4 + row // groups == col).astype(bf16)


def dot(a, b, dims):
    return lax.dot_general(a, b, (dims, ((), ())), preferred_element_type=f32)


def gather_by_exchange(block, axis, size):
    return lax.all_to_all(jnp.broadcast_to(block[None], (size, *block.shape)), axis, 0, 0)


def zhi_exchange(block, flip0, flip1):
    pairs = [
        (z * 2 + c, (z ^ (flip0, flip1)[c]) * 2 + c) for z in range(4) for c in range(2)
    ]
    return lax.ppermute(block, ("zhi", "core"), pairs)


EXTRA = 16


def pack(values):
    rows, powers = [], []
    for value in values:
        most = jnp.max(jnp.abs(value), axis=0, keepdims=True)
        power = jnp.ceil(jnp.log2(jnp.maximum(most, 1e-30))) - 14.0
        rows.append(to_int16(jnp.round(value * jnp.exp2(-power))))
        powers.append(power)
    spot = lax.broadcasted_iota(jnp.int32, (EXTRA, values[0].shape[1]), 0)
    tail = jnp.where(spot == 0, powers[0], jnp.where(spot == 1, powers[1], powers[2]))
    return rows, to_int16(tail)


def to_int16(values):
    return values.astype(jnp.int32).astype(jnp.int16)


def wide(block):
    return block.astype(jnp.int32).astype(f32)


def unpack(block, units):
    powers = wide(block[3 * units : 3 * units + EXTRA, :])
    return [
        wide(block[i * units : (i + 1) * units, :]) * jnp.exp2(powers[i : i + 1, :])
        for i in range(3)
    ]


def partial_kernel(gate_ref, up_ref, down_ref, own_ref, other_ref, out_ref):
    ny, units = out_ref.shape[0], gate_ref.shape[0] // out_ref.shape[0]
    half = own_ref.shape[1]
    for spot, side in enumerate((own_ref, other_ref)):
        products = [
            dot(gate_ref[...], side[0], ((1,), (1,))),
            dot(up_ref[...], side[0], ((1,), (1,))),
            dot(down_ref[...], side[1], ((1,), (1,))),
        ]
        for c in range(ny):
            rows, tail = pack([p[c * units : (c + 1) * units] for p in products])
            for i in range(3):
                out_ref[c, i * units : (i + 1) * units, spot * half : (spot + 1) * half] = rows[i]
            out_ref[c, 3 * units :, spot * half : (spot + 1) * half] = tail


def first_sum_kernel(block_ref, *outs):
    ny, units = block_ref.shape[0], outs[0].shape[1]
    half = outs[0].shape[2]
    for spot in range(2):
        lanes = slice(spot * half, (spot + 1) * half)
        total = [0.0, 0.0, 0.0]
        for c in range(ny):
            powers = wide(block_ref[c, 3 * units :, lanes])
            for i in range(3):
                total[i] += wide(block_ref[c, i * units : (i + 1) * units, lanes]) * jnp.exp2(
                    powers[i : i + 1, :]
                )
        store(total, outs[2 * spot], outs[2 * spot + 1])


def store(total, total_ref, send_ref):
    units = total_ref.shape[1]
    rows, tail = pack(total)
    for i in range(3):
        total_ref[i] = total[i]
        send_ref[i * units : (i + 1) * units, :] = rows[i]
    send_ref[3 * units :, :] = tail


def next_sum_kernel(total_ref, block_ref, out_ref, send_ref):
    parts = unpack(block_ref, total_ref.shape[1])
    store([total_ref[i] + parts[i] for i in range(3)], out_ref, send_ref)


def swiglu_kernel(total_ref, block_ref, out_ref):
    units = total_ref.shape[1]
    parts = unpack(block_ref, units)
    gate_pre, up_pre, hidden_grad = [total_ref[i] + parts[i] for i in range(3)]
    sigmoid_gate = jax.nn.sigmoid(gate_pre)
    silu_gate = gate_pre * sigmoid_gate
    results = (
        silu_gate * up_pre,
        hidden_grad * up_pre * sigmoid_gate * (1.0 + gate_pre * (1.0 - sigmoid_gate)),
        hidden_grad * silu_gate,
    )
    for i, result in enumerate(results):
        result = result.astype(bf16)
        for c in range(out_ref.shape[0]):
            out_ref[c, i * units : (i + 1) * units, :] = result


def call(kernel, outs, *args):
    return pl.pallas_call(
        kernel,
        out_shape=[jax.ShapeDtypeStruct(shape, kind) for shape, kind in outs],
        compiler_params=pltpu.CompilerParams(vmem_limit_bytes=32 * 2**20),
        cost_estimate=pl.CostEstimate(flops=2 * 10**10, bytes_accessed=1024, transcendentals=0),
    )(*args)


def body(inputs, cotangent, gate_weight, up_weight, down_weight, gate_pattern, up_pattern, down_pattern):
    sizes = {"zhi": 4, "y": 4, "zlo": 8, "x": 4, "core": 2}
    rows, width = inputs.shape
    hidden_units = down_weight.shape[0]
    half = rows * sizes["zlo"] * sizes["x"]
    ny = sizes["y"]
    quarter = hidden_units // ny
    spread_width = spread_matrix(width // 4)
    spread_units = spread_matrix(hidden_units // 4)
    gate_keep = dot(jnp.concatenate(keep_planes(gate_pattern.T), axis=1), spread_width, ((1,), (0,))) > 0.5
    up_keep = dot(jnp.concatenate(keep_planes(up_pattern.T), axis=1), spread_width, ((1,), (0,))) > 0.5
    down_keep = dot(spread_units, jnp.concatenate(keep_planes(down_pattern), axis=0), ((0,), (0,))) > 0.5
    zero = jnp.zeros((), bf16)
    gate_eff = jnp.where(gate_keep, gate_weight.T, zero)
    up_eff = jnp.where(up_keep, up_weight.T, zero)
    down_eff = jnp.where(down_keep, down_weight, zero)

    swap = [(0, 1), (1, 0)]
    both = jnp.stack([inputs, cotangent])
    both = gather_by_exchange(both, "zlo", sizes["zlo"])
    both = gather_by_exchange(both, "x", sizes["x"])
    own = both.transpose(2, 0, 1, 3, 4).reshape(2, half, width)
    other = lax.ppermute(own, "core", swap)

    i16 = jnp.int16
    packed = 3 * quarter + EXTRA
    (block,) = call(
        partial_kernel,
        [((ny, packed, 2 * half), i16)],
        gate_eff, up_eff, down_eff, own, other,
    )
    block = lax.all_to_all(block, "y", 0, 0)

    pair = [((3, quarter, half), f32), ((packed, half), i16)]
    total1, send1, total2, send2 = call(first_sum_kernel, pair + pair, block)
    got1 = zhi_exchange(send1, 1, 3)
    got2 = zhi_exchange(send2, 1, 3)
    total1, send1 = call(next_sum_kernel, pair, total1, got1)
    got1 = zhi_exchange(send1, 3, 1)
    total2, send2 = call(next_sum_kernel, pair, total2, got2)
    got2 = zhi_exchange(send2, 3, 1)
    spread = [((ny, 3 * quarter, half), bf16)]
    (spread1,) = call(swiglu_kernel, spread, total1, got1)
    second = lax.all_to_all(spread1, "y", 0, 0)
    (spread2,) = call(swiglu_kernel, spread, total2, got2)
    first = lax.all_to_all(spread2, "y", 0, 0)

    def units(block):
        block = block.reshape(ny, 3, quarter, half)
        return block.transpose(1, 0, 2, 3).reshape(3, hidden_units, half)

    first, second = units(first), units(second)

    def back_of(side):
        return dot(side[1], gate_eff, ((0,), (0,))) + dot(side[2], up_eff, ((0,), (0,)))

    back = back_of(second) + lax.ppermute(back_of(first), "core", swap)
    back = lax.all_to_all(back.reshape(sizes["x"], half // sizes["x"], width), "x", 0, 0).sum(axis=0)
    back = lax.all_to_all(back.reshape(sizes["zlo"], rows, width), "zlo", 0, 0).sum(axis=0)

    def weight_grad(member, side):
        return dot(first[member], other[side], ((1,), (0,))) + dot(
            second[member], own[side], ((1,), (0,))
        )

    grad_gate = jnp.where(gate_keep, weight_grad(1, 0), 0.0).astype(bf16)
    grad_up = jnp.where(up_keep, weight_grad(2, 0), 0.0).astype(bf16)
    grad_down = jnp.where(down_keep, weight_grad(0, 1), 0.0).astype(bf16)
    return (back.astype(bf16), grad_gate.T, grad_up.T, grad_down)


def solution(mesh):
    fine = Mesh(
        np.asarray(mesh.devices).reshape(4, 4, 8, 4, 2), ("zhi", "y", "zlo", "x", "core")
    )
    row, col = ("zhi", "y"), ("zlo", "x", "core")
    return jax.shard_map(
        body,
        mesh=fine,
        in_specs=(
            P(col, row),
            P(col, row),
            P(row, col),
            P(row, col),
            P(col, row),
            P(row, col),
            P(row, col),
            P(col, row),
        ),
        out_specs=(P(col, row), P(row, col), P(row, col), P(col, row)),
        check_vma=False,
    )
```

time: 215 us -> 212 us (0.986)
  blocking collectives: 0 us -> 22.7 us
  starting transfers between devices: 87.9 us -> 75.1 us
  other arithmetic: 13.4 us -> 5.14 us
  waiting for transfers between devices: 89.4 us -> 84.2 us
  local copies, waits for them, and re-layouts: 8.92 us -> 4.53 us
  Pallas kernels: 0 us -> 3.67 us
    all_to_all x0 -> x1, blocking collectives: none -> 22.7 us  [body(): block = lax.all_to_all(block, 'y', 0, 0)]
    all_to_all x1, starting transfers between devices: 13.3 us -> 3.37 us  [body(): lax.all_to_all(back.reshape(sizes['zlo'], rows, width), 'zlo', 0, 0)]
    all_to_all x4 -> x2, starting transfers between devices: 28.4 us -> 19.4 us  [gather_by_exchange(): lax.all_to_all(jnp.broadcast_to(block[None], (size, *block.shape)), axis,...]
    ppermute x3 -> x4, starting transfers between devices: 28.7 us -> 36.8 us  [zhi_exchange(): return lax.ppermute(block, ('zhi', 'core'), pairs)]
    all_to_all x4 -> x2, waiting for transfers between devices: 17.3 us -> 13.2 us  [gather_by_exchange(): lax.all_to_all(jnp.broadcast_to(block[None], (size, *block.shape)), axis,...]
    pallas_call x0 -> x6, Pallas kernels: none -> 3.67 us  [call(): pl.pallas_call(kernel, out_shape=[jax.ShapeDtypeStruct(shape, kind) for s...]
    ppermute x3 -> x4, waiting for transfers between devices: 43.7 us -> 46.4 us  [zhi_exchange(): return lax.ppermute(block, ('zhi', 'core'), pairs)]
    all_to_all x1, waiting for transfers between devices: 7.51 us -> 4.79 us  [body(): lax.all_to_all(back.reshape(sizes['x'], half // sizes['x'], width), 'x',...]
  transfers between devices with their start and end apart: 13 -> 12, of which waited for: 10 -> 8; matrix products, arithmetic and copies ran while one was open for 8% -> 9% of each run, Pallas kernels for 0% -> 1%
where the time goes in v4:
time: 212 us; the launch traced here: 210 us
  waiting for transfers between devices  84.2 us (40%)
  starting transfers between devices  75.1 us (35%)
  blocking collectives  22.7 us (11%)
  matrix products  13.7 us (6%)
  other arithmetic  5.14 us (2%)
  local copies, waits for them, and re-layouts  4.53 us (2%)
  Pallas kernels  3.67 us (2%)
    ppermute x4, waiting for transfers between devices, zhi_exchange(): return lax.ppermute(block, ('zhi', 'core'), pairs)  46.4 us
    ppermute x4, starting transfers between devices, zhi_exchange(): return lax.ppermute(block, ('zhi', 'core'), pairs)  36.8 us
    all_to_all x1, blocking collectives, body(): block = lax.all_to_all(block, 'y', 0, 0)  22.7 us
    all_to_all x2, starting transfers between devices, gather_by_exchange(): lax.all_to_all(jnp.broadcast_to(block[None], (size, *block.shape)), axis,...  19.4 us
    dot_general x13, matrix products, dot(): return lax.dot_general(a, b, (dims, ((), ())), preferred_element_type=f32)  13.7 us
    all_to_all x2, waiting for transfers between devices, gather_by_exchange(): lax.all_to_all(jnp.broadcast_to(block[None], (size, *block.shape)), axis,...  13.2 us
    all_to_all x1, waiting for transfers between devices, body(): first = lax.all_to_all(spread2, 'y', 0, 0)  9.57 us
    all_to_all x1, waiting for transfers between devices, body(): lax.all_to_all(back.reshape(sizes['zlo'], rows, width), 'zlo', 0, 0)  5.8 us
  transfers between devices with their start and end apart: 12, of which 8 were waited for; matrix products, arithmetic and copies ran while one was open for 9% of the time, Pallas kernels for 1%

profile of v4, /device:TPU:6, one launch (start us, length us, event | category | flops | bytes accessed | tf_op | source)
XLA Modules:
  0.0 210.1 jit_solution(1932908515199673691)
XLA Ops:
  0.7 0.8 pad_maximum_fusion
  1.4 0.7 broadcast_in_dim.27
  2.1 12.5 %all-to-all-start = ((bf16[8,2,8,512]{3,2,1,0:T(8,128)(2,1)}), bf16[8,2,8,512]{3,2,1,0:T(8,128)(2,1)S(1)}, u32[]{:S(2)}, u32[]{:S(2)}) async-start(bf16[8,2,8,512]{3,2,1,0:T(8,128)(2,1)} %broadcast_in_dim.27), calls=%async_computation | async-start | bytes 262144 | tf_op jit(solution)/shard_map/all_to_all | solution.py:35
  14.7 1.1 or_bitcast_fusion.7
  15.8 1.1 or_bitcast_fusion.6
  17.8 8.7 %all-to-all-done = bf16[8,2,8,512]{3,2,1,0:T(8,128)(2,1)S(1)} async-done(((bf16[8,2,8,512]{3,2,1,0:T(8,128)(2,1)}), bf16[8,2,8,512]{3,2,1,0:T(8,128)(2,1)S(1)}, u32[]{:S(2)}, u32[]{:S(2)}) %all-to-all-start) | async-done | bytes 131104 | tf_op jit(solution)/shard_map/all_to_all | solution.py:35
  26.6 0.9 broadcast_in_dim.28
  27.5 6.8 %all-to-all-start.1 = ((bf16[4,8,2,8,512]{4,3,1,2,0:T(8,128)(2,1)}), bf16[4,8,2,8,512]{4,3,1,2,0:T(8,128)(2,1)S(1)}, u32[]{:S(2)}, u32[]{:S(2)}) async-start(bf16[4,8,2,8,512]{4,3,1,2,0:T(8,128)(2,1)} %broadcast_in_dim.28), calls=%async_computation.1 | async-start | bytes 1048576 | tf_op jit(solution)/shard_map/all_to_all | solution.py:35
  34.3 1.5 bitcast_select_fusion
  35.9 4.4 %all-to-all-done.1 = bf16[4,8,2,8,512]{4,3,1,2,0:T(8,128)(2,1)S(1)} async-done(((bf16[4,8,2,8,512]{4,3,1,2,0:T(8,128)(2,1)}), bf16[4,8,2,8,512]{4,3,1,2,0:T(8,128)(2,1)S(1)}, u32[]{:S(2)}, u32[]{:S(2)}) %all-to-all-start.1) | async-done | bytes 524320 | tf_op jit(solution)/shard_map/all_to_all | solution.py:35
  40.4 1.9 collective-permute-start
  42.3 1.7 broadcast_select_fusion
  44.0 1.5 bitcast_select_fusion.1
  45.5 1.0 shard_map.111
  46.6 22.7 %all_to_all.35.block_ref = s16[4,352,512]{2,1,0:T(8,128)(2,1)S(1)} all-to-all(s16[4,352,512]{2,1,0:T(8,128)(2,1)S(1)} %shard_map.111), channel_id=1, replica_groups=mesh['zhi'=4,'y'=4,'zlo'=8,'x'=4,'core'=2] {'y'}, dimensions={0} | all-to-all | bytes 2883584 | tf_op jit(solution)/shard_map/all_to_all | solution.py:178
  69.3 0.5 shard_map.112
  69.7 15.2 %collective-permute-start.3 = (s16[352,256]{1,0:T(8,128)(2,1)S(1)}, s16[352,256]{1,0:T(8,128)(2,1)S(1)}, u32[]{:S(2)}, u32[]{:S(2)}) collective-permute-start(s16[352,256]{1,0:T(8,128)(2,1)S(1)} %get-tuple-element.17), channel_id=1, source_target_pairs={{0,256},{1,769},{256,0},{257,513},{512,768},{513,257},{768,512},{7... | collective-permute-start | bytes 540680 | tf_op jit(solution)/shard_map/ppermute | solution.py:42
  84.9 1.9 collective-permute-start.1
  86.8 31.1 %collective-permute-done.3.block_ref = s16[352,256]{1,0:T(8,128)(2,1)S(1)} collective-permute-done((s16[352,256]{1,0:T(8,128)(2,1)S(1)}, s16[352,256]{1,0:T(8,128)(2,1)S(1)}, u32[]{:S(2)}, u32[]{:S(2)}) %collective-permute-start.3) | collective-permute-done | bytes 180256 | tf_op jit(solution)/shard_map/ppermute | solution.py:42
  118.1 17.8 %collective-permute-start.4 = (s16[352,256]{1,0:T(8,128)(2,1)S(1)}, s16[352,256]{1,0:T(8,128)(2,1)S(1)}, u32[]{:S(2)}, u32[]{:S(2)}) collective-permute-start(s16[352,256]{1,0:T(8,128)(2,1)S(1)} %get-tuple-element.19), channel_id=1, source_target_pairs={{0,768},{1,257},{256,512},{257,1},{512,256},{513,769},{768,0},{769... | collective-permute-start | bytes 540680 | tf_op jit(solution)/shard_map/ppermute | solution.py:42
  136.0 1.9 collective-permute-start.2
  137.9 15.3 %collective-permute-done.4.block_ref = s16[352,256]{1,0:T(8,128)(2,1)S(1)} collective-permute-done((s16[352,256]{1,0:T(8,128)(2,1)S(1)}, s16[352,256]{1,0:T(8,128)(2,1)S(1)}, u32[]{:S(2)}, u32[]{:S(2)}) %collective-permute-start.4) | collective-permute-done | bytes 180256 | tf_op jit(solution)/shard_map/ppermute | solution.py:42
  153.2 1.0 shard_map.116
  154.2 3.5 %all-to-all-start.4 = ((bf16[4,336,256]{2,1,0:T(8,128)(2,1)}), bf16[4,336,256]{2,1,0:T(8,128)(2,1)S(1)}, u32[]{:S(2)}, u32[]{:S(2)}) async-start(bf16[4,336,256]{2,1,0:T(8,128)(2,1)} %shard_map.116), calls=%async_computation.4 | async-start | bytes 1376256 | tf_op jit(solution)/shard_map/all_to_all | solution.py:192
  157.7 1.0 shard_map.114
  158.7 9.6 %all-to-all-done.4 = bf16[4,336,256]{2,1,0:T(8,128)(2,1)S(1)} async-done(((bf16[4,336,256]{2,1,0:T(8,128)(2,1)}), bf16[4,336,256]{2,1,0:T(8,128)(2,1)S(1)}, u32[]{:S(2)}, u32[]{:S(2)}) %all-to-all-start.4) | async-done | bytes 688160 | tf_op jit(solution)/shard_map/all_to_all | solution.py:192
  168.2 3.5 %all-to-all-start.3 = ((bf16[4,336,256]{2,1,0:T(8,128)(2,1)}), bf16[4,336,256]{2,1,0:T(8,128)(2,1)S(1)}, u32[]{:S(2)}, u32[]{:S(2)}) async-start(bf16[4,336,256]{2,1,0:T(8,128)(2,1)} %shard_map.114), calls=%async_computation.3 | async-start | bytes 1376256 | tf_op jit(solution)/shard_map/all_to_all | solution.py:190
  171.7 0.7 fusion.51
  172.5 0.3 fusion.55
  172.8 1.1 convolution_add_fusion.3
  173.9 1.9 collective-permute-start.5
  175.9 0.7 fusion.53
  176.6 4.5 %all-to-all-done.3 = bf16[4,336,256]{2,1,0:T(8,128)(2,1)S(1)} async-done(((bf16[4,336,256]{2,1,0:T(8,128)(2,1)}), bf16[4,336,256]{2,1,0:T(8,128)(2,1)S(1)}, u32[]{:S(2)}, u32[]{:S(2)}) %all-to-all-start.3) | async-done | bytes 688160 | tf_op jit(solution)/shard_map/all_to_all | solution.py:190
  181.1 0.7 fusion.52
  181.8 0.3 fusion.54
  182.1 1.1 fusion.6
  183.3 4.7 %all-to-all-start.5 = ((f32[4,64,512]{2,1,0:T(8,128)}), f32[4,64,512]{2,1,0:T(8,128)S(1)}, u32[]{:S(2)}, u32[]{:S(2)}) async-start(f32[4,64,512]{2,1,0:T(8,128)} %bitcast.24), calls=%async_computation.5 | async-start | bytes 1048576 | tf_op jit(solution)/shard_map/all_to_all | solution.py:204
  188.3 0.7 copy-done.6
  188.9 0.3 fusion.57
  189.2 4.8 %all-to-all-done.5 = f32[4,64,512]{2,1,0:T(8,128)S(1)} async-done(((f32[4,64,512]{2,1,0:T(8,128)}), f32[4,64,512]{2,1,0:T(8,128)S(1)}, u32[]{:S(2)}, u32[]{:S(2)}) %all-to-all-start.5) | async-done | bytes 524320 | tf_op jit(solution)/shard_map/all_to_all | solution.py:204
  194.0 0.7 reduce_sum.18
  194.7 3.4 %all-to-all-start.6 = ((f32[8,8,512]{2,1,0:T(8,128)}), f32[8,8,512]{2,1,0:T(8,128)S(1)}, u32[]{:S(2)}, u32[]{:S(2)}) async-start(f32[8,8,512]{2,1,0:T(8,128)} %bitcast.25), calls=%async_computation.6 | async-start | bytes 262144 | tf_op jit(solution)/shard_map/all_to_all | solution.py:205
  198.1 1.4 fusion.56
  199.5 2.0 fusion.5
  201.5 1.1 fusion.4
  202.6 1.1 fusion.3
  203.6 5.8 %all-to-all-done.6 = f32[8,8,512]{2,1,0:T(8,128)S(1)} async-done(((f32[8,8,512]{2,1,0:T(8,128)}), f32[8,8,512]{2,1,0:T(8,128)S(1)}, u32[]{:S(2)}, u32[]{:S(2)}) %all-to-all-start.6) | async-done | bytes 131104 | tf_op jit(solution)/shard_map/all_to_all | solution.py:205
  209.4 0.6 reduce_sum.19
  (54 shorter events, 1.5 us)
Async XLA Ops:
  0.6 16.5 %copy-start = (s32[128,448]{0,1:T(8,128)S(1)}, s32[128,448]{0,1:T(8,128)}, u32[]{:S(2)}) copy-start(s32[128,448]{0,1:T(8,128)} %param.13) | copy-start | bytes 688132
  0.6 16.2 %copy-start.1 = (s32[128,448]{0,1:T(8,128)S(1)}, s32[128,448]{0,1:T(8,128)}, u32[]{:S(2)}) copy-start(s32[128,448]{0,1:T(8,128)} %param.14) | copy-start | bytes 688132
  2.1 24.5 %all-to-all-start = ((bf16[8,2,8,512]{3,2,1,0:T(8,128)(2,1)}), bf16[8,2,8,512]{3,2,1,0:T(8,128)(2,1)S(1)}, u32[]{:S(2)}, u32[]{:S(2)}) async-start(bf16[8,2,8,512]{3,2,1,0:T(8,128)(2,1)} %broadcast_in_dim.27), calls=%async_computation | async-start | bytes 262144 | tf_op jit(solution)/shard_map/all_to_all | solution.py:35
  15.8 1.7 copy-start.2
  17.7 16.7 %copy-start.12 = (bf16[512,448]{0,1:T(8,128)(2,1)S(1)}, bf16[512,448]{0,1:T(8,128)(2,1)}, u32[]{:S(2)}) copy-start(bf16[512,448]{0,1:T(8,128)(2,1)} %param.11) | copy-start | bytes 1376260
  27.5 12.9 %all-to-all-start.1 = ((bf16[4,8,2,8,512]{4,3,1,2,0:T(8,128)(2,1)}), bf16[4,8,2,8,512]{4,3,1,2,0:T(8,128)(2,1)S(1)}, u32[]{:S(2)}, u32[]{:S(2)}) async-start(bf16[4,8,2,8,512]{4,3,1,2,0:T(8,128)(2,1)} %broadcast_in_dim.28), calls=%async_computation.1 | async-start | bytes 1048576 | tf_op jit(solution)/shard_map/all_to_all | solution.py:35
  34.3 8.0 %copy-start.13 = (bf16[448,512]{1,0:T(8,128)(2,1)S(1)}, bf16[448,512]{1,0:T(8,128)(2,1)}, u32[]{:S(2)}) copy-start(bf16[448,512]{1,0:T(8,128)(2,1)} %param.12) | copy-start | bytes 1376260
  40.4 5.2 %collective-permute-start = (bf16[2,256,512]{2,1,0:T(8,128)(2,1)S(1)}, bf16[2,256,512]{2,1,0:T(8,128)(2,1)S(1)}, u32[]{:S(2)}, u32[]{:S(2)}) collective-permute-start(bf16[2,256,512]{2,1,0:T(8,128)(2,1)S(1)} %bitcast.68), channel_id=1, source_target_pairs={{0,1},{1,0},{2,3},{3,2},{4,5},{5,4},{6,7},{7,6},{8,9},{9,8},{10,11... | collective-permute-start | bytes 1572872 | tf_op jit(solution)/shard_map/ppermute | solution.py:169
  42.3 1.7 copy-start.14
  69.7 48.3 %collective-permute-start.3 = (s16[352,256]{1,0:T(8,128)(2,1)S(1)}, s16[352,256]{1,0:T(8,128)(2,1)S(1)}, u32[]{:S(2)}, u32[]{:S(2)}) collective-permute-start(s16[352,256]{1,0:T(8,128)(2,1)S(1)} %get-tuple-element.17), channel_id=1, source_target_pairs={{0,256},{1,769},{256,0},{257,513},{512,768},{513,257},{768,512},{7... | collective-permute-start | bytes 540680 | tf_op jit(solution)/shard_map/ppermute | solution.py:42
  84.9 50.9 %collective-permute-start.1 = (s16[352,256]{1,0:T(8,128)(2,1)S(1)}, s16[352,256]{1,0:T(8,128)(2,1)S(1)}, u32[]{:S(2)}, u32[]{:S(2)}) collective-permute-start(s16[352,256]{1,0:T(8,128)(2,1)S(1)} %get-tuple-element.13), channel_id=1, source_target_pairs={{0,256},{1,769},{256,0},{257,513},{512,768},{513,257},{768,512},{7... | collective-permute-start | bytes 540680 | tf_op jit(solution)/shard_map/ppermute | solution.py:42
  118.1 35.1 %collective-permute-start.4 = (s16[352,256]{1,0:T(8,128)(2,1)S(1)}, s16[352,256]{1,0:T(8,128)(2,1)S(1)}, u32[]{:S(2)}, u32[]{:S(2)}) collective-permute-start(s16[352,256]{1,0:T(8,128)(2,1)S(1)} %get-tuple-element.19), channel_id=1, source_target_pairs={{0,768},{1,257},{256,512},{257,1},{512,256},{513,769},{768,0},{769... | collective-permute-start | bytes 540680 | tf_op jit(solution)/shard_map/ppermute | solution.py:42
  136.0 21.7 %collective-permute-start.2 = (s16[352,256]{1,0:T(8,128)(2,1)S(1)}, s16[352,256]{1,0:T(8,128)(2,1)S(1)}, u32[]{:S(2)}, u32[]{:S(2)}) collective-permute-start(s16[352,256]{1,0:T(8,128)(2,1)S(1)} %get-tuple-element.15), channel_id=1, source_target_pairs={{0,768},{1,257},{256,512},{257,1},{512,256},{513,769},{768,0},{769... | collective-permute-start | bytes 540680 | tf_op jit(solution)/shard_map/ppermute | solution.py:42
  154.2 14.0 %all-to-all-start.4 = ((bf16[4,336,256]{2,1,0:T(8,128)(2,1)}), bf16[4,336,256]{2,1,0:T(8,128)(2,1)S(1)}, u32[]{:S(2)}, u32[]{:S(2)}) async-start(bf16[4,336,256]{2,1,0:T(8,128)(2,1)} %shard_map.116), calls=%async_computation.4 | async-start | bytes 1376256 | tf_op jit(solution)/shard_map/all_to_all | solution.py:192
  168.2 12.8 %all-to-all-start.3 = ((bf16[4,336,256]{2,1,0:T(8,128)(2,1)}), bf16[4,336,256]{2,1,0:T(8,128)(2,1)S(1)}, u32[]{:S(2)}, u32[]{:S(2)}) async-start(bf16[4,336,256]{2,1,0:T(8,128)(2,1)} %shard_map.114), calls=%async_computation.3 | async-start | bytes 1376256 | tf_op jit(solution)/shard_map/all_to_all | solution.py:190
  172.5 1.5 copy-start.3
  172.5 1.5 copy-start.7
  173.9 8.2 %collective-permute-start.5 = (f32[256,512]{1,0:T(8,128)}, f32[256,512]{1,0:T(8,128)S(1)}, u32[]{:S(2)}, u32[]{:S(2)}) collective-permute-start(f32[256,512]{1,0:T(8,128)} %convolution_add_fusion.3), channel_id=1, source_target_pairs={{0,1},{1,0},{2,3},{3,2},{4,5},{5,4},{6,7},{7,6},{8,9},{9,8},{10,11... | collective-permute-start | bytes 1572872 | tf_op jit(solution)/shard_map/ppermute | solution.py:203
  181.8 1.5 copy-start.5
  183.3 10.8 %all-to-all-start.5 = ((f32[4,64,512]{2,1,0:T(8,128)}), f32[4,64,512]{2,1,0:T(8,128)S(1)}, u32[]{:S(2)}, u32[]{:S(2)}) async-start(f32[4,64,512]{2,1,0:T(8,128)} %bitcast.24), calls=%async_computation.5 | async-start | bytes 1048576 | tf_op jit(solution)/shard_map/all_to_all | solution.py:204
  188.0 0.9 copy-start.6
  189.2 10.3 %copy-start.8 = (bf16[1,4,112,256]{3,2,0,1:T(8,128)(2,1)S(1)}, bf16[1,4,112,256]{3,2,0,1:T(8,128)(2,1)}, u32[]{:S(2)}) copy-start(bf16[1,4,112,256]{3,2,0,1:T(8,128)(2,1)} %copy-done.7) | copy-start | bytes 688132
  194.7 14.7 %all-to-all-start.6 = ((f32[8,8,512]{2,1,0:T(8,128)}), f32[8,8,512]{2,1,0:T(8,128)S(1)}, u32[]{:S(2)}, u32[]{:S(2)}) async-start(f32[8,8,512]{2,1,0:T(8,128)} %bitcast.25), calls=%async_computation.6 | async-start | bytes 262144 | tf_op jit(solution)/shard_map/all_to_all | solution.py:205
  198.1 3.4 %copy-start.4 = (bf16[1,4,112,256]{3,2,0,1:T(8,128)(2,1)S(1)}, bf16[1,4,112,256]{3,2,0,1:T(8,128)(2,1)}, u32[]{:S(2)}) copy-start(bf16[1,4,112,256]{3,2,0,1:T(8,128)(2,1)} %copy-done.3) | copy-start | bytes 688132
  198.1 3.4 %copy-start.11 = (pred[448,512]{1,0:T(32,128)(4,1)S(1)}, pred[448,512]{1,0:T(32,128)(4,1)}, u32[]{:S(2)}) copy-start(pred[448,512]{1,0:T(32,128)(4,1)} %get-tuple-element.56) | copy-start | bytes 688132
  201.5 1.1 copy-start.9
  201.5 1.1 copy-start.10

commit v5 on v4

v5 whole, which is shorter than its diff:
```python
import jax
import jax.numpy as jnp
import numpy as np
from jax import lax
from jax.experimental import pallas as pl
from jax.experimental.pallas import tpu as pltpu
from jax.sharding import Mesh, PartitionSpec as P

bf16 = jnp.bfloat16
f32 = jnp.float32
keep_sets = ((0, 1, 2), (0, 3, 4), (1, 3, 5), (2, 4, 5))


def keep_planes(pattern):
    planes = []
    for members in keep_sets:
        kept = pattern == members[0]
        for member in members[1:]:
            kept = kept | (pattern == member)
        planes.append(kept.astype(bf16))
    return planes


def spread_matrix(groups):
    row = lax.broadcasted_iota(jnp.int32, (4 * groups, 4 * groups), 0)
    col = lax.broadcasted_iota(jnp.int32, (4 * groups, 4 * groups), 1)
    return ((row % groups) * 4 + row // groups == col).astype(bf16)


def dot(a, b, dims):
    return lax.dot_general(a, b, (dims, ((), ())), preferred_element_type=f32)


def zhi_exchange(block, flip0, flip1):
    pairs = [
        (z * 2 + c, (z ^ (flip0, flip1)[c]) * 2 + c) for z in range(4) for c in range(2)
    ]
    return lax.ppermute(block, ("zhi", "core"), pairs)


EXTRA = 16
COST = 2 * 10**9


def pack(values):
    rows, powers = [], []
    for value in values:
        most = jnp.max(jnp.abs(value), axis=0, keepdims=True)
        power = jnp.ceil(jnp.log2(jnp.maximum(most, 1e-30))) - 14.0
        rows.append(to_int16(jnp.round(value * jnp.exp2(-power))))
        powers.append(power)
    spot = lax.broadcasted_iota(jnp.int32, (EXTRA, values[0].shape[1]), 0)
    tail = jnp.where(spot == 0, powers[0], jnp.where(spot == 1, powers[1], powers[2]))
    return rows, to_int16(tail)


def to_int16(values):
    return values.astype(jnp.int32).astype(jnp.int16)


def wide(block):
    return block.astype(jnp.int32).astype(f32)


def unpack(block, units):
    powers = wide(block[3 * units : 3 * units + EXTRA, :])
    return [
        wide(block[i * units : (i + 1) * units, :]) * jnp.exp2(powers[i : i + 1, :])
        for i in range(3)
    ]


def spread_kernel(*refs):
    out_ref = refs[-1]
    for c in range(out_ref.shape[0]):
        if len(refs) == 2:
            out_ref[c] = refs[0][...]
        else:
            for i, ref in enumerate(refs[:-1]):
                out_ref[c, i] = ref[...]


def partial_kernel(flag_ref, gate_ref, up_ref, down_ref, own_ref, other_ref, out_ref):
    ny, units = out_ref.shape[0], gate_ref.shape[0] // out_ref.shape[0]
    is_own = flag_ref[0] == 1
    tokens = jnp.where(is_own, own_ref[0], other_ref[0])
    grad_out = jnp.where(is_own, own_ref[1], other_ref[1])
    products = [
        dot(gate_ref[...], tokens, ((1,), (1,))),
        dot(up_ref[...], tokens, ((1,), (1,))),
        dot(down_ref[...], grad_out, ((1,), (1,))),
    ]
    for c in range(ny):
        store([p[c * units : (c + 1) * units] for p in products], out_ref.at[c])


def store(values, send_ref):
    units = values[0].shape[0]
    rows, tail = pack(values)
    for i in range(3):
        send_ref[i * units : (i + 1) * units, :] = rows[i]
    send_ref[3 * units :, :] = tail


def sum_over_blocks(block_ref):
    units = (block_ref.shape[1] - EXTRA) // 3
    total = [0.0, 0.0, 0.0]
    for c in range(block_ref.shape[0]):
        parts = unpack(block_ref.at[c], units)
        total = [total[i] + parts[i] for i in range(3)]
    return total


def sent_sum_kernel(block_ref, send_ref):
    store(sum_over_blocks(block_ref), send_ref)


def kept_sum_kernel(block_ref, got_ref, total_ref, send_ref):
    total = sum_over_blocks(block_ref)
    parts = unpack(got_ref, total_ref.shape[1])
    total = [total[i] + parts[i] for i in range(3)]
    for i in range(3):
        total_ref[i] = total[i]
    store(total, send_ref)


def swiglu_kernel(total_ref, got_ref, out_ref, spread_ref):
    units = total_ref.shape[1]
    parts = unpack(got_ref, units)
    gate_pre, up_pre, hidden_grad = [total_ref[i] + parts[i] for i in range(3)]
    sigmoid_gate = jax.nn.sigmoid(gate_pre)
    silu_gate = gate_pre * sigmoid_gate
    results = (
        silu_gate * up_pre,
        hidden_grad * up_pre * sigmoid_gate * (1.0 + gate_pre * (1.0 - sigmoid_gate)),
        hidden_grad * silu_gate,
    )
    for i, result in enumerate(results):
        result = result.astype(bf16)
        out_ref[i * units : (i + 1) * units, :] = result
        for c in range(spread_ref.shape[0]):
            spread_ref[c, i * units : (i + 1) * units, :] = result


def call(kernel, outs, *args, scalars=0):
    places = [pltpu.SMEM] * scalars + [pltpu.VMEM] * (len(args) - scalars)
    return pl.pallas_call(
        kernel,
        in_specs=[pl.BlockSpec(memory_space=place) for place in places],
        out_shape=[jax.ShapeDtypeStruct(shape, kind) for shape, kind in outs],
        compiler_params=pltpu.CompilerParams(vmem_limit_bytes=32 * 2**20),
        cost_estimate=pl.CostEstimate(flops=COST, bytes_accessed=1024, transcendentals=0),
    )(*args)


def body(inputs, cotangent, gate_weight, up_weight, down_weight, gate_pattern, up_pattern, down_pattern):
    sizes = {"zhi": 4, "y": 4, "zlo": 8, "x": 4, "core": 2}
    rows, width = inputs.shape
    hidden_units = down_weight.shape[0]
    half = rows * sizes["zlo"] * sizes["x"]
    ny = sizes["y"]
    quarter = hidden_units // ny
    spread_width = spread_matrix(width // 4)
    spread_units = spread_matrix(hidden_units // 4)
    gate_keep = dot(jnp.concatenate(keep_planes(gate_pattern.T), axis=1), spread_width, ((1,), (0,))) > 0.5
    up_keep = dot(jnp.concatenate(keep_planes(up_pattern.T), axis=1), spread_width, ((1,), (0,))) > 0.5
    down_keep = dot(spread_units, jnp.concatenate(keep_planes(down_pattern), axis=0), ((0,), (0,))) > 0.5
    zero = jnp.zeros((), bf16)
    gate_eff = jnp.where(gate_keep, gate_weight.T, zero)
    up_eff = jnp.where(up_keep, up_weight.T, zero)
    down_eff = jnp.where(down_keep, down_weight, zero)

    swap = [(0, 1), (1, 0)]
    nx, nzlo = sizes["x"], sizes["zlo"]
    (both,) = call(spread_kernel, [((nzlo, 2, rows, width), bf16)], inputs, cotangent)
    both = lax.all_to_all(both, "zlo", 0, 0)
    both, gate_eff, up_eff, down_eff = lax.optimization_barrier(
        (both, gate_eff, up_eff, down_eff)
    )
    (both,) = call(spread_kernel, [((nx, nzlo, 2, rows, width), bf16)], both)
    both = lax.all_to_all(both, "x", 0, 0)
    own = both.transpose(2, 0, 1, 3, 4).reshape(2, half, width)
    other = lax.ppermute(own, "core", swap)

    zhi, core = lax.axis_index("zhi"), lax.axis_index("core")
    keep = jnp.where(core == 0, (zhi ^ (zhi >> 1)) & 1, zhi >> 1)
    own_kept = keep == core
    flag = own_kept.astype(jnp.int32).reshape(1)

    i16 = jnp.int16
    packed = 3 * quarter + EXTRA
    block = [((ny, packed, half), i16)]
    operands = (gate_eff, up_eff, down_eff, own, other)
    (sent,) = call(partial_kernel, block, 1 - flag, *operands, scalars=1)
    (kept,) = call(partial_kernel, block, flag, *operands, scalars=1)
    sent = lax.all_to_all(sent, "y", 0, 0)
    (send,) = call(sent_sum_kernel, [((packed, half), i16)], sent)
    got = zhi_exchange(send, 1, 3)
    kept = lax.all_to_all(kept, "y", 0, 0)
    total, send = call(
        kept_sum_kernel, [((3, quarter, half), f32), ((packed, half), i16)], kept, got
    )
    got = zhi_exchange(send, 3, 1)
    spread = ((ny, 3 * quarter, half), bf16)
    mine, to_y = call(swiglu_kernel, [((3 * quarter, half), bf16), spread], total, got)
    theirs = zhi_exchange(mine, 1, 3)
    first = lax.all_to_all(to_y, "y", 0, 0)
    (to_y,) = call(spread_kernel, [spread], theirs)
    second = lax.all_to_all(to_y, "y", 0, 0)

    def units(block):
        block = block.reshape(ny, 3, quarter, half)
        return block.transpose(1, 0, 2, 3).reshape(3, hidden_units, half)

    first, second = units(first), units(second)

    def back_of(side):
        return dot(side[1], gate_eff, ((0,), (0,))) + dot(side[2], up_eff, ((0,), (0,)))

    back_first, back_second = back_of(first), back_of(second)
    stays = jnp.where(own_kept, back_first, back_second)
    leaves = jnp.where(own_kept, back_second, back_first)
    back = stays + lax.ppermute(leaves, "core", swap)
    back = lax.all_to_all(back.reshape(nx, half // nx, width), "x", 0, 0).sum(axis=0)
    back = lax.all_to_all(back.reshape(nzlo, rows, width), "zlo", 0, 0).sum(axis=0)

    kept_side = jnp.where(own_kept, own, other)
    sent_side = jnp.where(own_kept, other, own)

    def weight_grad(member, side):
        return dot(first[member], kept_side[side], ((1,), (0,))) + dot(
            second[member], sent_side[side], ((1,), (0,))
        )

    grad_gate = jnp.where(gate_keep, weight_grad(1, 0), 0.0).astype(bf16)
    grad_up = jnp.where(up_keep, weight_grad(2, 0), 0.0).astype(bf16)
    grad_down = jnp.where(down_keep, weight_grad(0, 1), 0.0).astype(bf16)
    return (back.astype(bf16), grad_gate.T, grad_up.T, grad_down)


def solution(mesh):
    fine = Mesh(
        np.asarray(mesh.devices).reshape(4, 4, 8, 4, 2), ("zhi", "y", "zlo", "x", "core")
    )
    row, col = ("zhi", "y"), ("zlo", "x", "core")
    return jax.shard_map(
        body,
        mesh=fine,
        in_specs=(
            P(col, row),
            P(col, row),
            P(row, col),
            P(row, col),
            P(col, row),
            P(row, col),
            P(row, col),
            P(col, row),
        ),
        out_specs=(P(col, row), P(row, col), P(row, col), P(col, row)),
        check_vma=False,
    )
```

time: 212 us -> 210 us (level)
  waiting for transfers between devices: 84.2 us -> 97 us
  blocking collectives: 22.7 us -> 11.8 us
  starting transfers between devices: 75.1 us -> 66.3 us
  local copies, waits for them, and re-layouts: 4.53 us -> 11.4 us
  matrix products: 13.7 us -> 10.1 us
  Pallas kernels: 3.67 us -> 5.95 us
    ppermute x4 -> x3, starting transfers between devices: 36.8 us -> 22.1 us  [zhi_exchange(): return lax.ppermute(block, ('zhi', 'core'), pairs)]
    ppermute x4 -> x3, waiting for transfers between devices: 46.4 us -> 59 us  [zhi_exchange(): return lax.ppermute(block, ('zhi', 'core'), pairs)]
    all_to_all x1, blocking collectives: 22.7 us -> 11.8 us  [body(): both = lax.all_to_all(both, 'x', 0, 0)]
    unnamed x30 -> x50, local copies, waits for them, and re-layouts: 0.74 us -> 8.75 us
    all_to_all x6 -> x7, starting transfers between devices: 34.5 us -> 40.3 us  [the longest x1 12.7 us: body(): both = lax.all_to_all(both, 'zlo', 0, 0)]
    dot_general x13, matrix products: 13.7 us -> 10.1 us  [dot(): return lax.dot_general(a, b, (dims, ((), ())), preferred_element_type=f32)]
    all_to_all x6 -> x7, waiting for transfers between devices: 37.8 us -> 35.2 us  [the longest x1 10.6 us: body(): sent = lax.all_to_all(sent, 'y', 0, 0)]
    pallas_call x6 -> x8, Pallas kernels: 3.67 us -> 5.95 us  [call(): pl.pallas_call(kernel, in_specs=[pl.BlockSpec(memory_space=place) for pla...]
  transfers between devices with their start and end apart: 12 -> 12, of which waited for: 8 -> 10; matrix products, arithmetic and copies ran while one was open for 9% -> 6% of each run, Pallas kernels for 1% -> 1%
where the time goes in v5:
time: 210 us; the launch traced here: 208 us
  waiting for transfers between devices  97 us (46%)
  starting transfers between devices  66.3 us (32%)
  blocking collectives  11.8 us (6%)
  local copies, waits for them, and re-layouts  11.4 us (5%)
  matrix products  10.1 us (5%)
  Pallas kernels  5.95 us (3%)
  other arithmetic  4.32 us (2%)
    ppermute x3, waiting for transfers between devices, zhi_exchange(): return lax.ppermute(block, ('zhi', 'core'), pairs)  59 us
    ppermute x3, starting transfers between devices, zhi_exchange(): return lax.ppermute(block, ('zhi', 'core'), pairs)  22.1 us
    all_to_all x1, starting transfers between devices, body(): both = lax.all_to_all(both, 'zlo', 0, 0)  12.7 us
    all_to_all x1, blocking collectives, body(): both = lax.all_to_all(both, 'x', 0, 0)  11.8 us
    all_to_all x1, waiting for transfers between devices, body(): sent = lax.all_to_all(sent, 'y', 0, 0)  10.6 us
    dot_general x13, matrix products, dot(): return lax.dot_general(a, b, (dims, ((), ())), preferred_element_type=f32)  10.1 us
    unnamed x50, local copies, waits for them, and re-layouts  8.75 us
    all_to_all x1, waiting for transfers between devices, body(): second = lax.all_to_all(to_y, 'y', 0, 0)  7.23 us
  transfers between devices with their start and end apart: 12, of which 10 were waited for; matrix products, arithmetic and copies ran while one was open for 6% of the time, Pallas kernels for 1%

profile of v5, /device:TPU:6, one launch (start us, length us, event | category | flops | bytes accessed | tf_op | source)
XLA Modules:
  0.0 207.8 jit_solution(15388883328258489931)
XLA Ops:
  0.6 0.7 copy-done.3
  1.3 0.7 copy-done.4
  2.7 12.7 %all-to-all-start = ((bf16[8,2,8,512]{3,2,1,0:T(8,128)(2,1)}), bf16[8,2,8,512]{3,2,1,0:T(8,128)(2,1)S(1)}, u32[]{:S(2)}, u32[]{:S(2)}) async-start(bf16[8,2,8,512]{3,2,1,0:T(8,128)(2,1)} %shard_map.111), calls=%async_computation | async-start | bytes 262144 | tf_op jit(solution)/shard_map/all_to_all | solution.py:176
  15.7 0.8 copy-done.7
  16.7 0.8 copy-done.8
  18.3 0.8 copy-done.22
  19.1 1.7 broadcast_select_fusion.3
  20.8 1.5 bitcast_select_fusion
  22.3 1.5 bitcast_select_fusion.1
  23.8 3.4 %all-to-all-done.refs_0_ = bf16[8,2,8,512]{3,2,1,0:T(8,128)(2,1)S(1)} async-done(((bf16[8,2,8,512]{3,2,1,0:T(8,128)(2,1)}), bf16[8,2,8,512]{3,2,1,0:T(8,128)(2,1)S(1)}, u32[]{:S(2)}, u32[]{:S(2)}) %all-to-all-start) | async-done | bytes 131104 | tf_op jit(solution)/shard_map/all_to_all | solution.py:176
  27.3 11.8 %all_to_all.40 = bf16[4,8,2,8,512]{4,3,2,1,0:T(8,128)(2,1)S(1)} all-to-all(bf16[4,8,2,8,512]{4,3,2,1,0:T(8,128)(2,1)S(1)} %shard_map.112), channel_id=1, replica_groups=mesh['zhi'=4,'y'=4,'zlo'=8,'x'=4,'core'=2] {'x'}, dimensions={0} | all-to-all | bytes 1048576 | tf_op jit(solution)/shard_map/all_to_all | solution.py:181
  39.2 1.9 collective-permute-start
  41.1 1.9 collective-permute-done.other_ref
  43.0 1.5 shard_map.114
  44.5 3.5 %all-to-all-start.3 = ((s16[4,352,256]{2,1,0:T(8,128)(2,1)}), s16[4,352,256]{2,1,0:T(8,128)(2,1)S(1)}, u32[]{:S(2)}, u32[]{:S(2)}) async-start(s16[4,352,256]{2,1,0:T(8,128)(2,1)} %shard_map.114), calls=%async_computation.3 | async-start | bytes 1441792 | tf_op jit(solution)/shard_map/all_to_all | solution.py:196
  48.0 0.7 shard_map.113
  48.7 0.9 copy-done
  49.6 10.6 %all-to-all-done.3.block_ref = s16[4,352,256]{2,1,0:T(8,128)(2,1)S(1)} async-done(((s16[4,352,256]{2,1,0:T(8,128)(2,1)}), s16[4,352,256]{2,1,0:T(8,128)(2,1)S(1)}, u32[]{:S(2)}, u32[]{:S(2)}) %all-to-all-start.3) | async-done | bytes 720928 | tf_op jit(solution)/shard_map/all_to_all | solution.py:196
  60.1 3.5 %all-to-all-start.2 = ((s16[4,352,256]{2,1,0:T(8,128)(2,1)}), s16[4,352,256]{2,1,0:T(8,128)(2,1)S(1)}, u32[]{:S(2)}, u32[]{:S(2)}) async-start(s16[4,352,256]{2,1,0:T(8,128)(2,1)} %copy-done), calls=%async_computation.2 | async-start | bytes 1441792 | tf_op jit(solution)/shard_map/all_to_all | solution.py:199
  63.6 0.9 shard_map.115
  64.5 15.2 %collective-permute-start.1 = (s16[352,256]{1,0:T(8,128)(2,1)}, s16[352,256]{1,0:T(8,128)(2,1)S(1)}, u32[]{:S(2)}, u32[]{:S(2)}) collective-permute-start(s16[352,256]{1,0:T(8,128)(2,1)} %shard_map.115), channel_id=1, source_target_pairs={{0,256},{1,769},{256,0},{257,513},{512,768},{513,257},{768,512},{7... | collective-permute-start | bytes 540680 | tf_op jit(solution)/shard_map/ppermute | solution.py:38
  79.8 17.3 %collective-permute-done.1.got_ref = s16[352,256]{1,0:T(8,128)(2,1)S(1)} collective-permute-done((s16[352,256]{1,0:T(8,128)(2,1)}, s16[352,256]{1,0:T(8,128)(2,1)S(1)}, u32[]{:S(2)}, u32[]{:S(2)}) %collective-permute-start.1) | collective-permute-done | bytes 180256 | tf_op jit(solution)/shard_map/ppermute | solution.py:38
  97.1 0.7 copy-done.1
  97.8 0.9 copy-done.2
  99.0 4.8 %collective-permute-start.2 = (s16[352,256]{1,0:T(8,128)(2,1)S(1)}, s16[352,256]{1,0:T(8,128)(2,1)S(1)}, u32[]{:S(2)}, u32[]{:S(2)}) collective-permute-start(s16[352,256]{1,0:T(8,128)(2,1)S(1)} %get-tuple-element.17), channel_id=1, source_target_pairs={{0,768},{1,257},{256,512},{257,1},{512,256},{513,769},{768,0},{769... | collective-permute-start | bytes 540680 | tf_op jit(solution)/shard_map/ppermute | solution.py:38
  103.8 22.5 %collective-permute-done.2.got_ref = s16[352,256]{1,0:T(8,128)(2,1)S(1)} collective-permute-done((s16[352,256]{1,0:T(8,128)(2,1)S(1)}, s16[352,256]{1,0:T(8,128)(2,1)S(1)}, u32[]{:S(2)}, u32[]{:S(2)}) %collective-permute-start.2) | collective-permute-done | bytes 180256 | tf_op jit(solution)/shard_map/ppermute | solution.py:38
  126.3 1.0 shard_map.117
  127.3 4.6 %all-to-all-start.4 = ((bf16[4,336,256]{2,1,0:T(8,128)(2,1)}), bf16[4,336,256]{2,1,0:T(8,128)(2,1)S(1)}, u32[]{:S(2)}, u32[]{:S(2)}) async-start(bf16[4,336,256]{2,1,0:T(8,128)(2,1)} %get-tuple-element.18), calls=%async_computation.4 | async-start | bytes 1376256 | tf_op jit(solution)/shard_map/all_to_all | solution.py:207
  131.9 2.1 collective-permute-start.3
  133.9 19.2 %collective-permute-done.3.refs_0_ = bf16[336,256]{1,0:T(8,128)(2,1)S(1)} collective-permute-done((bf16[336,256]{1,0:T(8,128)(2,1)S(1)}, bf16[336,256]{1,0:T(8,128)(2,1)S(1)}, u32[]{:S(2)}, u32[]{:S(2)}) %collective-permute-start.3) | collective-permute-done | bytes 172064 | tf_op jit(solution)/shard_map/ppermute | solution.py:38
  153.1 0.9 shard_map.118
  154.0 4.8 %all-to-all-start.5 = ((bf16[4,336,256]{2,1,0:T(8,128)(2,1)}), bf16[4,336,256]{2,1,0:T(8,128)(2,1)}, u32[]{:S(2)}, u32[]{:S(2)}) async-start(bf16[4,336,256]{2,1,0:T(8,128)(2,1)} %shard_map.118), calls=%async_computation.5 | async-start | bytes 1376256 | tf_op jit(solution)/shard_map/all_to_all | solution.py:209
  158.8 0.7 fusion.53
  160.7 7.2 %all-to-all-done.5 = bf16[4,336,256]{2,1,0:T(8,128)(2,1)} async-done(((bf16[4,336,256]{2,1,0:T(8,128)(2,1)}), bf16[4,336,256]{2,1,0:T(8,128)(2,1)}, u32[]{:S(2)}, u32[]{:S(2)}) %all-to-all-start.5) | async-done | bytes 688160 | tf_op jit(solution)/shard_map/all_to_all | solution.py:209
  167.9 1.9 fusion.54
  170.9 1.9 collective-permute-start.4
  172.8 0.9 broadcast_select_fusion.1
  173.7 1.0 collective-permute-done.4
  174.7 1.0 select_add_fusion
  175.7 5.6 %all-to-all-start.6 = ((f32[4,64,512]{2,1,0:T(8,128)}), f32[4,64,512]{2,1,0:T(8,128)S(1)}, u32[]{:S(2)}, u32[]{:S(2)}) async-start(f32[4,64,512]{2,1,0:T(8,128)} %bitcast.23), calls=%async_computation.6 | async-start | bytes 1048576 | tf_op jit(solution)/shard_map/all_to_all | solution.py:224
  182.5 6.8 %all-to-all-done.6 = f32[4,64,512]{2,1,0:T(8,128)S(1)} async-done(((f32[4,64,512]{2,1,0:T(8,128)}), f32[4,64,512]{2,1,0:T(8,128)S(1)}, u32[]{:S(2)}, u32[]{:S(2)}) %all-to-all-start.6) | async-done | bytes 524320 | tf_op jit(solution)/shard_map/all_to_all | solution.py:224
  189.3 0.7 reduce_sum.18
  190.0 5.7 %all-to-all-start.7 = ((f32[8,8,512]{2,1,0:T(8,128)}), f32[8,8,512]{2,1,0:T(8,128)S(1)}, u32[]{:S(2)}, u32[]{:S(2)}) async-start(f32[8,8,512]{2,1,0:T(8,128)} %bitcast.24), calls=%async_computation.7 | async-start | bytes 262144 | tf_op jit(solution)/shard_map/all_to_all | solution.py:225
  196.0 0.7 copy-done.5
  196.9 1.1 fusion.5
  197.9 1.1 fusion.4
  199.0 1.1 fusion.3
  200.1 7.1 %all-to-all-done.7 = f32[8,8,512]{2,1,0:T(8,128)S(1)} async-done(((f32[8,8,512]{2,1,0:T(8,128)}), f32[8,8,512]{2,1,0:T(8,128)S(1)}, u32[]{:S(2)}, u32[]{:S(2)}) %all-to-all-start.7) | async-done | bytes 131104 | tf_op jit(solution)/shard_map/all_to_all | solution.py:225
  (73 shorter events, 6.6 us)
Async XLA Ops:
  0.6 0.7 copy-start.3
  1.3 0.7 copy-start.4
  2.7 12.7 %copy-start.6 = (s32[128,448]{0,1:T(8,128)S(1)}, s32[128,448]{0,1:T(8,128)}, u32[]{:S(2)}) copy-start(s32[128,448]{0,1:T(8,128)} %param.13) | copy-start | bytes 688132
  2.7 24.6 %all-to-all-start = ((bf16[8,2,8,512]{3,2,1,0:T(8,128)(2,1)}), bf16[8,2,8,512]{3,2,1,0:T(8,128)(2,1)S(1)}, u32[]{:S(2)}, u32[]{:S(2)}) async-start(bf16[8,2,8,512]{3,2,1,0:T(8,128)(2,1)} %shard_map.111), calls=%async_computation | async-start | bytes 262144 | tf_op jit(solution)/shard_map/all_to_all | solution.py:176
  15.6 0.9 copy-start.7
  16.6 0.9 copy-start.8
  18.1 1.0 copy-start.22
  19.1 1.7 copy-start.23
  20.8 1.5 copy-start.24
  39.2 3.8 %collective-permute-start = (bf16[2,256,512]{2,1,0:T(8,128)(2,1)S(1)}, bf16[2,256,512]{2,1,0:T(8,128)(2,1)S(1)}, u32[]{:S(2)}, u32[]{:S(2)}) collective-permute-start(bf16[2,256,512]{2,1,0:T(8,128)(2,1)S(1)} %bitcast.71), channel_id=1, source_target_pairs={{0,1},{1,0},{2,3},{3,2},{4,5},{5,4},{6,7},{7,6},{8,9},{9,8},{10,11... | collective-permute-start | bytes 1572872 | tf_op jit(solution)/shard_map/ppermute | solution.py:183
  44.5 15.6 %all-to-all-start.3 = ((s16[4,352,256]{2,1,0:T(8,128)(2,1)}), s16[4,352,256]{2,1,0:T(8,128)(2,1)S(1)}, u32[]{:S(2)}, u32[]{:S(2)}) async-start(s16[4,352,256]{2,1,0:T(8,128)(2,1)} %shard_map.114), calls=%async_computation.3 | async-start | bytes 1441792 | tf_op jit(solution)/shard_map/all_to_all | solution.py:196
  48.7 0.9 copy-start
  60.1 19.6 %all-to-all-start.2 = ((s16[4,352,256]{2,1,0:T(8,128)(2,1)}), s16[4,352,256]{2,1,0:T(8,128)(2,1)S(1)}, u32[]{:S(2)}, u32[]{:S(2)}) async-start(s16[4,352,256]{2,1,0:T(8,128)(2,1)} %copy-done), calls=%async_computation.2 | async-start | bytes 1441792 | tf_op jit(solution)/shard_map/all_to_all | solution.py:199
  64.5 32.5 %collective-permute-start.1 = (s16[352,256]{1,0:T(8,128)(2,1)}, s16[352,256]{1,0:T(8,128)(2,1)S(1)}, u32[]{:S(2)}, u32[]{:S(2)}) collective-permute-start(s16[352,256]{1,0:T(8,128)(2,1)} %shard_map.115), channel_id=1, source_target_pairs={{0,256},{1,769},{256,0},{257,513},{512,768},{513,257},{768,512},{7... | collective-permute-start | bytes 540680 | tf_op jit(solution)/shard_map/ppermute | solution.py:38
  97.1 0.7 copy-start.1
  97.8 0.9 copy-start.2
  99.0 27.3 %collective-permute-start.2 = (s16[352,256]{1,0:T(8,128)(2,1)S(1)}, s16[352,256]{1,0:T(8,128)(2,1)S(1)}, u32[]{:S(2)}, u32[]{:S(2)}) collective-permute-start(s16[352,256]{1,0:T(8,128)(2,1)S(1)} %get-tuple-element.17), channel_id=1, source_target_pairs={{0,768},{1,257},{256,512},{257,1},{512,256},{513,769},{768,0},{769... | collective-permute-start | bytes 540680 | tf_op jit(solution)/shard_map/ppermute | solution.py:38
  127.3 26.7 %all-to-all-start.4 = ((bf16[4,336,256]{2,1,0:T(8,128)(2,1)}), bf16[4,336,256]{2,1,0:T(8,128)(2,1)S(1)}, u32[]{:S(2)}, u32[]{:S(2)}) async-start(bf16[4,336,256]{2,1,0:T(8,128)(2,1)} %get-tuple-element.18), calls=%async_computation.4 | async-start | bytes 1376256 | tf_op jit(solution)/shard_map/all_to_all | solution.py:207
  131.9 21.3 %collective-permute-start.3 = (bf16[336,256]{1,0:T(8,128)(2,1)S(1)}, bf16[336,256]{1,0:T(8,128)(2,1)S(1)}, u32[]{:S(2)}, u32[]{:S(2)}) collective-permute-start(bf16[336,256]{1,0:T(8,128)(2,1)S(1)} %get-tuple-element.19), channel_id=1, source_target_pairs={{0,256},{1,769},{256,0},{257,513},{512,768},{513,257},{768,512},{7... | collective-permute-start | bytes 516104 | tf_op jit(solution)/shard_map/ppermute | solution.py:38
  154.0 13.9 %all-to-all-start.5 = ((bf16[4,336,256]{2,1,0:T(8,128)(2,1)}), bf16[4,336,256]{2,1,0:T(8,128)(2,1)}, u32[]{:S(2)}, u32[]{:S(2)}) async-start(bf16[4,336,256]{2,1,0:T(8,128)(2,1)} %shard_map.118), calls=%async_computation.5 | async-start | bytes 1376256 | tf_op jit(solution)/shard_map/all_to_all | solution.py:209
  159.6 0.7 copy-start.11
  159.6 0.8 copy-start.15
  169.8 0.7 copy-start.13
  169.8 0.8 copy-start.9
  170.9 3.8 %collective-permute-start.4 = (f32[256,512]{1,0:T(8,128)S(1)}, f32[256,512]{1,0:T(8,128)S(1)}, u32[]{:S(2)}, u32[]{:S(2)}) collective-permute-start(f32[256,512]{1,0:T(8,128)S(1)} %get-tuple-element.61), channel_id=1, source_target_pairs={{0,1},{1,0},{2,3},{3,2},{4,5},{5,4},{6,7},{7,6},{8,9},{9,8},{10,11... | collective-permute-start | bytes 1572872 | tf_op jit(solution)/shard_map/ppermute | solution.py:223
  175.7 5.6 %copy-start.10 = (bf16[1,4,112,256]{3,2,0,1:T(8,128)(2,1)S(1)}, bf16[1,4,112,256]{3,2,0,1:T(8,128)(2,1)}, u32[]{:S(2)}) copy-start(bf16[1,4,112,256]{3,2,0,1:T(8,128)(2,1)} %copy-done.9) | copy-start | bytes 688132
  175.7 13.6 %all-to-all-start.6 = ((f32[4,64,512]{2,1,0:T(8,128)}), f32[4,64,512]{2,1,0:T(8,128)S(1)}, u32[]{:S(2)}, u32[]{:S(2)}) async-start(f32[4,64,512]{2,1,0:T(8,128)} %bitcast.23), calls=%async_computation.6 | async-start | bytes 1048576 | tf_op jit(solution)/shard_map/all_to_all | solution.py:224
  181.3 0.9 copy-start.14
  190.0 5.7 %copy-start.18 = (bf16[1,4,112,256]{3,2,0,1:T(8,128)(2,1)S(1)}, bf16[1,4,112,256]{3,2,0,1:T(8,128)(2,1)}, u32[]{:S(2)}) copy-start(bf16[1,4,112,256]{3,2,0,1:T(8,128)(2,1)} %get-tuple-element.52) | copy-start | bytes 688132
  190.0 17.2 %all-to-all-start.7 = ((f32[8,8,512]{2,1,0:T(8,128)}), f32[8,8,512]{2,1,0:T(8,128)S(1)}, u32[]{:S(2)}, u32[]{:S(2)}) async-start(f32[8,8,512]{2,1,0:T(8,128)} %bitcast.24), calls=%async_computation.7 | async-start | bytes 262144 | tf_op jit(solution)/shard_map/all_to_all | solution.py:225
  195.7 1.0 copy-start.5
  195.7 1.1 copy-start.16
  195.7 1.1 copy-start.20
  196.9 1.1 copy-start.12
  196.9 1.1 copy-start.21
  197.9 1.1 copy-start.17
  197.9 1.1 copy-start.19

commit v6 on v5

--- a/solution.py
+++ b/solution.py
@@ -70,14 +70,9 @@
     ]
 
 
-def spread_kernel(*refs):
-    out_ref = refs[-1]
+def spread_kernel(block_ref, out_ref):
     for c in range(out_ref.shape[0]):
-        if len(refs) == 2:
-            out_ref[c] = refs[0][...]
-        else:
-            for i, ref in enumerate(refs[:-1]):
-                out_ref[c, i] = ref[...]
+        out_ref[c] = block_ref[...]
 
 
 def partial_kernel(flag_ref, gate_ref, up_ref, down_ref, own_ref, other_ref, out_ref):
@@ -142,11 +137,58 @@
             spread_ref[c, i * units : (i + 1) * units, :] = result
 
 
+def back_product(block_ref, gate_ref, up_ref):
+    ny, units = block_ref.shape[0], block_ref.shape[1] // 3
+
+    def member(i):
+        return jnp.concatenate(
+            [block_ref[c, i * units : (i + 1) * units, :] for c in range(ny)], axis=0
+        )
+
+    return dot(member(1), gate_ref[...], ((0,), (0,))) + dot(
+        member(2), up_ref[...], ((0,), (0,))
+    )
+
+
+def first_back_kernel(block_ref, gate_ref, up_ref, out_ref):
+    out_ref[...] = back_product(block_ref, gate_ref, up_ref)
+
+
+def second_back_kernel(flag_ref, first_ref, block_ref, gate_ref, up_ref, stays_ref, leaves_ref):
+    first, second = first_ref[...], back_product(block_ref, gate_ref, up_ref)
+    first_stays = flag_ref[0] == 1
+    stays_ref[...] = jnp.where(first_stays, first, second)
+    leaves_ref[...] = jnp.where(first_stays, second, first)
+
+
+def core_sum_kernel(stays_ref, got_ref, send_ref):
+    rows = send_ref.shape[1] - EXTRA
+    for c in range(send_ref.shape[0]):
+        part = slice(c * rows, (c + 1) * rows)
+        value = stays_ref[part, :] + got_ref[part, :]
+        most = jnp.max(jnp.abs(value), axis=0, keepdims=True)
+        power = jnp.ceil(jnp.log2(jnp.maximum(most, 1e-30))) - 14.0
+        send_ref[c, :rows, :] = to_int16(jnp.round(value * jnp.exp2(-power)))
+        send_ref[c, rows:, :] = to_int16(jnp.broadcast_to(power, (EXTRA, value.shape[1])))
+
+
+def x_sum_kernel(block_ref, out_ref):
+    rows = block_ref.shape[1] - EXTRA
+    total = 0.0
+    for c in range(block_ref.shape[0]):
+        powers = wide(block_ref[c, rows:, :])
+        total = total + wide(block_ref[c, :rows, :]) * jnp.exp2(powers[:1, :])
+    count, each = out_ref.shape[0], out_ref.shape[1]
+    for c in range(count):
+        out_ref[c] = total[c * each : (c + 1) * each]
+
+
 def call(kernel, outs, *args, scalars=0):
-    places = [pltpu.SMEM] * scalars + [pltpu.VMEM] * (len(args) - scalars)
+    specs = [pl.BlockSpec(memory_space=pltpu.SMEM)] * scalars
+    specs += [pl.BlockSpec()] * (len(args) - scalars)
     return pl.pallas_call(
         kernel,
-        in_specs=[pl.BlockSpec(memory_space=place) for place in places],
+        in_specs=specs,
         out_shape=[jax.ShapeDtypeStruct(shape, kind) for shape, kind in outs],
         compiler_params=pltpu.CompilerParams(vmem_limit_bytes=32 * 2**20),
         cost_estimate=pl.CostEstimate(flops=COST, bytes_accessed=1024, transcendentals=0),
@@ -172,7 +214,8 @@
 
     swap = [(0, 1), (1, 0)]
     nx, nzlo = sizes["x"], sizes["zlo"]
-    (both,) = call(spread_kernel, [((nzlo, 2, rows, width), bf16)], inputs, cotangent)
+    both = jnp.stack([inputs, cotangent])
+    both = jnp.broadcast_to(both[None], (nzlo, *both.shape))
     both = lax.all_to_all(both, "zlo", 0, 0)
     both, gate_eff, up_eff, down_eff = lax.optimization_barrier(
         (both, gate_eff, up_eff, down_eff)
@@ -195,6 +238,7 @@
     (kept,) = call(partial_kernel, block, flag, *operands, scalars=1)
     sent = lax.all_to_all(sent, "y", 0, 0)
     (send,) = call(sent_sum_kernel, [((packed, half), i16)], sent)
+    kept, send = lax.optimization_barrier((kept, send))
     got = zhi_exchange(send, 1, 3)
     kept = lax.all_to_all(kept, "y", 0, 0)
     total, send = call(
@@ -208,22 +252,27 @@
     (to_y,) = call(spread_kernel, [spread], theirs)
     second = lax.all_to_all(to_y, "y", 0, 0)
 
+    (back_first,) = call(
+        first_back_kernel, [((half, width), f32)], first, gate_eff, up_eff
+    )
+    stays, leaves = call(
+        second_back_kernel,
+        [((half, width), f32)] * 2,
+        flag, back_first, second, gate_eff, up_eff,
+        scalars=1,
+    )
+    got = lax.ppermute(leaves, "core", swap)
+    (back,) = call(core_sum_kernel, [((nx, half // nx + EXTRA, width), i16)], stays, got)
+    back, first, second = lax.optimization_barrier((back, first, second))
+    back = lax.all_to_all(back, "x", 0, 0)
+    (back,) = call(x_sum_kernel, [((nzlo, rows, width), f32)], back)
+    back = lax.all_to_all(back, "zlo", 0, 0).sum(axis=0)
+
     def units(block):
         block = block.reshape(ny, 3, quarter, half)
         return block.transpose(1, 0, 2, 3).reshape(3, hidden_units, half)
 
     first, second = units(first), units(second)
-
-    def back_of(side):
-        return dot(side[1], gate_eff, ((0,), (0,))) + dot(side[2], up_eff, ((0,), (0,)))
-
-    back_first, back_second = back_of(first), back_of(second)
-    stays = jnp.where(own_kept, back_first, back_second)
-    leaves = jnp.where(own_kept, back_second, back_first)
-    back = stays + lax.ppermute(leaves, "core", swap)
-    back = lax.all_to_all(back.reshape(nx, half // nx, width), "x", 0, 0).sum(axis=0)
-    back = lax.all_to_all(back.reshape(nzlo, rows, width), "zlo", 0, 0).sum(axis=0)
-
     kept_side = jnp.where(own_kept, own, other)
     sent_side = jnp.where(own_kept, other, own)
 

time: 210 us -> 205 us (0.976)
  local copies, waits for them, and re-layouts: 11.4 us -> 6.1 us
    all_to_all x2, waiting for transfers between devices: 13.9 us -> 9.11 us  [the longest x1 6.41 us: body(): back = lax.all_to_all(back, 'zlo', 0, 0).sum(axis=0)]
    unnamed x50 -> x28, local copies, waits for them, and re-layouts: 8.75 us -> 5.3 us
    ppermute x3, waiting for transfers between devices: 59 us -> 61.5 us  [zhi_exchange(): return lax.ppermute(block, ('zhi', 'core'), pairs)]
    pallas_call x8 -> x11, Pallas kernels: 5.95 us -> 8.01 us  [call(): pl.pallas_call(kernel, in_specs=specs, out_shape=[jax.ShapeDtypeStruct(sh...]
    dot_general x13 -> x9, matrix products: 10.1 us -> 11.7 us  [dot(): return lax.dot_general(a, b, (dims, ((), ())), preferred_element_type=f32)]
  transfers between devices with their start and end apart: 12 -> 12, of which waited for: 10 -> 10; matrix products, arithmetic and copies ran while one was open for 6% -> 7% of each run, Pallas kernels for 1% -> 1%
where the time goes in v6:
time: 205 us; the launch traced here: 203 us
  waiting for transfers between devices  95.2 us (46%)
  starting transfers between devices  65.1 us (32%)
  blocking collectives  11.8 us (6%)
  matrix products  11.7 us (6%)
  Pallas kernels  8.01 us (4%)
  local copies, waits for them, and re-layouts  6.1 us (3%)
  other arithmetic  4.33 us (2%)
    ppermute x3, waiting for transfers between devices, zhi_exchange(): return lax.ppermute(block, ('zhi', 'core'), pairs)  61.5 us
    ppermute x3, starting transfers between devices, zhi_exchange(): return lax.ppermute(block, ('zhi', 'core'), pairs)  22.2 us
    all_to_all x1, starting transfers between devices, body(): both = lax.all_to_all(both, 'zlo', 0, 0)  12.5 us
    all_to_all x1, blocking collectives, body(): both = lax.all_to_all(both, 'x', 0, 0)  11.8 us
    dot_general x9, matrix products, dot(): return lax.dot_general(a, b, (dims, ((), ())), preferred_element_type=f32)  11.7 us
    all_to_all x1, waiting for transfers between devices, body(): sent = lax.all_to_all(sent, 'y', 0, 0)  10.6 us
    pallas_call x11, Pallas kernels, call(): pl.pallas_call(kernel, in_specs=specs, out_shape=[jax.ShapeDtypeStruct(sh...  8.01 us
    all_to_all x1, waiting for transfers between devices, body(): second = lax.all_to_all(to_y, 'y', 0, 0)  7.68 us
  transfers between devices with their start and end apart: 12, of which 10 were waited for; matrix products, arithmetic and copies ran while one was open for 7% of the time, Pallas kernels for 1%

profile of v6, /device:TPU:6, one launch (start us, length us, event | category | flops | bytes accessed | tf_op | source)
XLA Modules:
  0.0 203.3 jit_solution(12096051454135853526)
XLA Ops:
  0.6 0.8 pad_maximum_fusion
  1.4 0.7 broadcast_in_dim.20
  2.1 12.5 %all-to-all-start = ((bf16[8,2,8,512]{3,2,1,0:T(8,128)(2,1)}), bf16[8,2,8,512]{3,2,1,0:T(8,128)(2,1)S(1)}, u32[]{:S(2)}, u32[]{:S(2)}) async-start(bf16[8,2,8,512]{3,2,1,0:T(8,128)(2,1)} %broadcast_in_dim.20), calls=%async_computation | async-start | bytes 262144 | tf_op jit(solution)/shard_map/all_to_all | solution.py:219
  14.9 0.8 copy-done.7
  16.0 0.8 copy-done.8
  17.5 0.8 copy-done.11
  18.3 1.7 broadcast_select_fusion.2
  20.0 1.5 bitcast_select_fusion
  21.6 1.5 bitcast_select_fusion.1
  23.1 3.4 %all-to-all-done.block_ref = bf16[8,2,8,512]{3,2,1,0:T(8,128)(2,1)S(1)} async-done(((bf16[8,2,8,512]{3,2,1,0:T(8,128)(2,1)}), bf16[8,2,8,512]{3,2,1,0:T(8,128)(2,1)S(1)}, u32[]{:S(2)}, u32[]{:S(2)}) %all-to-all-start) | async-done | bytes 131104 | tf_op jit(solution)/shard_map/all_to_all | solution.py:219
  26.6 11.8 %all_to_all.40 = bf16[4,8,2,8,512]{4,3,2,1,0:T(8,128)(2,1)S(1)} all-to-all(bf16[4,8,2,8,512]{4,3,2,1,0:T(8,128)(2,1)S(1)} %shard_map.111), channel_id=1, replica_groups=mesh['zhi'=4,'y'=4,'zlo'=8,'x'=4,'core'=2] {'x'}, dimensions={0} | all-to-all | bytes 1048576 | tf_op jit(solution)/shard_map/all_to_all | solution.py:224
  38.4 1.9 collective-permute-start
  40.4 1.9 collective-permute-done.other_ref
  42.2 1.5 shard_map.113
  43.8 3.5 %all-to-all-start.2 = ((s16[4,352,256]{2,1,0:T(8,128)(2,1)}), s16[4,352,256]{2,1,0:T(8,128)(2,1)S(1)}, u32[]{:S(2)}, u32[]{:S(2)}) async-start(s16[4,352,256]{2,1,0:T(8,128)(2,1)} %shard_map.113), calls=%async_computation.2 | async-start | bytes 1441792 | tf_op jit(solution)/shard_map/all_to_all | solution.py:239
  47.3 1.5 shard_map.112
  48.8 10.6 %all-to-all-done.2.block_ref = s16[4,352,256]{2,1,0:T(8,128)(2,1)S(1)} async-done(((s16[4,352,256]{2,1,0:T(8,128)(2,1)}), s16[4,352,256]{2,1,0:T(8,128)(2,1)S(1)}, u32[]{:S(2)}, u32[]{:S(2)}) %all-to-all-start.2) | async-done | bytes 720928 | tf_op jit(solution)/shard_map/all_to_all | solution.py:239
  59.6 3.5 %all-to-all-start.3 = ((s16[4,352,256]{2,1,0:T(8,128)(2,1)}), s16[4,352,256]{2,1,0:T(8,128)(2,1)S(1)}, u32[]{:S(2)}, u32[]{:S(2)}) async-start(s16[4,352,256]{2,1,0:T(8,128)(2,1)} %shard_map.112), calls=%async_computation.3 | async-start | bytes 1441792 | tf_op jit(solution)/shard_map/all_to_all | solution.py:243
  63.1 15.2 %collective-permute-start.1 = (s16[352,256]{1,0:T(8,128)(2,1)S(1)}, s16[352,256]{1,0:T(8,128)(2,1)S(1)}, u32[]{:S(2)}, u32[]{:S(2)}) collective-permute-start(s16[352,256]{1,0:T(8,128)(2,1)S(1)} %shard_map.114), channel_id=1, source_target_pairs={{0,256},{1,769},{256,0},{257,513},{512,768},{513,257},{768,512},{7... | collective-permute-start | bytes 540680 | tf_op jit(solution)/shard_map/ppermute | solution.py:38
  78.4 17.1 %collective-permute-done.1.got_ref = s16[352,256]{1,0:T(8,128)(2,1)S(1)} collective-permute-done((s16[352,256]{1,0:T(8,128)(2,1)S(1)}, s16[352,256]{1,0:T(8,128)(2,1)S(1)}, u32[]{:S(2)}, u32[]{:S(2)}) %collective-permute-start.1) | collective-permute-done | bytes 180256 | tf_op jit(solution)/shard_map/ppermute | solution.py:38
  95.8 4.7 %collective-permute-start.2 = (s16[352,256]{1,0:T(8,128)(2,1)S(1)}, s16[352,256]{1,0:T(8,128)(2,1)S(1)}, u32[]{:S(2)}, u32[]{:S(2)}) collective-permute-start(s16[352,256]{1,0:T(8,128)(2,1)S(1)} %get-tuple-element.26), channel_id=1, source_target_pairs={{0,768},{1,257},{256,512},{257,1},{512,256},{513,769},{768,0},{769... | collective-permute-start | bytes 540680 | tf_op jit(solution)/shard_map/ppermute | solution.py:38
  100.5 22.7 %collective-permute-done.2.got_ref = s16[352,256]{1,0:T(8,128)(2,1)S(1)} collective-permute-done((s16[352,256]{1,0:T(8,128)(2,1)S(1)}, s16[352,256]{1,0:T(8,128)(2,1)S(1)}, u32[]{:S(2)}, u32[]{:S(2)}) %collective-permute-start.2) | collective-permute-done | bytes 180256 | tf_op jit(solution)/shard_map/ppermute | solution.py:38
  123.1 1.0 shard_map.116
  124.1 3.5 %all-to-all-start.4 = ((bf16[4,336,256]{2,1,0:T(8,128)(2,1)}), bf16[4,336,256]{2,1,0:T(8,128)(2,1)S(1)}, u32[]{:S(2)}, u32[]{:S(2)}) async-start(bf16[4,336,256]{2,1,0:T(8,128)(2,1)} %get-tuple-element.27), calls=%async_computation.4 | async-start | bytes 1376256 | tf_op jit(solution)/shard_map/all_to_all | solution.py:251
  127.6 2.3 %collective-permute-start.3 = (bf16[336,256]{1,0:T(8,128)(2,1)S(1)}, bf16[336,256]{1,0:T(8,128)(2,1)S(1)}, u32[]{:S(2)}, u32[]{:S(2)}) collective-permute-start(bf16[336,256]{1,0:T(8,128)(2,1)S(1)} %get-tuple-element.28), channel_id=1, source_target_pairs={{0,256},{1,769},{256,0},{257,513},{512,768},{513,257},{768,512},{7... | collective-permute-start | bytes 516104 | tf_op jit(solution)/shard_map/ppermute | solution.py:38
  130.0 21.7 %collective-permute-done.3.block_ref = bf16[336,256]{1,0:T(8,128)(2,1)S(1)} collective-permute-done((bf16[336,256]{1,0:T(8,128)(2,1)S(1)}, bf16[336,256]{1,0:T(8,128)(2,1)S(1)}, u32[]{:S(2)}, u32[]{:S(2)}) %collective-permute-start.3) | collective-permute-done | bytes 172064 | tf_op jit(solution)/shard_map/ppermute | solution.py:38
  151.7 0.9 shard_map.118
  152.6 4.6 %all-to-all-start.5 = ((bf16[4,336,256]{2,1,0:T(8,128)(2,1)}), bf16[4,336,256]{2,1,0:T(8,128)(2,1)S(1)}, u32[]{:S(2)}, u32[]{:S(2)}) async-start(bf16[4,336,256]{2,1,0:T(8,128)(2,1)} %shard_map.118), calls=%async_computation.5 | async-start | bytes 1376256 | tf_op jit(solution)/shard_map/all_to_all | solution.py:253
  157.6 0.8 copy-done
  158.4 7.7 %all-to-all-done.5.block_ref = bf16[4,336,256]{2,1,0:T(8,128)(2,1)S(1)} async-done(((bf16[4,336,256]{2,1,0:T(8,128)(2,1)}), bf16[4,336,256]{2,1,0:T(8,128)(2,1)S(1)}, u32[]{:S(2)}, u32[]{:S(2)}) %all-to-all-start.5) | async-done | bytes 688160 | tf_op jit(solution)/shard_map/all_to_all | solution.py:253
  166.1 1.0 copy-done.1
  167.1 0.5 shard_map.119
  167.6 1.9 collective-permute-start.4
  169.5 0.9 broadcast_select_fusion.1
  170.5 1.0 collective-permute-done.4.got_ref
  171.4 0.8 shard_map.120
  172.3 4.5 %all-to-all-start.6 = ((s16[4,80,512]{2,1,0:T(8,128)(2,1)}), s16[4,80,512]{2,1,0:T(8,128)(2,1)S(1)}, u32[]{:S(2)}, u32[]{:S(2)}) async-start(s16[4,80,512]{2,1,0:T(8,128)(2,1)} %shard_map.120), calls=%async_computation.6 | async-start | bytes 655360 | tf_op jit(solution)/shard_map/all_to_all | solution.py:267
  176.9 1.3 fusion.36
  178.1 1.3 fusion.34
  179.7 2.7 %all-to-all-done.6.block_ref = s16[4,80,512]{2,1,0:T(8,128)(2,1)S(1)} async-done(((s16[4,80,512]{2,1,0:T(8,128)(2,1)}), s16[4,80,512]{2,1,0:T(8,128)(2,1)S(1)}, u32[]{:S(2)}, u32[]{:S(2)}) %all-to-all-start.6) | async-done | bytes 327712 | tf_op jit(solution)/shard_map/all_to_all | solution.py:267
  182.4 0.7 shard_map.121
  183.2 7.0 %all-to-all-start.7 = ((f32[8,8,512]{2,1,0:T(8,128)}), f32[8,8,512]{2,1,0:T(8,128)}, u32[]{:S(2)}, u32[]{:S(2)}) async-start(f32[8,8,512]{2,1,0:T(8,128)} %shard_map.121), calls=%async_computation.7 | async-start | bytes 262144 | tf_op jit(solution)/shard_map/all_to_all | solution.py:269
  190.2 1.0 copy-done.5
  191.2 2.0 %fusion.5 = bf16[512,448]{0,1:T(8,128)(2,1)} fusion(f32[512,448]{0,1:T(8,128)S(1)} %copy-done.2, bf16[448,256]{1,0:T(8,128)(2,1)S(1)} %bitcast.71, pred[448,512]{1,0:T(32,128)(4,1)} %get-tuple-element.72, bf16[2,256,512]{2,1,0:T(8,128)(2,1)S(1)} %copy-done.5), kind=kOutput, calls=%fused_computation.8 | convolution fusion | flops 118128640 | bytes 2097152 | tf_op jit(solution)/shard_map/dot_general | solution.py:31
  193.2 1.1 fusion.3
  194.3 1.1 fusion.4
  195.3 6.4 %all-to-all-done.7 = f32[8,8,512]{2,1,0:T(8,128)} async-done(((f32[8,8,512]{2,1,0:T(8,128)}), f32[8,8,512]{2,1,0:T(8,128)}, u32[]{:S(2)}, u32[]{:S(2)}) %all-to-all-start.7) | async-done | bytes 131104 | tf_op jit(solution)/shard_map/all_to_all | solution.py:269
  201.7 1.5 reduce_sum.9
  (50 shorter events, 2.6 us)
Async XLA Ops:
  0.6 14.0 %copy-start.6 = (s32[128,448]{0,1:T(8,128)S(1)}, s32[128,448]{0,1:T(8,128)}, u32[]{:S(2)}) copy-start(s32[128,448]{0,1:T(8,128)} %param.13) | copy-start | bytes 688132
  2.1 24.5 %all-to-all-start = ((bf16[8,2,8,512]{3,2,1,0:T(8,128)(2,1)}), bf16[8,2,8,512]{3,2,1,0:T(8,128)(2,1)S(1)}, u32[]{:S(2)}, u32[]{:S(2)}) async-start(bf16[8,2,8,512]{3,2,1,0:T(8,128)(2,1)} %broadcast_in_dim.20), calls=%async_computation | async-start | bytes 262144 | tf_op jit(solution)/shard_map/all_to_all | solution.py:219
  14.8 0.9 copy-start.7
  15.9 0.9 copy-start.8
  17.3 1.0 copy-start.11
  18.3 1.7 copy-start.12
  20.0 1.5 copy-start.13
  38.4 3.8 %collective-permute-start = (bf16[2,256,512]{2,1,0:T(8,128)(2,1)S(1)}, bf16[2,256,512]{2,1,0:T(8,128)(2,1)S(1)}, u32[]{:S(2)}, u32[]{:S(2)}) collective-permute-start(bf16[2,256,512]{2,1,0:T(8,128)(2,1)S(1)} %bitcast.65), channel_id=1, source_target_pairs={{0,1},{1,0},{2,3},{3,2},{4,5},{5,4},{6,7},{7,6},{8,9},{9,8},{10,11... | collective-permute-start | bytes 1572872 | tf_op jit(solution)/shard_map/ppermute | solution.py:226
  43.8 15.6 %all-to-all-start.2 = ((s16[4,352,256]{2,1,0:T(8,128)(2,1)}), s16[4,352,256]{2,1,0:T(8,128)(2,1)S(1)}, u32[]{:S(2)}, u32[]{:S(2)}) async-start(s16[4,352,256]{2,1,0:T(8,128)(2,1)} %shard_map.113), calls=%async_computation.2 | async-start | bytes 1441792 | tf_op jit(solution)/shard_map/all_to_all | solution.py:239
  59.6 35.9 %all-to-all-start.3 = ((s16[4,352,256]{2,1,0:T(8,128)(2,1)}), s16[4,352,256]{2,1,0:T(8,128)(2,1)S(1)}, u32[]{:S(2)}, u32[]{:S(2)}) async-start(s16[4,352,256]{2,1,0:T(8,128)(2,1)} %shard_map.112), calls=%async_computation.3 | async-start | bytes 1441792 | tf_op jit(solution)/shard_map/all_to_all | solution.py:243
  63.1 32.4 %collective-permute-start.1 = (s16[352,256]{1,0:T(8,128)(2,1)S(1)}, s16[352,256]{1,0:T(8,128)(2,1)S(1)}, u32[]{:S(2)}, u32[]{:S(2)}) collective-permute-start(s16[352,256]{1,0:T(8,128)(2,1)S(1)} %shard_map.114), channel_id=1, source_target_pairs={{0,256},{1,769},{256,0},{257,513},{512,768},{513,257},{768,512},{7... | collective-permute-start | bytes 540680 | tf_op jit(solution)/shard_map/ppermute | solution.py:38
  95.8 27.4 %collective-permute-start.2 = (s16[352,256]{1,0:T(8,128)(2,1)S(1)}, s16[352,256]{1,0:T(8,128)(2,1)S(1)}, u32[]{:S(2)}, u32[]{:S(2)}) collective-permute-start(s16[352,256]{1,0:T(8,128)(2,1)S(1)} %get-tuple-element.26), channel_id=1, source_target_pairs={{0,768},{1,257},{256,512},{257,1},{512,256},{513,769},{768,0},{769... | collective-permute-start | bytes 540680 | tf_op jit(solution)/shard_map/ppermute | solution.py:38
  124.1 28.5 %all-to-all-start.4 = ((bf16[4,336,256]{2,1,0:T(8,128)(2,1)}), bf16[4,336,256]{2,1,0:T(8,128)(2,1)S(1)}, u32[]{:S(2)}, u32[]{:S(2)}) async-start(bf16[4,336,256]{2,1,0:T(8,128)(2,1)} %get-tuple-element.27), calls=%async_computation.4 | async-start | bytes 1376256 | tf_op jit(solution)/shard_map/all_to_all | solution.py:251
  127.6 24.1 %collective-permute-start.3 = (bf16[336,256]{1,0:T(8,128)(2,1)S(1)}, bf16[336,256]{1,0:T(8,128)(2,1)S(1)}, u32[]{:S(2)}, u32[]{:S(2)}) collective-permute-start(bf16[336,256]{1,0:T(8,128)(2,1)S(1)} %get-tuple-element.28), channel_id=1, source_target_pairs={{0,256},{1,769},{256,0},{257,513},{512,768},{513,257},{768,512},{7... | collective-permute-start | bytes 516104 | tf_op jit(solution)/shard_map/ppermute | solution.py:38
  152.6 13.5 %all-to-all-start.5 = ((bf16[4,336,256]{2,1,0:T(8,128)(2,1)}), bf16[4,336,256]{2,1,0:T(8,128)(2,1)S(1)}, u32[]{:S(2)}, u32[]{:S(2)}) async-start(bf16[4,336,256]{2,1,0:T(8,128)(2,1)} %shard_map.118), calls=%async_computation.5 | async-start | bytes 1376256 | tf_op jit(solution)/shard_map/all_to_all | solution.py:253
  157.6 0.8 copy-start
  166.1 1.0 copy-start.1
  167.6 3.8 %collective-permute-start.4 = (f32[256,512]{1,0:T(8,128)S(1)}, f32[256,512]{1,0:T(8,128)S(1)}, u32[]{:S(2)}, u32[]{:S(2)}) collective-permute-start(f32[256,512]{1,0:T(8,128)S(1)} %get-tuple-element.30), channel_id=1, source_target_pairs={{0,1},{1,0},{2,3},{3,2},{4,5},{5,4},{6,7},{7,6},{8,9},{9,8},{10,11... | collective-permute-start | bytes 1572872 | tf_op jit(solution)/shard_map/ppermute | solution.py:264
  170.5 6.4 %copy-start.3 = (bf16[2,256,512]{2,1,0:T(8,128)(2,1)}, bf16[2,256,512]{2,1,0:T(8,128)(2,1)S(1)}, u32[]{:S(2)}) copy-start(bf16[2,256,512]{2,1,0:T(8,128)(2,1)S(1)} %get-tuple-element.62) | copy-start | bytes 1572868
  172.3 10.1 %all-to-all-start.6 = ((s16[4,80,512]{2,1,0:T(8,128)(2,1)}), s16[4,80,512]{2,1,0:T(8,128)(2,1)S(1)}, u32[]{:S(2)}, u32[]{:S(2)}) async-start(s16[4,80,512]{2,1,0:T(8,128)(2,1)} %shard_map.120), calls=%async_computation.6 | async-start | bytes 655360 | tf_op jit(solution)/shard_map/all_to_all | solution.py:267
  178.1 1.3 copy-start.4
  183.1 7.0 %copy-start.2 = (f32[512,448]{0,1:T(8,128)S(1)}, f32[512,448]{0,1:T(8,128)}, u32[]{:S(2)}) copy-start(f32[512,448]{0,1:T(8,128)} %fusion.36) | copy-start | bytes 2752516
  183.2 18.6 %all-to-all-start.7 = ((f32[8,8,512]{2,1,0:T(8,128)}), f32[8,8,512]{2,1,0:T(8,128)}, u32[]{:S(2)}, u32[]{:S(2)}) async-start(f32[8,8,512]{2,1,0:T(8,128)} %shard_map.121), calls=%async_computation.7 | async-start | bytes 262144 | tf_op jit(solution)/shard_map/all_to_all | solution.py:269
  190.1 1.0 copy-start.5
  191.2 2.0 %copy-start.9 = (pred[448,512]{1,0:T(32,128)(4,1)S(1)}, pred[448,512]{1,0:T(32,128)(4,1)}, u32[]{:S(2)}) copy-start(pred[448,512]{1,0:T(32,128)(4,1)} %get-tuple-element.74) | copy-start | bytes 688132
  193.2 1.1 copy-start.10

commit v7 on v6

--- a/solution.py
+++ b/solution.py
@@ -77,16 +77,21 @@
 
 def partial_kernel(flag_ref, gate_ref, up_ref, down_ref, own_ref, other_ref, out_ref):
     ny, units = out_ref.shape[0], gate_ref.shape[0] // out_ref.shape[0]
-    is_own = flag_ref[0] == 1
-    tokens = jnp.where(is_own, own_ref[0], other_ref[0])
-    grad_out = jnp.where(is_own, own_ref[1], other_ref[1])
-    products = [
-        dot(gate_ref[...], tokens, ((1,), (1,))),
-        dot(up_ref[...], tokens, ((1,), (1,))),
-        dot(down_ref[...], grad_out, ((1,), (1,))),
-    ]
-    for c in range(ny):
-        store([p[c * units : (c + 1) * units] for p in products], out_ref.at[c])
+    half = own_ref.shape[1]
+    own_front = flag_ref[0] == 1
+    for spot, (a_ref, b_ref) in enumerate(((own_ref, other_ref), (other_ref, own_ref))):
+        tokens = jnp.where(own_front, a_ref[0], b_ref[0])
+        grad_out = jnp.where(own_front, a_ref[1], b_ref[1])
+        products = [
+            dot(gate_ref[...], tokens, ((1,), (1,))),
+            dot(up_ref[...], tokens, ((1,), (1,))),
+            dot(down_ref[...], grad_out, ((1,), (1,))),
+        ]
+        for c in range(ny):
+            store(
+                [p[c * units : (c + 1) * units] for p in products],
+                out_ref.at[c, :, spot * half : (spot + 1) * half],
+            )
 
 
 def store(values, send_ref):
@@ -106,20 +111,23 @@
     return total
 
 
-def sent_sum_kernel(block_ref, send_ref):
-    store(sum_over_blocks(block_ref), send_ref)
-
-
-def kept_sum_kernel(block_ref, got_ref, total_ref, send_ref):
-    total = sum_over_blocks(block_ref)
-    parts = unpack(got_ref, total_ref.shape[1])
-    total = [total[i] + parts[i] for i in range(3)]
+def first_sum_kernel(block_ref, total_ref, send_ref):
+    half = total_ref.shape[2]
+    total = sum_over_blocks(block_ref.at[:, :, :half])
     for i in range(3):
         total_ref[i] = total[i]
+    store(sum_over_blocks(block_ref.at[:, :, half:]), send_ref)
+
+
+def next_sum_kernel(total_ref, got_ref, out_ref, send_ref):
+    parts = unpack(got_ref, total_ref.shape[1])
+    total = [total_ref[i] + parts[i] for i in range(3)]
+    for i in range(3):
+        out_ref[i] = total[i]
     store(total, send_ref)
 
 
-def swiglu_kernel(total_ref, got_ref, out_ref, spread_ref):
+def swiglu_kernel(total_ref, got_ref, out_ref):
     units = total_ref.shape[1]
     parts = unpack(got_ref, units)
     gate_pre, up_pre, hidden_grad = [total_ref[i] + parts[i] for i in range(3)]
@@ -131,10 +139,7 @@
         hidden_grad * silu_gate,
     )
     for i, result in enumerate(results):
-        result = result.astype(bf16)
-        out_ref[i * units : (i + 1) * units, :] = result
-        for c in range(spread_ref.shape[0]):
-            spread_ref[c, i * units : (i + 1) * units, :] = result
+        out_ref[i * units : (i + 1) * units, :] = result.astype(bf16)
 
 
 def back_product(block_ref, gate_ref, up_ref):
@@ -232,24 +237,24 @@
 
     i16 = jnp.int16
     packed = 3 * quarter + EXTRA
-    block = [((ny, packed, half), i16)]
-    operands = (gate_eff, up_eff, down_eff, own, other)
-    (sent,) = call(partial_kernel, block, 1 - flag, *operands, scalars=1)
-    (kept,) = call(partial_kernel, block, flag, *operands, scalars=1)
-    sent = lax.all_to_all(sent, "y", 0, 0)
-    (send,) = call(sent_sum_kernel, [((packed, half), i16)], sent)
-    kept, send = lax.optimization_barrier((kept, send))
+    (block,) = call(
+        partial_kernel,
+        [((ny, packed, 2 * half), i16)],
+        flag, gate_eff, up_eff, down_eff, own, other,
+        scalars=1,
+    )
+    block = lax.all_to_all(block, "y", 0, 0)
+    pair = [((3, quarter, half), f32), ((packed, half), i16)]
+    total, send = call(first_sum_kernel, pair, block)
     got = zhi_exchange(send, 1, 3)
-    kept = lax.all_to_all(kept, "y", 0, 0)
-    total, send = call(
-        kept_sum_kernel, [((3, quarter, half), f32), ((packed, half), i16)], kept, got
-    )
+    total, send = call(next_sum_kernel, pair, total, got)
     got = zhi_exchange(send, 3, 1)
-    spread = ((ny, 3 * quarter, half), bf16)
-    mine, to_y = call(swiglu_kernel, [((3 * quarter, half), bf16), spread], total, got)
+    (mine,) = call(swiglu_kernel, [((3 * quarter, half), bf16)], total, got)
     theirs = zhi_exchange(mine, 1, 3)
+    spread = [((ny, 3 * quarter, half), bf16)]
+    (to_y,) = call(spread_kernel, spread, mine)
     first = lax.all_to_all(to_y, "y", 0, 0)
-    (to_y,) = call(spread_kernel, [spread], theirs)
+    (to_y,) = call(spread_kernel, spread, theirs)
     second = lax.all_to_all(to_y, "y", 0, 0)
 
     (back_first,) = call(

time: 205 us -> 207 us (level)
  blocking collectives: 11.8 us -> 34.5 us
  waiting for transfers between devices: 95.2 us -> 83.9 us
  starting transfers between devices: 65.1 us -> 58.1 us
  local copies, waits for them, and re-layouts: 6.1 us -> 3.92 us
    all_to_all x0 -> x1, blocking collectives: none -> 22.6 us  [body(): block = lax.all_to_all(block, 'y', 0, 0)]
    all_to_all x2 -> x0, waiting for transfers between devices: 10.6 us -> none  [the longest x1 10.6 us: body(): sent = lax.all_to_all(sent, 'y', 0, 0)]
    all_to_all x2 -> x0, starting transfers between devices: 6.99 us -> none  [the longest x1 3.5 us: body(): kept = lax.all_to_all(kept, 'y', 0, 0)]
    unnamed x28, local copies, waits for them, and re-layouts: 5.3 us -> 3.12 us
    all_to_all x1, starting transfers between devices: 4.54 us -> 6.61 us  [body(): back = lax.all_to_all(back, 'x', 0, 0)]
  transfers between devices with their start and end apart: 12 -> 10, of which waited for: 10 -> 9; matrix products, arithmetic and copies ran while one was open for 7% -> 8% of each run, Pallas kernels for 1% -> 1%
where the time goes in v7:
time: 207 us; the launch traced here: 205 us
  waiting for transfers between devices  83.9 us (41%)
  starting transfers between devices  58.1 us (28%)
  blocking collectives  34.5 us (17%)
  matrix products  11.7 us (6%)
  other arithmetic  6.26 us (3%)
  Pallas kernels  6.15 us (3%)
  local copies, waits for them, and re-layouts  3.92 us (2%)
    ppermute x3, waiting for transfers between devices, zhi_exchange(): return lax.ppermute(block, ('zhi', 'core'), pairs)  59.8 us
    all_to_all x1, blocking collectives, body(): block = lax.all_to_all(block, 'y', 0, 0)  22.6 us
    ppermute x3, starting transfers between devices, zhi_exchange(): return lax.ppermute(block, ('zhi', 'core'), pairs)  22.3 us
    all_to_all x1, starting transfers between devices, body(): both = lax.all_to_all(both, 'zlo', 0, 0)  12.5 us
    all_to_all x1, blocking collectives, body(): both = lax.all_to_all(both, 'x', 0, 0)  11.8 us
    dot_general x9, matrix products, dot(): return lax.dot_general(a, b, (dims, ((), ())), preferred_element_type=f32)  11.7 us
    all_to_all x1, waiting for transfers between devices, body(): second = lax.all_to_all(to_y, 'y', 0, 0)  7.7 us
    all_to_all x1, starting transfers between devices, body(): back = lax.all_to_all(back, 'x', 0, 0)  6.61 us
  transfers between devices with their start and end apart: 10, of which 9 were waited for; matrix products, arithmetic and copies ran while one was open for 8% of the time, Pallas kernels for 1%

profile of v7, /device:TPU:6, one launch (start us, length us, event | category | flops | bytes accessed | tf_op | source)
XLA Modules:
  0.0 205.5 jit_solution(17573049436149832274)
XLA Ops:
  0.7 0.8 pad_maximum_fusion
  1.4 0.7 broadcast_in_dim.20
  2.1 12.5 %all-to-all-start = ((bf16[8,2,8,512]{3,2,1,0:T(8,128)(2,1)}), bf16[8,2,8,512]{3,2,1,0:T(8,128)(2,1)S(1)}, u32[]{:S(2)}, u32[]{:S(2)}) async-start(bf16[8,2,8,512]{3,2,1,0:T(8,128)(2,1)} %broadcast_in_dim.20), calls=%async_computation | async-start | bytes 262144 | tf_op jit(solution)/shard_map/all_to_all | solution.py:224
  14.7 1.1 or_bitcast_fusion.7
  15.8 1.0 or_bitcast_fusion.6
  17.8 0.3 copy-done.11
  18.1 1.7 broadcast_select_fusion.2
  19.8 1.5 bitcast_select_fusion
  21.4 1.5 bitcast_select_fusion.1
  22.9 3.7 %all-to-all-done.block_ref = bf16[8,2,8,512]{3,2,1,0:T(8,128)(2,1)S(1)} async-done(((bf16[8,2,8,512]{3,2,1,0:T(8,128)(2,1)}), bf16[8,2,8,512]{3,2,1,0:T(8,128)(2,1)S(1)}, u32[]{:S(2)}, u32[]{:S(2)}) %all-to-all-start) | async-done | bytes 131104 | tf_op jit(solution)/shard_map/all_to_all | solution.py:224
  26.6 11.8 %all_to_all.35 = bf16[4,8,2,8,512]{4,3,2,1,0:T(8,128)(2,1)S(1)} all-to-all(bf16[4,8,2,8,512]{4,3,2,1,0:T(8,128)(2,1)S(1)} %shard_map.111), channel_id=1, replica_groups=mesh['zhi'=4,'y'=4,'zlo'=8,'x'=4,'core'=2] {'x'}, dimensions={0} | all-to-all | bytes 1048576 | tf_op jit(solution)/shard_map/all_to_all | solution.py:229
  38.5 1.9 collective-permute-start
  40.4 1.9 collective-permute-done.other_ref
  42.3 1.1 shard_map.112
  43.3 22.6 %all_to_all.36.block_ref = s16[4,352,512]{2,1,0:T(8,128)(2,1)S(1)} all-to-all(s16[4,352,512]{2,1,0:T(8,128)(2,1)S(1)} %shard_map.112), channel_id=1, replica_groups=mesh['zhi'=4,'y'=4,'zlo'=8,'x'=4,'core'=2] {'y'}, dimensions={0} | all-to-all | bytes 2883584 | tf_op jit(solution)/shard_map/all_to_all | solution.py:246
  66.0 0.5 shard_map.113
  66.5 15.7 %collective-permute-start.1 = (s16[352,256]{1,0:T(8,128)(2,1)S(1)}, s16[352,256]{1,0:T(8,128)(2,1)S(1)}, u32[]{:S(2)}, u32[]{:S(2)}) collective-permute-start(s16[352,256]{1,0:T(8,128)(2,1)S(1)} %get-tuple-element.22), channel_id=1, source_target_pairs={{0,256},{1,769},{256,0},{257,513},{512,768},{513,257},{768,512},{7... | collective-permute-start | bytes 540680 | tf_op jit(solution)/shard_map/ppermute | solution.py:38
  82.2 17.1 %collective-permute-done.1.got_ref = s16[352,256]{1,0:T(8,128)(2,1)S(1)} collective-permute-done((s16[352,256]{1,0:T(8,128)(2,1)S(1)}, s16[352,256]{1,0:T(8,128)(2,1)S(1)}, u32[]{:S(2)}, u32[]{:S(2)}) %collective-permute-start.1) | collective-permute-done | bytes 180256 | tf_op jit(solution)/shard_map/ppermute | solution.py:38
  99.5 4.6 %collective-permute-start.2 = (s16[352,256]{1,0:T(8,128)(2,1)S(1)}, s16[352,256]{1,0:T(8,128)(2,1)S(1)}, u32[]{:S(2)}, u32[]{:S(2)}) collective-permute-start(s16[352,256]{1,0:T(8,128)(2,1)S(1)} %get-tuple-element.24), channel_id=1, source_target_pairs={{0,768},{1,257},{256,512},{257,1},{512,256},{513,769},{768,0},{769... | collective-permute-start | bytes 540680 | tf_op jit(solution)/shard_map/ppermute | solution.py:38
  104.1 22.9 %collective-permute-done.2.got_ref = s16[352,256]{1,0:T(8,128)(2,1)S(1)} collective-permute-done((s16[352,256]{1,0:T(8,128)(2,1)S(1)}, s16[352,256]{1,0:T(8,128)(2,1)S(1)}, u32[]{:S(2)}, u32[]{:S(2)}) %collective-permute-start.2) | collective-permute-done | bytes 180256 | tf_op jit(solution)/shard_map/ppermute | solution.py:38
  127.1 0.9 shard_map.116
  128.1 3.5 %all-to-all-start.3 = ((bf16[4,336,256]{2,1,0:T(8,128)(2,1)}), bf16[4,336,256]{2,1,0:T(8,128)(2,1)S(1)}, u32[]{:S(2)}, u32[]{:S(2)}) async-start(bf16[4,336,256]{2,1,0:T(8,128)(2,1)} %shard_map.116), calls=%async_computation.3 | async-start | bytes 1376256 | tf_op jit(solution)/shard_map/all_to_all | solution.py:256
  131.5 1.9 collective-permute-start.3
  133.5 19.7 %collective-permute-done.3.block_ref = bf16[336,256]{1,0:T(8,128)(2,1)S(1)} collective-permute-done((bf16[336,256]{1,0:T(8,128)(2,1)S(1)}, bf16[336,256]{1,0:T(8,128)(2,1)S(1)}, u32[]{:S(2)}, u32[]{:S(2)}) %collective-permute-start.3) | collective-permute-done | bytes 172064 | tf_op jit(solution)/shard_map/ppermute | solution.py:38
  153.2 0.9 shard_map.118
  154.1 4.5 %all-to-all-start.4 = ((bf16[4,336,256]{2,1,0:T(8,128)(2,1)}), bf16[4,336,256]{2,1,0:T(8,128)(2,1)S(1)}, u32[]{:S(2)}, u32[]{:S(2)}) async-start(bf16[4,336,256]{2,1,0:T(8,128)(2,1)} %shard_map.118), calls=%async_computation.4 | async-start | bytes 1376256 | tf_op jit(solution)/shard_map/all_to_all | solution.py:258
  158.6 0.5 shard_map.117.first_ref
  159.0 0.8 copy-done
  159.8 7.7 %all-to-all-done.4.block_ref = bf16[4,336,256]{2,1,0:T(8,128)(2,1)S(1)} async-done(((bf16[4,336,256]{2,1,0:T(8,128)(2,1)}), bf16[4,336,256]{2,1,0:T(8,128)(2,1)S(1)}, u32[]{:S(2)}, u32[]{:S(2)}) %all-to-all-start.4) | async-done | bytes 688160 | tf_op jit(solution)/shard_map/all_to_all | solution.py:258
  167.5 1.0 copy-done.1
  168.6 0.5 shard_map.119
  169.0 1.9 collective-permute-start.4
  171.0 0.9 broadcast_select_fusion.1
  171.9 1.0 collective-permute-done.4.got_ref
  172.8 0.8 shard_map.120
  173.7 6.6 %all-to-all-start.5 = ((s16[4,80,512]{2,1,0:T(8,128)(2,1)}), s16[4,80,512]{2,1,0:T(8,128)(2,1)S(1)}, u32[]{:S(2)}, u32[]{:S(2)}) async-start(s16[4,80,512]{2,1,0:T(8,128)(2,1)} %shard_map.120), calls=%async_computation.5 | async-start | bytes 655360 | tf_op jit(solution)/shard_map/all_to_all | solution.py:272
  180.4 1.2 fusion.36
  181.6 1.3 fusion.34
  182.9 0.3 fusion.35
  183.2 3.4 %all-to-all-done.5.block_ref = s16[4,80,512]{2,1,0:T(8,128)(2,1)S(1)} async-done(((s16[4,80,512]{2,1,0:T(8,128)(2,1)}), s16[4,80,512]{2,1,0:T(8,128)(2,1)S(1)}, u32[]{:S(2)}, u32[]{:S(2)}) %all-to-all-start.5) | async-done | bytes 327712 | tf_op jit(solution)/shard_map/all_to_all | solution.py:272
  186.6 0.7 shard_map.121
  187.4 5.0 %all-to-all-start.6 = ((f32[8,8,512]{2,1,0:T(8,128)}), f32[8,8,512]{2,1,0:T(8,128)}, u32[]{:S(2)}, u32[]{:S(2)}) async-start(f32[8,8,512]{2,1,0:T(8,128)} %shard_map.121), calls=%async_computation.6 | async-start | bytes 262144 | tf_op jit(solution)/shard_map/all_to_all | solution.py:274
  192.4 1.0 copy-done.5
  193.3 2.0 fusion.5
  195.3 1.1 fusion.3
  196.4 1.1 fusion.4
  197.5 6.5 %all-to-all-done.6 = f32[8,8,512]{2,1,0:T(8,128)} async-done(((f32[8,8,512]{2,1,0:T(8,128)}), f32[8,8,512]{2,1,0:T(8,128)}, u32[]{:S(2)}, u32[]{:S(2)}) %all-to-all-start.6) | async-done | bytes 131104 | tf_op jit(solution)/shard_map/all_to_all | solution.py:274
  203.9 1.5 reduce_sum.9
  (47 shorter events, 1.4 us)
Async XLA Ops:
  0.6 16.2 %copy-start.7 = (s32[128,448]{0,1:T(8,128)S(1)}, s32[128,448]{0,1:T(8,128)}, u32[]{:S(2)}) copy-start(s32[128,448]{0,1:T(8,128)} %param.14) | copy-start | bytes 688132
  0.6 16.4 %copy-start.8 = (s32[112,512]{1,0:T(8,128)S(1)}, s32[112,512]{1,0:T(8,128)}, u32[]{:S(2)}) copy-start(s32[112,512]{1,0:T(8,128)} %param.15) | copy-start | bytes 688132
  2.1 24.5 %all-to-all-start = ((bf16[8,2,8,512]{3,2,1,0:T(8,128)(2,1)}), bf16[8,2,8,512]{3,2,1,0:T(8,128)(2,1)S(1)}, u32[]{:S(2)}, u32[]{:S(2)}) async-start(bf16[8,2,8,512]{3,2,1,0:T(8,128)(2,1)} %broadcast_in_dim.20), calls=%async_computation | async-start | bytes 262144 | tf_op jit(solution)/shard_map/all_to_all | solution.py:224
  14.6 2.7 %copy-start.6 = (s32[128,448]{0,1:T(8,128)S(1)}, s32[128,448]{0,1:T(8,128)}, u32[]{:S(2)}) copy-start(s32[128,448]{0,1:T(8,128)} %param.13) | copy-start | bytes 688132
  17.1 1.0 copy-start.11
  18.1 1.7 copy-start.12
  19.8 1.6 copy-start.13
  38.5 3.8 %collective-permute-start = (bf16[2,256,512]{2,1,0:T(8,128)(2,1)S(1)}, bf16[2,256,512]{2,1,0:T(8,128)(2,1)S(1)}, u32[]{:S(2)}, u32[]{:S(2)}) collective-permute-start(bf16[2,256,512]{2,1,0:T(8,128)(2,1)S(1)} %bitcast.65), channel_id=1, source_target_pairs={{0,1},{1,0},{2,3},{3,2},{4,5},{5,4},{6,7},{7,6},{8,9},{9,8},{10,11... | collective-permute-start | bytes 1572872 | tf_op jit(solution)/shard_map/ppermute | solution.py:231
  66.5 32.9 %collective-permute-start.1 = (s16[352,256]{1,0:T(8,128)(2,1)S(1)}, s16[352,256]{1,0:T(8,128)(2,1)S(1)}, u32[]{:S(2)}, u32[]{:S(2)}) collective-permute-start(s16[352,256]{1,0:T(8,128)(2,1)S(1)} %get-tuple-element.22), channel_id=1, source_target_pairs={{0,256},{1,769},{256,0},{257,513},{512,768},{513,257},{768,512},{7... | collective-permute-start | bytes 540680 | tf_op jit(solution)/shard_map/ppermute | solution.py:38
  99.5 27.6 %collective-permute-start.2 = (s16[352,256]{1,0:T(8,128)(2,1)S(1)}, s16[352,256]{1,0:T(8,128)(2,1)S(1)}, u32[]{:S(2)}, u32[]{:S(2)}) collective-permute-start(s16[352,256]{1,0:T(8,128)(2,1)S(1)} %get-tuple-element.24), channel_id=1, source_target_pairs={{0,768},{1,257},{256,512},{257,1},{512,256},{513,769},{768,0},{769... | collective-permute-start | bytes 540680 | tf_op jit(solution)/shard_map/ppermute | solution.py:38
  128.1 26.1 %all-to-all-start.3 = ((bf16[4,336,256]{2,1,0:T(8,128)(2,1)}), bf16[4,336,256]{2,1,0:T(8,128)(2,1)S(1)}, u32[]{:S(2)}, u32[]{:S(2)}) async-start(bf16[4,336,256]{2,1,0:T(8,128)(2,1)} %shard_map.116), calls=%async_computation.3 | async-start | bytes 1376256 | tf_op jit(solution)/shard_map/all_to_all | solution.py:256
  131.5 21.6 %collective-permute-start.3 = (bf16[336,256]{1,0:T(8,128)(2,1)S(1)}, bf16[336,256]{1,0:T(8,128)(2,1)S(1)}, u32[]{:S(2)}, u32[]{:S(2)}) collective-permute-start(bf16[336,256]{1,0:T(8,128)(2,1)S(1)} %shard_map.115.block_ref), channel_id=1, source_target_pairs={{0,256},{1,769},{256,0},{257,513},{512,768},{513,257},{768,512},{7... | collective-permute-start | bytes 516104 | tf_op jit(solution)/shard_map/ppermute | solution.py:38
  154.1 13.4 %all-to-all-start.4 = ((bf16[4,336,256]{2,1,0:T(8,128)(2,1)}), bf16[4,336,256]{2,1,0:T(8,128)(2,1)S(1)}, u32[]{:S(2)}, u32[]{:S(2)}) async-start(bf16[4,336,256]{2,1,0:T(8,128)(2,1)} %shard_map.118), calls=%async_computation.4 | async-start | bytes 1376256 | tf_op jit(solution)/shard_map/all_to_all | solution.py:258
  159.0 0.8 copy-start
  167.5 1.0 copy-start.1
  169.0 3.8 %collective-permute-start.4 = (f32[256,512]{1,0:T(8,128)S(1)}, f32[256,512]{1,0:T(8,128)S(1)}, u32[]{:S(2)}, u32[]{:S(2)}) collective-permute-start(f32[256,512]{1,0:T(8,128)S(1)} %get-tuple-element.26), channel_id=1, source_target_pairs={{0,1},{1,0},{2,3},{3,2},{4,5},{5,4},{6,7},{7,6},{8,9},{9,8},{10,11... | collective-permute-start | bytes 1572872 | tf_op jit(solution)/shard_map/ppermute | solution.py:269
  171.9 8.5 %copy-start.3 = (bf16[2,256,512]{2,1,0:T(8,128)(2,1)}, bf16[2,256,512]{2,1,0:T(8,128)(2,1)S(1)}, u32[]{:S(2)}) copy-start(bf16[2,256,512]{2,1,0:T(8,128)(2,1)S(1)} %get-tuple-element.58) | copy-start | bytes 1572868
  173.7 12.9 %all-to-all-start.5 = ((s16[4,80,512]{2,1,0:T(8,128)(2,1)}), s16[4,80,512]{2,1,0:T(8,128)(2,1)S(1)}, u32[]{:S(2)}, u32[]{:S(2)}) async-start(s16[4,80,512]{2,1,0:T(8,128)(2,1)} %shard_map.120), calls=%async_computation.5 | async-start | bytes 655360 | tf_op jit(solution)/shard_map/all_to_all | solution.py:272
  181.6 1.3 copy-start.4
  187.4 5.0 %copy-start.2 = (f32[512,448]{0,1:T(8,128)S(1)}, f32[512,448]{0,1:T(8,128)}, u32[]{:S(2)}) copy-start(f32[512,448]{0,1:T(8,128)} %fusion.36) | copy-start | bytes 2752516
  187.4 16.6 %all-to-all-start.6 = ((f32[8,8,512]{2,1,0:T(8,128)}), f32[8,8,512]{2,1,0:T(8,128)}, u32[]{:S(2)}, u32[]{:S(2)}) async-start(f32[8,8,512]{2,1,0:T(8,128)} %shard_map.121), calls=%async_computation.6 | async-start | bytes 262144 | tf_op jit(solution)/shard_map/all_to_all | solution.py:274
  192.3 1.0 copy-start.5
  192.3 3.0 %copy-start.9 = (pred[448,512]{1,0:T(32,128)(4,1)S(1)}, pred[448,512]{1,0:T(32,128)(4,1)}, u32[]{:S(2)}) copy-start(pred[448,512]{1,0:T(32,128)(4,1)} %get-tuple-element.70) | copy-start | bytes 688132
  195.3 1.1 copy-start.10

commit v8 on v6

--- a/solution.py
+++ b/solution.py
@@ -11,20 +11,21 @@
 keep_sets = ((0, 1, 2), (0, 3, 4), (1, 3, 5), (2, 4, 5))
 
 
-def keep_planes(pattern):
+def keep_planes(pattern, axis):
     planes = []
     for members in keep_sets:
         kept = pattern == members[0]
         for member in members[1:]:
             kept = kept | (pattern == member)
-        planes.append(kept.astype(bf16))
-    return planes
-
-
-def spread_matrix(groups):
-    row = lax.broadcasted_iota(jnp.int32, (4 * groups, 4 * groups), 0)
-    col = lax.broadcasted_iota(jnp.int32, (4 * groups, 4 * groups), 1)
-    return ((row % groups) * 4 + row // groups == col).astype(bf16)
+        planes.append(jnp.where(kept, 1.0, 0.0).astype(bf16))
+    return jnp.concatenate(planes, axis=axis)
+
+
+def spread_matrix(size, axis):
+    place = lax.broadcasted_iota(jnp.int32, (size, size), axis)
+    source = lax.broadcasted_iota(jnp.int32, (size, size), 1 - axis)
+    moved = (place >> 2) + (place & 3) * (size // 4) == source
+    return jnp.where(moved, 1.0, 0.0).astype(bf16)
 
 
 def dot(a, b, dims):
@@ -68,6 +69,19 @@
         wide(block[i * units : (i + 1) * units, :]) * jnp.exp2(powers[i : i + 1, :])
         for i in range(3)
     ]
+
+
+def mask_kernel(*refs):
+    patterns, weights, kept, masks = refs[:3], refs[3:6], refs[6:9], refs[9:]
+    units, width = weights[0].shape
+    across, down = spread_matrix(width, 1), spread_matrix(units, 0)
+    for i in range(3):
+        if i < 2:
+            mask = dot(keep_planes(patterns[i][...], 1), across, ((1,), (0,)))
+        else:
+            mask = dot(down, keep_planes(patterns[i][...], 0), ((1,), (0,)))
+        masks[i][...] = mask.astype(bf16)
+        kept[i][...] = jnp.where(mask > 0.5, weights[i][...].astype(f32), 0.0).astype(bf16)
 
 
 def spread_kernel(block_ref, out_ref):
@@ -150,12 +164,9 @@
     )
 
 
-def first_back_kernel(block_ref, gate_ref, up_ref, out_ref):
-    out_ref[...] = back_product(block_ref, gate_ref, up_ref)
-
-
-def second_back_kernel(flag_ref, first_ref, block_ref, gate_ref, up_ref, stays_ref, leaves_ref):
-    first, second = first_ref[...], back_product(block_ref, gate_ref, up_ref)
+def back_kernel(flag_ref, first_ref, second_ref, gate_ref, up_ref, stays_ref, leaves_ref):
+    first = back_product(first_ref, gate_ref, up_ref)
+    second = back_product(second_ref, gate_ref, up_ref)
     first_stays = flag_ref[0] == 1
     stays_ref[...] = jnp.where(first_stays, first, second)
     leaves_ref[...] = jnp.where(first_stays, second, first)
@@ -181,6 +192,13 @@
     count, each = out_ref.shape[0], out_ref.shape[1]
     for c in range(count):
         out_ref[c] = total[c * each : (c + 1) * each]
+
+
+def last_sum_kernel(block_ref, out_ref):
+    total = block_ref[0]
+    for c in range(1, block_ref.shape[0]):
+        total = total + block_ref[c]
+    out_ref[...] = total.astype(bf16)
 
 
 def call(kernel, outs, *args, scalars=0):
@@ -202,15 +220,12 @@
     half = rows * sizes["zlo"] * sizes["x"]
     ny = sizes["y"]
     quarter = hidden_units // ny
-    spread_width = spread_matrix(width // 4)
-    spread_units = spread_matrix(hidden_units // 4)
-    gate_keep = dot(jnp.concatenate(keep_planes(gate_pattern.T), axis=1), spread_width, ((1,), (0,))) > 0.5
-    up_keep = dot(jnp.concatenate(keep_planes(up_pattern.T), axis=1), spread_width, ((1,), (0,))) > 0.5
-    down_keep = dot(spread_units, jnp.concatenate(keep_planes(down_pattern), axis=0), ((0,), (0,))) > 0.5
-    zero = jnp.zeros((), bf16)
-    gate_eff = jnp.where(gate_keep, gate_weight.T, zero)
-    up_eff = jnp.where(up_keep, up_weight.T, zero)
-    down_eff = jnp.where(down_keep, down_weight, zero)
+    gate_eff, up_eff, down_eff, gate_mask, up_mask, down_mask = call(
+        mask_kernel,
+        [((hidden_units, width), bf16)] * 6,
+        gate_pattern.T, up_pattern.T, down_pattern,
+        gate_weight.T, up_weight.T, down_weight,
+    )
 
     swap = [(0, 1), (1, 0)]
     nx, nzlo = sizes["x"], sizes["zlo"]
@@ -252,13 +267,10 @@
     (to_y,) = call(spread_kernel, [spread], theirs)
     second = lax.all_to_all(to_y, "y", 0, 0)
 
-    (back_first,) = call(
-        first_back_kernel, [((half, width), f32)], first, gate_eff, up_eff
-    )
     stays, leaves = call(
-        second_back_kernel,
+        back_kernel,
         [((half, width), f32)] * 2,
-        flag, back_first, second, gate_eff, up_eff,
+        flag, first, second, gate_eff, up_eff,
         scalars=1,
     )
     got = lax.ppermute(leaves, "core", swap)
@@ -266,7 +278,8 @@
     back, first, second = lax.optimization_barrier((back, first, second))
     back = lax.all_to_all(back, "x", 0, 0)
     (back,) = call(x_sum_kernel, [((nzlo, rows, width), f32)], back)
-    back = lax.all_to_all(back, "zlo", 0, 0).sum(axis=0)
+    back = lax.all_to_all(back, "zlo", 0, 0)
+    (back,) = call(last_sum_kernel, [((rows, width), bf16)], back)
 
     def units(block):
         block = block.reshape(ny, 3, quarter, half)
@@ -281,10 +294,10 @@
             second[member], sent_side[side], ((1,), (0,))
         )
 
-    grad_gate = jnp.where(gate_keep, weight_grad(1, 0), 0.0).astype(bf16)
-    grad_up = jnp.where(up_keep, weight_grad(2, 0), 0.0).astype(bf16)
-    grad_down = jnp.where(down_keep, weight_grad(0, 1), 0.0).astype(bf16)
-    return (back.astype(bf16), grad_gate.T, grad_up.T, grad_down)
+    grad_gate = jnp.where(gate_mask > 0.5, weight_grad(1, 0), 0.0).astype(bf16)
+    grad_up = jnp.where(up_mask > 0.5, weight_grad(2, 0), 0.0).astype(bf16)
+    grad_down = jnp.where(down_mask > 0.5, weight_grad(0, 1), 0.0).astype(bf16)
+    return (back, grad_gate.T, grad_up.T, grad_down)
 
 
 def solution(mesh):

time: 205 us -> 201 us (0.980)
  waiting for transfers between devices: 95.2 us -> 68.7 us
  blocking collectives: 11.8 us -> 26.4 us
  starting transfers between devices: 65.1 us -> 76.9 us
  matrix products: 11.7 us -> 4.92 us
  local copies, waits for them, and re-layouts: 6.1 us -> 11.3 us
  other arithmetic: 4.33 us -> 1.82 us
    ppermute x3, waiting for transfers between devices: 61.5 us -> 42.2 us  [zhi_exchange(): return lax.ppermute(block, ('zhi', 'core'), pairs)]
    ppermute x3, starting transfers between devices: 22.2 us -> 36.8 us  [zhi_exchange(): return lax.ppermute(block, ('zhi', 'core'), pairs)]
    all_to_all x0 -> x1, blocking collectives: none -> 14.6 us  [body(): second = lax.all_to_all(to_y, 'y', 0, 0)]
    all_to_all x2 -> x1, starting transfers between devices: 11.5 us -> 3.37 us  [body(): back = lax.all_to_all(back, 'zlo', 0, 0)]
    dot_general x9 -> x6, matrix products: 11.7 us -> 4.92 us  [dot(): return lax.dot_general(a, b, (dims, ((), ())), preferred_element_type=f32)]
    all_to_all x2 -> x1, waiting for transfers between devices: 14.1 us -> 7.47 us  [body(): back = lax.all_to_all(back, 'zlo', 0, 0)]
    unnamed x28 -> x44, local copies, waits for them, and re-layouts: 5.3 us -> 10.5 us
    all_to_all x1, starting transfers between devices: 4.54 us -> 9.11 us  [body(): back = lax.all_to_all(back, 'x', 0, 0)]
  transfers between devices with their start and end apart: 12 -> 11, of which waited for: 10 -> 9; matrix products, arithmetic and copies ran while one was open for 7% -> 3% of each run, Pallas kernels for 1% -> 1%
where the time goes in v8:
time: 201 us; the launch traced here: 200 us
  starting transfers between devices  76.9 us (38%)
  waiting for transfers between devices  68.7 us (34%)
  blocking collectives  26.4 us (13%)
  local copies, waits for them, and re-layouts  11.3 us (6%)
  Pallas kernels  8.95 us (4%)
  matrix products  4.92 us (2%)
    ppermute x3, waiting for transfers between devices, zhi_exchange(): return lax.ppermute(block, ('zhi', 'core'), pairs)  42.2 us
    ppermute x3, starting transfers between devices, zhi_exchange(): return lax.ppermute(block, ('zhi', 'core'), pairs)  36.8 us
    all_to_all x1, blocking collectives, body(): second = lax.all_to_all(to_y, 'y', 0, 0)  14.6 us
    all_to_all x1, starting transfers between devices, body(): both = lax.all_to_all(both, 'zlo', 0, 0)  12.5 us
    all_to_all x1, blocking collectives, body(): both = lax.all_to_all(both, 'x', 0, 0)  11.8 us
    unnamed x44, local copies, waits for them, and re-layouts  10.5 us
    all_to_all x1, waiting for transfers between devices, body(): sent = lax.all_to_all(sent, 'y', 0, 0)  9.55 us
    all_to_all x1, starting transfers between devices, body(): back = lax.all_to_all(back, 'x', 0, 0)  9.11 us
  transfers between devices with their start and end apart: 11, of which 9 were waited for; matrix products, arithmetic and copies ran while one was open for 3% of the time, Pallas kernels for 1%

profile of v8, /device:TPU:6, one launch (start us, length us, event | category | flops | bytes accessed | tf_op | source)
XLA Modules:
  0.0 199.8 jit_solution(17399775219714594745)
XLA Ops:
  0.6 0.8 pad_maximum_fusion
  1.4 0.7 broadcast_in_dim.12
  2.1 12.5 %all-to-all-start = ((bf16[8,2,8,512]{3,2,1,0:T(8,128)(2,1)}), bf16[8,2,8,512]{3,2,1,0:T(8,128)(2,1)S(1)}, u32[]{:S(2)}, u32[]{:S(2)}) async-start(bf16[8,2,8,512]{3,2,1,0:T(8,128)(2,1)} %broadcast_in_dim.12), calls=%async_computation | async-start | bytes 262144 | tf_op jit(solution)/shard_map/all_to_all | solution.py:234
  14.6 1.0 copy-done.6
  15.6 1.0 copy-done.7
  16.6 1.0 copy-done.8
  17.6 0.9 copy-done.10
  18.6 0.9 copy-done.11
  19.5 1.4 shard_map.111
  20.9 0.8 copy-done
  21.7 0.8 copy-done.2
  22.5 0.8 copy-done.4
  23.3 3.3 %all-to-all-done.block_ref = bf16[8,2,8,512]{3,2,1,0:T(8,128)(2,1)S(1)} async-done(((bf16[8,2,8,512]{3,2,1,0:T(8,128)(2,1)}), bf16[8,2,8,512]{3,2,1,0:T(8,128)(2,1)S(1)}, u32[]{:S(2)}, u32[]{:S(2)}) %all-to-all-start) | async-done | bytes 131104 | tf_op jit(solution)/shard_map/all_to_all | solution.py:234
  26.6 11.8 %all_to_all.40 = bf16[4,8,2,8,512]{4,3,2,1,0:T(8,128)(2,1)S(1)} all-to-all(bf16[4,8,2,8,512]{4,3,2,1,0:T(8,128)(2,1)S(1)} %shard_map.112), channel_id=1, replica_groups=mesh['zhi'=4,'y'=4,'zlo'=8,'x'=4,'core'=2] {'x'}, dimensions={0} | all-to-all | bytes 1048576 | tf_op jit(solution)/shard_map/all_to_all | solution.py:239
  38.4 2.1 %collective-permute-start = (bf16[2,256,512]{2,1,0:T(8,128)(2,1)S(1)}, bf16[2,256,512]{2,1,0:T(8,128)(2,1)S(1)}, u32[]{:S(2)}, u32[]{:S(2)}) collective-permute-start(bf16[2,256,512]{2,1,0:T(8,128)(2,1)S(1)} %bitcast.49), channel_id=1, source_target_pairs={{0,1},{1,0},{2,3},{3,2},{4,5},{5,4},{6,7},{7,6},{8,9},{9,8},{10,11... | collective-permute-start | bytes 1572872 | tf_op jit(solution)/shard_map/ppermute | solution.py:241
  40.5 1.9 collective-permute-done.other_ref
  42.4 1.5 shard_map.114
  43.9 3.5 %all-to-all-start.2 = ((s16[4,352,256]{2,1,0:T(8,128)(2,1)}), s16[4,352,256]{2,1,0:T(8,128)(2,1)S(1)}, u32[]{:S(2)}, u32[]{:S(2)}) async-start(s16[4,352,256]{2,1,0:T(8,128)(2,1)} %shard_map.114), calls=%async_computation.2 | async-start | bytes 1441792 | tf_op jit(solution)/shard_map/all_to_all | solution.py:254
  47.4 1.0 copy-done.18
  48.4 1.5 shard_map.113
  50.0 9.6 %all-to-all-done.2.block_ref = s16[4,352,256]{2,1,0:T(8,128)(2,1)S(1)} async-done(((s16[4,352,256]{2,1,0:T(8,128)(2,1)}), s16[4,352,256]{2,1,0:T(8,128)(2,1)S(1)}, u32[]{:S(2)}, u32[]{:S(2)}) %all-to-all-start.2) | async-done | bytes 720928 | tf_op jit(solution)/shard_map/all_to_all | solution.py:254
  59.8 3.5 %all-to-all-start.3 = ((s16[4,352,256]{2,1,0:T(8,128)(2,1)}), s16[4,352,256]{2,1,0:T(8,128)(2,1)S(1)}, u32[]{:S(2)}, u32[]{:S(2)}) async-start(s16[4,352,256]{2,1,0:T(8,128)(2,1)} %shard_map.113), calls=%async_computation.3 | async-start | bytes 1441792 | tf_op jit(solution)/shard_map/all_to_all | solution.py:258
  63.3 15.2 %collective-permute-start.1 = (s16[352,256]{1,0:T(8,128)(2,1)S(1)}, s16[352,256]{1,0:T(8,128)(2,1)S(1)}, u32[]{:S(2)}, u32[]{:S(2)}) collective-permute-start(s16[352,256]{1,0:T(8,128)(2,1)S(1)} %shard_map.115), channel_id=1, source_target_pairs={{0,256},{1,769},{256,0},{257,513},{512,768},{513,257},{768,512},{7... | collective-permute-start | bytes 540680 | tf_op jit(solution)/shard_map/ppermute | solution.py:39
  78.5 16.1 %collective-permute-done.1.got_ref = s16[352,256]{1,0:T(8,128)(2,1)S(1)} collective-permute-done((s16[352,256]{1,0:T(8,128)(2,1)S(1)}, s16[352,256]{1,0:T(8,128)(2,1)S(1)}, u32[]{:S(2)}, u32[]{:S(2)}) %collective-permute-start.1) | collective-permute-done | bytes 180256 | tf_op jit(solution)/shard_map/ppermute | solution.py:39
  94.9 1.9 collective-permute-start.2
  96.8 18.8 %collective-permute-done.2.got_ref = s16[352,256]{1,0:T(8,128)(2,1)S(1)} collective-permute-done((s16[352,256]{1,0:T(8,128)(2,1)S(1)}, s16[352,256]{1,0:T(8,128)(2,1)S(1)}, u32[]{:S(2)}, u32[]{:S(2)}) %collective-permute-start.2) | collective-permute-done | bytes 180256 | tf_op jit(solution)/shard_map/ppermute | solution.py:39
  115.6 1.0 shard_map.117
  116.6 4.1 %all-to-all-start.4 = ((bf16[4,336,256]{2,1,0:T(8,128)(2,1)}), bf16[4,336,256]{2,1,0:T(8,128)(2,1)S(1)}, u32[]{:S(2)}, u32[]{:S(2)}) async-start(bf16[4,336,256]{2,1,0:T(8,128)(2,1)} %get-tuple-element.36), calls=%async_computation.4 | async-start | bytes 1376256 | tf_op jit(solution)/shard_map/all_to_all | solution.py:266
  120.6 19.7 %collective-permute-start.3 = (bf16[336,256]{1,0:T(8,128)(2,1)S(1)}, bf16[336,256]{1,0:T(8,128)(2,1)S(1)}, u32[]{:S(2)}, u32[]{:S(2)}) collective-permute-start(bf16[336,256]{1,0:T(8,128)(2,1)S(1)} %get-tuple-element.37), channel_id=1, source_target_pairs={{0,256},{1,769},{256,0},{257,513},{512,768},{513,257},{768,512},{7... | collective-permute-start | bytes 516104 | tf_op jit(solution)/shard_map/ppermute | solution.py:39
  140.3 7.4 %collective-permute-done.3.block_ref = bf16[336,256]{1,0:T(8,128)(2,1)S(1)} collective-permute-done((bf16[336,256]{1,0:T(8,128)(2,1)S(1)}, bf16[336,256]{1,0:T(8,128)(2,1)S(1)}, u32[]{:S(2)}, u32[]{:S(2)}) %collective-permute-start.3) | collective-permute-done | bytes 172064 | tf_op jit(solution)/shard_map/ppermute | solution.py:39
  147.8 14.6 %all_to_all.41.second_ref = bf16[4,336,256]{2,1,0:T(8,128)(2,1)S(1)} all-to-all(bf16[4,336,256]{2,1,0:T(8,128)(2,1)S(1)} %shard_map.118), channel_id=1, replica_groups=mesh['zhi'=4,'y'=4,'zlo'=8,'x'=4,'core'=2] {'y'}, dimensions={0} | all-to-all | bytes 1376256 | tf_op jit(solution)/shard_map/all_to_all | solution.py:268
  162.4 0.7 shard_map.119
  163.1 1.9 collective-permute-start.4
  165.0 1.1 broadcast_select_fusion.1
  166.1 0.8 collective-permute-done.4.got_ref
  166.9 0.8 shard_map.120
  167.8 9.1 %all-to-all-start.6 = ((s16[4,80,512]{2,1,0:T(8,128)(2,1)}), s16[4,80,512]{2,1,0:T(8,128)(2,1)S(1)}, u32[]{:S(2)}, u32[]{:S(2)}) async-start(s16[4,80,512]{2,1,0:T(8,128)(2,1)} %shard_map.120), calls=%async_computation.6 | async-start | bytes 655360 | tf_op jit(solution)/shard_map/all_to_all | solution.py:279
  176.9 1.0 copy-done.21
  177.9 1.2 fusion.9
  179.7 3.5 %all-to-all-done.6.block_ref = s16[4,80,512]{2,1,0:T(8,128)(2,1)S(1)} async-done(((s16[4,80,512]{2,1,0:T(8,128)(2,1)}), s16[4,80,512]{2,1,0:T(8,128)(2,1)S(1)}, u32[]{:S(2)}, u32[]{:S(2)}) %all-to-all-start.6) | async-done | bytes 327712 | tf_op jit(solution)/shard_map/all_to_all | solution.py:279
  183.2 0.7 shard_map.121
  183.9 3.4 %all-to-all-start.7 = ((f32[8,8,512]{2,1,0:T(8,128)}), f32[8,8,512]{2,1,0:T(8,128)S(1)}, u32[]{:S(2)}, u32[]{:S(2)}) async-start(f32[8,8,512]{2,1,0:T(8,128)} %shard_map.121), calls=%async_computation.7 | async-start | bytes 262144 | tf_op jit(solution)/shard_map/all_to_all | solution.py:281
  187.4 1.1 copy-done.19
  188.6 1.1 fusion.6
  189.6 1.1 fusion.5
  190.7 1.1 fusion.7
  191.8 7.5 %all-to-all-done.7.block_ref = f32[8,8,512]{2,1,0:T(8,128)S(1)} async-done(((f32[8,8,512]{2,1,0:T(8,128)}), f32[8,8,512]{2,1,0:T(8,128)S(1)}, u32[]{:S(2)}, u32[]{:S(2)}) %all-to-all-start.7) | async-done | bytes 131104 | tf_op jit(solution)/shard_map/all_to_all | solution.py:281
  199.2 0.6 shard_map.122
  (44 shorter events, 1.5 us)
Async XLA Ops:
  0.6 14.0 %copy-start.9 = (s32[128,448]{0,1:T(8,128)S(1)}, s32[128,448]{0,1:T(8,128)}, u32[]{:S(2)}) copy-start(s32[128,448]{0,1:T(8,128)} %param.13) | copy-start | bytes 688132
  2.1 24.5 %all-to-all-start = ((bf16[8,2,8,512]{3,2,1,0:T(8,128)(2,1)}), bf16[8,2,8,512]{3,2,1,0:T(8,128)(2,1)S(1)}, u32[]{:S(2)}, u32[]{:S(2)}) async-start(bf16[8,2,8,512]{3,2,1,0:T(8,128)(2,1)} %broadcast_in_dim.12), calls=%async_computation | async-start | bytes 262144 | tf_op jit(solution)/shard_map/all_to_all | solution.py:234
  14.6 1.0 copy-start.6
  15.6 1.0 copy-start.7
  16.6 1.0 copy-start.8
  17.6 0.9 copy-start.10
  18.6 0.9 copy-start.11
  20.9 0.8 copy-start
  21.7 0.8 copy-start.2
  22.5 0.8 copy-start.4
  23.3 3.3 %copy-start.16 = (bf16[448,512]{1,0:T(8,128)(2,1)}, bf16[448,512]{1,0:T(8,128)(2,1)S(1)}, u32[]{:S(2)}) copy-start(bf16[448,512]{1,0:T(8,128)(2,1)S(1)} %get-tuple-element.30.down_ref) | copy-start | bytes 1376260
  23.3 24.1 %copy-start.12 = (bf16[448,512]{1,0:T(8,128)(2,1)}, bf16[448,512]{1,0:T(8,128)(2,1)S(1)}, u32[]{:S(2)}) copy-start(bf16[448,512]{1,0:T(8,128)(2,1)S(1)} %get-tuple-element.28.gate_ref) | copy-start | bytes 1376260
  23.3 24.2 %copy-start.14 = (bf16[448,512]{1,0:T(8,128)(2,1)}, bf16[448,512]{1,0:T(8,128)(2,1)S(1)}, u32[]{:S(2)}) copy-start(bf16[448,512]{1,0:T(8,128)(2,1)S(1)} %get-tuple-element.29.up_ref) | copy-start | bytes 1376260
  38.4 4.0 %copy-start.17 = (bf16[448,512]{1,0:T(8,128)(2,1)S(1)}, bf16[448,512]{1,0:T(8,128)(2,1)}, u32[]{:S(2)}) copy-start(bf16[448,512]{1,0:T(8,128)(2,1)} %copy-done.16) | copy-start | bytes 1376260
  38.4 3.9 %collective-permute-start = (bf16[2,256,512]{2,1,0:T(8,128)(2,1)S(1)}, bf16[2,256,512]{2,1,0:T(8,128)(2,1)S(1)}, u32[]{:S(2)}, u32[]{:S(2)}) collective-permute-start(bf16[2,256,512]{2,1,0:T(8,128)(2,1)S(1)} %bitcast.49), channel_id=1, source_target_pairs={{0,1},{1,0},{2,3},{3,2},{4,5},{5,4},{6,7},{7,6},{8,9},{9,8},{10,11... | collective-permute-start | bytes 1572872 | tf_op jit(solution)/shard_map/ppermute | solution.py:241
  43.9 15.6 %all-to-all-start.2 = ((s16[4,352,256]{2,1,0:T(8,128)(2,1)}), s16[4,352,256]{2,1,0:T(8,128)(2,1)S(1)}, u32[]{:S(2)}, u32[]{:S(2)}) async-start(s16[4,352,256]{2,1,0:T(8,128)(2,1)} %shard_map.114), calls=%async_computation.2 | async-start | bytes 1441792 | tf_op jit(solution)/shard_map/all_to_all | solution.py:254
  47.4 1.0 copy-start.18
  59.8 34.8 %all-to-all-start.3 = ((s16[4,352,256]{2,1,0:T(8,128)(2,1)}), s16[4,352,256]{2,1,0:T(8,128)(2,1)S(1)}, u32[]{:S(2)}, u32[]{:S(2)}) async-start(s16[4,352,256]{2,1,0:T(8,128)(2,1)} %shard_map.113), calls=%async_computation.3 | async-start | bytes 1441792 | tf_op jit(solution)/shard_map/all_to_all | solution.py:258
  63.3 31.3 %collective-permute-start.1 = (s16[352,256]{1,0:T(8,128)(2,1)S(1)}, s16[352,256]{1,0:T(8,128)(2,1)S(1)}, u32[]{:S(2)}, u32[]{:S(2)}) collective-permute-start(s16[352,256]{1,0:T(8,128)(2,1)S(1)} %shard_map.115), channel_id=1, source_target_pairs={{0,256},{1,769},{256,0},{257,513},{512,768},{513,257},{768,512},{7... | collective-permute-start | bytes 540680 | tf_op jit(solution)/shard_map/ppermute | solution.py:39
  94.9 20.7 %collective-permute-start.2 = (s16[352,256]{1,0:T(8,128)(2,1)S(1)}, s16[352,256]{1,0:T(8,128)(2,1)S(1)}, u32[]{:S(2)}, u32[]{:S(2)}) collective-permute-start(s16[352,256]{1,0:T(8,128)(2,1)S(1)} %get-tuple-element.35), channel_id=1, source_target_pairs={{0,768},{1,257},{256,512},{257,1},{512,256},{513,769},{768,0},{769... | collective-permute-start | bytes 540680 | tf_op jit(solution)/shard_map/ppermute | solution.py:39
  116.6 31.2 %all-to-all-start.4 = ((bf16[4,336,256]{2,1,0:T(8,128)(2,1)}), bf16[4,336,256]{2,1,0:T(8,128)(2,1)S(1)}, u32[]{:S(2)}, u32[]{:S(2)}) async-start(bf16[4,336,256]{2,1,0:T(8,128)(2,1)} %get-tuple-element.36), calls=%async_computation.4 | async-start | bytes 1376256 | tf_op jit(solution)/shard_map/all_to_all | solution.py:266
  120.6 27.1 %collective-permute-start.3 = (bf16[336,256]{1,0:T(8,128)(2,1)S(1)}, bf16[336,256]{1,0:T(8,128)(2,1)S(1)}, u32[]{:S(2)}, u32[]{:S(2)}) collective-permute-start(bf16[336,256]{1,0:T(8,128)(2,1)S(1)} %get-tuple-element.37), channel_id=1, source_target_pairs={{0,256},{1,769},{256,0},{257,513},{512,768},{513,257},{768,512},{7... | collective-permute-start | bytes 516104 | tf_op jit(solution)/shard_map/ppermute | solution.py:39
  147.8 14.6 %copy-start.13 = (bf16[448,512]{1,0:T(8,128)(2,1)S(1)}, bf16[448,512]{1,0:T(8,128)(2,1)}, u32[]{:S(2)}) copy-start(bf16[448,512]{1,0:T(8,128)(2,1)} %copy-done.12) | copy-start | bytes 1376260
  147.8 14.6 %copy-start.15 = (bf16[448,512]{1,0:T(8,128)(2,1)S(1)}, bf16[448,512]{1,0:T(8,128)(2,1)}, u32[]{:S(2)}) copy-start(bf16[448,512]{1,0:T(8,128)(2,1)} %copy-done.14) | copy-start | bytes 1376260
  163.1 3.8 %collective-permute-start.4 = (f32[256,512]{1,0:T(8,128)S(1)}, f32[256,512]{1,0:T(8,128)S(1)}, u32[]{:S(2)}, u32[]{:S(2)}) collective-permute-start(f32[256,512]{1,0:T(8,128)S(1)} %get-tuple-element.39), channel_id=1, source_target_pairs={{0,1},{1,0},{2,3},{3,2},{4,5},{5,4},{6,7},{7,6},{8,9},{9,8},{10,11... | collective-permute-start | bytes 1572872 | tf_op jit(solution)/shard_map/ppermute | solution.py:276
  167.8 15.4 %all-to-all-start.6 = ((s16[4,80,512]{2,1,0:T(8,128)(2,1)}), s16[4,80,512]{2,1,0:T(8,128)(2,1)S(1)}, u32[]{:S(2)}, u32[]{:S(2)}) async-start(s16[4,80,512]{2,1,0:T(8,128)(2,1)} %shard_map.120), calls=%async_computation.6 | async-start | bytes 655360 | tf_op jit(solution)/shard_map/all_to_all | solution.py:279
  176.9 1.0 copy-start.21
  183.2 4.2 %copy-start.20 = (bf16[2,256,512]{2,1,0:T(8,128)(2,1)S(1)}, bf16[2,256,512]{2,1,0:T(8,128)(2,1)}, u32[]{:S(2)}) copy-start(bf16[2,256,512]{2,1,0:T(8,128)(2,1)} %get-tuple-element.46) | copy-start | bytes 1572868
  183.9 15.3 %all-to-all-start.7 = ((f32[8,8,512]{2,1,0:T(8,128)}), f32[8,8,512]{2,1,0:T(8,128)S(1)}, u32[]{:S(2)}, u32[]{:S(2)}) async-start(f32[8,8,512]{2,1,0:T(8,128)} %shard_map.121), calls=%async_computation.7 | async-start | bytes 262144 | tf_op jit(solution)/shard_map/all_to_all | solution.py:281
  187.3 1.2 copy-start.19
  187.3 1.3 copy-start.5
  188.6 1.1 copy-start.3
  189.6 1.1 copy-start.1

commit v9 on v8

--- a/solution.py
+++ b/solution.py
@@ -220,6 +220,17 @@
     half = rows * sizes["zlo"] * sizes["x"]
     ny = sizes["y"]
     quarter = hidden_units // ny
+    swap = [(0, 1), (1, 0)]
+    nx, nzlo = sizes["x"], sizes["zlo"]
+    both = jnp.stack([inputs, cotangent])
+    both = jnp.broadcast_to(both[None], (nzlo, *both.shape))
+    both = lax.all_to_all(both, "zlo", 0, 0)
+    both, gate_pattern, up_pattern, down_pattern = lax.optimization_barrier(
+        (both, gate_pattern, up_pattern, down_pattern)
+    )
+    (both,) = call(spread_kernel, [((nx, nzlo, 2, rows, width), bf16)], both)
+    both = lax.all_to_all(both, "x", 0, 0)
+
     gate_eff, up_eff, down_eff, gate_mask, up_mask, down_mask = call(
         mask_kernel,
         [((hidden_units, width), bf16)] * 6,
@@ -227,16 +238,9 @@
         gate_weight.T, up_weight.T, down_weight,
     )
 
-    swap = [(0, 1), (1, 0)]
-    nx, nzlo = sizes["x"], sizes["zlo"]
-    both = jnp.stack([inputs, cotangent])
-    both = jnp.broadcast_to(both[None], (nzlo, *both.shape))
-    both = lax.all_to_all(both, "zlo", 0, 0)
     both, gate_eff, up_eff, down_eff = lax.optimization_barrier(
         (both, gate_eff, up_eff, down_eff)
     )
-    (both,) = call(spread_kernel, [((nx, nzlo, 2, rows, width), bf16)], both)
-    both = lax.all_to_all(both, "x", 0, 0)
     own = both.transpose(2, 0, 1, 3, 4).reshape(2, half, width)
     other = lax.ppermute(own, "core", swap)
 

time: 201 us -> 194 us (0.965)
  blocking collectives: 26.4 us -> 37.9 us
  waiting for transfers between devices: 68.7 us -> 59.5 us
  starting transfers between devices: 76.9 us -> 70.3 us
  local copies, waits for them, and re-layouts: 11.3 us -> 7.28 us
    all_to_all x1, blocking collectives: 11.8 us -> 24.3 us  [body(): both = lax.all_to_all(both, 'zlo', 0, 0)]
    all_to_all x1, starting transfers between devices: 12.5 us -> 6.25 us  [body(): both = lax.all_to_all(both, 'x', 0, 0)]
    ppermute x3, waiting for transfers between devices: 42.2 us -> 36.7 us  [zhi_exchange(): return lax.ppermute(block, ('zhi', 'core'), pairs)]
    all_to_all x1, starting transfers between devices: 9.11 us -> 5.52 us  [body(): back = lax.all_to_all(back, 'x', 0, 0)]
    unnamed x44 -> x46, local copies, waits for them, and re-layouts: 10.5 us -> 7.13 us
    all_to_all x1, starting transfers between devices: 3.37 us -> 6.19 us  [body(): back = lax.all_to_all(back, 'zlo', 0, 0)]
    all_to_all x1, waiting for transfers between devices: 3.26 us -> 0.7 us  [body(): both = lax.all_to_all(both, 'x', 0, 0)]
  transfers between devices with their start and end apart: 11 -> 11, of which waited for: 9 -> 9; matrix products, arithmetic and copies ran while one was open for 3% -> 3% of each run, Pallas kernels for 1% -> 2%
where the time goes in v9:
time: 194 us; the launch traced here: 192 us
  starting transfers between devices  70.3 us (36%)
  waiting for transfers between devices  59.5 us (31%)
  blocking collectives  37.9 us (20%)
  Pallas kernels  9.81 us (5%)
  local copies, waits for them, and re-layouts  7.28 us (4%)
  matrix products  4.94 us (3%)
    ppermute x3, waiting for transfers between devices, zhi_exchange(): return lax.ppermute(block, ('zhi', 'core'), pairs)  36.7 us
    ppermute x3, starting transfers between devices, zhi_exchange(): return lax.ppermute(block, ('zhi', 'core'), pairs)  36.3 us
    all_to_all x1, blocking collectives, body(): both = lax.all_to_all(both, 'zlo', 0, 0)  24.3 us
    all_to_all x1, blocking collectives, body(): second = lax.all_to_all(to_y, 'y', 0, 0)  13.6 us
    pallas_call x12, Pallas kernels, call(): pl.pallas_call(kernel, in_specs=specs, out_shape=[jax.ShapeDtypeStruct(sh...  9.81 us
    all_to_all x1, waiting for transfers between devices, body(): sent = lax.all_to_all(sent, 'y', 0, 0)  9.55 us
    unnamed x46, local copies, waits for them, and re-layouts  7.13 us
    all_to_all x1, waiting for transfers between devices, body(): back = lax.all_to_all(back, 'zlo', 0, 0)  7.03 us
  transfers between devices with their start and end apart: 11, of which 9 were waited for; matrix products, arithmetic and copies ran while one was open for 3% of the time, Pallas kernels for 2%

profile of v9, /device:TPU:6, one launch (start us, length us, event | category | flops | bytes accessed | tf_op | source)
XLA Modules:
  0.0 192.4 jit_solution(172660105757055034)
XLA Ops:
  0.6 0.7 pad_maximum_fusion
  1.4 24.3 %all_to_all.40.block_ref = bf16[8,2,8,512]{3,2,1,0:T(8,128)(2,1)S(1)} all-to-all(bf16[8,2,8,512]{3,2,1,0:T(8,128)(2,1)S(1)} %broadcast_in_dim.12), channel_id=1, replica_groups=mesh['zhi'=4,'y'=4,'zlo'=8,'x'=4,'core'=2] {'zlo'}, dimensions={0} | all-to-all | bytes 262144 | tf_op jit(solution)/shard_map/all_to_all | solution.py:227
  25.6 0.8 shard_map.111
  26.5 6.3 %all-to-all-start.1 = ((bf16[4,8,2,8,512]{4,3,2,1,0:T(8,128)(2,1)}), bf16[4,8,2,8,512]{4,3,2,1,0:T(8,128)(2,1)S(1)}, u32[]{:S(2)}, u32[]{:S(2)}) async-start(bf16[4,8,2,8,512]{4,3,2,1,0:T(8,128)(2,1)} %shard_map.111), calls=%async_computation.1 | async-start | bytes 1048576 | tf_op jit(solution)/shard_map/all_to_all | solution.py:232
  32.8 1.4 shard_map.112
  34.2 0.8 copy-done
  35.0 0.8 copy-done.2
  35.7 0.8 copy-done.4
  36.5 0.8 copy-done.14
  37.3 0.8 copy-done.17
  38.0 0.7 all-to-all-done.1
  38.8 2.1 %collective-permute-start = (bf16[2,256,512]{2,1,0:T(8,128)(2,1)S(1)}, bf16[2,256,512]{2,1,0:T(8,128)(2,1)S(1)}, u32[]{:S(2)}, u32[]{:S(2)}) collective-permute-start(bf16[2,256,512]{2,1,0:T(8,128)(2,1)S(1)} %bitcast.49), channel_id=1, source_target_pairs={{0,1},{1,0},{2,3},{3,2},{4,5},{5,4},{6,7},{7,6},{8,9},{9,8},{10,11... | collective-permute-start | bytes 1572872 | tf_op jit(solution)/shard_map/ppermute | solution.py:245
  40.9 1.9 collective-permute-done.other_ref
  42.7 1.6 shard_map.114
  44.3 3.5 %all-to-all-start.2 = ((s16[4,352,256]{2,1,0:T(8,128)(2,1)}), s16[4,352,256]{2,1,0:T(8,128)(2,1)S(1)}, u32[]{:S(2)}, u32[]{:S(2)}) async-start(s16[4,352,256]{2,1,0:T(8,128)(2,1)} %shard_map.114), calls=%async_computation.2 | async-start | bytes 1441792 | tf_op jit(solution)/shard_map/all_to_all | solution.py:258
  47.8 1.0 copy-done.19
  48.8 1.5 shard_map.113
  50.4 9.5 %all-to-all-done.2.block_ref = s16[4,352,256]{2,1,0:T(8,128)(2,1)S(1)} async-done(((s16[4,352,256]{2,1,0:T(8,128)(2,1)}), s16[4,352,256]{2,1,0:T(8,128)(2,1)S(1)}, u32[]{:S(2)}, u32[]{:S(2)}) %all-to-all-start.2) | async-done | bytes 720928 | tf_op jit(solution)/shard_map/all_to_all | solution.py:258
  60.2 3.5 %all-to-all-start.3 = ((s16[4,352,256]{2,1,0:T(8,128)(2,1)}), s16[4,352,256]{2,1,0:T(8,128)(2,1)S(1)}, u32[]{:S(2)}, u32[]{:S(2)}) async-start(s16[4,352,256]{2,1,0:T(8,128)(2,1)} %shard_map.113), calls=%async_computation.3 | async-start | bytes 1441792 | tf_op jit(solution)/shard_map/all_to_all | solution.py:262
  63.7 15.1 %collective-permute-start.1 = (s16[352,256]{1,0:T(8,128)(2,1)S(1)}, s16[352,256]{1,0:T(8,128)(2,1)S(1)}, u32[]{:S(2)}, u32[]{:S(2)}) collective-permute-start(s16[352,256]{1,0:T(8,128)(2,1)S(1)} %shard_map.115), channel_id=1, source_target_pairs={{0,256},{1,769},{256,0},{257,513},{512,768},{513,257},{768,512},{7... | collective-permute-start | bytes 540680 | tf_op jit(solution)/shard_map/ppermute | solution.py:39
  78.8 17.1 %collective-permute-done.1.got_ref = s16[352,256]{1,0:T(8,128)(2,1)S(1)} collective-permute-done((s16[352,256]{1,0:T(8,128)(2,1)S(1)}, s16[352,256]{1,0:T(8,128)(2,1)S(1)}, u32[]{:S(2)}, u32[]{:S(2)}) %collective-permute-start.1) | collective-permute-done | bytes 180256 | tf_op jit(solution)/shard_map/ppermute | solution.py:39
  95.8 0.3 shard_map.116
  96.1 11.2 %collective-permute-start.2 = (s16[352,256]{1,0:T(8,128)(2,1)S(1)}, s16[352,256]{1,0:T(8,128)(2,1)S(1)}, u32[]{:S(2)}, u32[]{:S(2)}) collective-permute-start(s16[352,256]{1,0:T(8,128)(2,1)S(1)} %get-tuple-element.43), channel_id=1, source_target_pairs={{0,768},{1,257},{256,512},{257,1},{512,256},{513,769},{768,0},{769... | collective-permute-start | bytes 540680 | tf_op jit(solution)/shard_map/ppermute | solution.py:39
  107.3 8.7 %collective-permute-done.2.got_ref = s16[352,256]{1,0:T(8,128)(2,1)S(1)} collective-permute-done((s16[352,256]{1,0:T(8,128)(2,1)S(1)}, s16[352,256]{1,0:T(8,128)(2,1)S(1)}, u32[]{:S(2)}, u32[]{:S(2)}) %collective-permute-start.2) | collective-permute-done | bytes 180256 | tf_op jit(solution)/shard_map/ppermute | solution.py:39
  116.0 1.0 shard_map.117
  117.0 5.0 %all-to-all-start.4 = ((bf16[4,336,256]{2,1,0:T(8,128)(2,1)}), bf16[4,336,256]{2,1,0:T(8,128)(2,1)S(1)}, u32[]{:S(2)}, u32[]{:S(2)}) async-start(bf16[4,336,256]{2,1,0:T(8,128)(2,1)} %get-tuple-element.44), calls=%async_computation.4 | async-start | bytes 1376256 | tf_op jit(solution)/shard_map/all_to_all | solution.py:270
  122.0 10.0 %collective-permute-start.3 = (bf16[336,256]{1,0:T(8,128)(2,1)S(1)}, bf16[336,256]{1,0:T(8,128)(2,1)S(1)}, u32[]{:S(2)}, u32[]{:S(2)}) collective-permute-start(bf16[336,256]{1,0:T(8,128)(2,1)S(1)} %get-tuple-element.45), channel_id=1, source_target_pairs={{0,256},{1,769},{256,0},{257,513},{512,768},{513,257},{768,512},{7... | collective-permute-start | bytes 516104 | tf_op jit(solution)/shard_map/ppermute | solution.py:39
  132.0 11.0 %collective-permute-done.3.block_ref = bf16[336,256]{1,0:T(8,128)(2,1)S(1)} collective-permute-done((bf16[336,256]{1,0:T(8,128)(2,1)S(1)}, bf16[336,256]{1,0:T(8,128)(2,1)S(1)}, u32[]{:S(2)}, u32[]{:S(2)}) %collective-permute-start.3) | collective-permute-done | bytes 172064 | tf_op jit(solution)/shard_map/ppermute | solution.py:39
  143.1 13.6 %all_to_all.41.second_ref = bf16[4,336,256]{2,1,0:T(8,128)(2,1)S(1)} all-to-all(bf16[4,336,256]{2,1,0:T(8,128)(2,1)S(1)} %shard_map.118), channel_id=1, replica_groups=mesh['zhi'=4,'y'=4,'zlo'=8,'x'=4,'core'=2] {'y'}, dimensions={0} | all-to-all | bytes 1376256 | tf_op jit(solution)/shard_map/all_to_all | solution.py:272
  156.7 0.7 shard_map.119
  157.5 1.9 collective-permute-start.4
  159.4 1.1 broadcast_select_fusion.1
  160.5 0.8 collective-permute-done.4.got_ref
  161.3 0.8 shard_map.120
  162.1 5.5 %all-to-all-start.6 = ((s16[4,80,512]{2,1,0:T(8,128)(2,1)}), s16[4,80,512]{2,1,0:T(8,128)(2,1)S(1)}, u32[]{:S(2)}, u32[]{:S(2)}) async-start(s16[4,80,512]{2,1,0:T(8,128)(2,1)} %shard_map.120), calls=%async_computation.6 | async-start | bytes 655360 | tf_op jit(solution)/shard_map/all_to_all | solution.py:283
  167.7 1.0 copy-done.22
  168.7 1.2 fusion.9
  169.9 0.3 fusion.8
  170.2 0.3 fusion.10
  170.4 2.9 %all-to-all-done.6.block_ref = s16[4,80,512]{2,1,0:T(8,128)(2,1)S(1)} async-done(((s16[4,80,512]{2,1,0:T(8,128)(2,1)}), s16[4,80,512]{2,1,0:T(8,128)(2,1)S(1)}, u32[]{:S(2)}, u32[]{:S(2)}) %all-to-all-start.6) | async-done | bytes 327712 | tf_op jit(solution)/shard_map/all_to_all | solution.py:283
  173.3 0.7 shard_map.121
  174.1 6.2 %all-to-all-start.7 = ((f32[8,8,512]{2,1,0:T(8,128)}), f32[8,8,512]{2,1,0:T(8,128)S(1)}, u32[]{:S(2)}, u32[]{:S(2)}) async-start(f32[8,8,512]{2,1,0:T(8,128)} %shard_map.121), calls=%async_computation.7 | async-start | bytes 262144 | tf_op jit(solution)/shard_map/all_to_all | solution.py:285
  180.3 1.1 copy-done.20
  181.5 1.1 fusion.6
  182.6 1.1 fusion.5
  183.7 1.1 fusion.7
  184.7 7.0 %all-to-all-done.7.block_ref = f32[8,8,512]{2,1,0:T(8,128)S(1)} async-done(((f32[8,8,512]{2,1,0:T(8,128)}), f32[8,8,512]{2,1,0:T(8,128)S(1)}, u32[]{:S(2)}, u32[]{:S(2)}) %all-to-all-start.7) | async-done | bytes 131104 | tf_op jit(solution)/shard_map/all_to_all | solution.py:285
  191.8 0.6 shard_map.122
  (46 shorter events, 0.6 us)
Async XLA Ops:
  25.6 7.1 %copy-start.8 = (bf16[448,512]{1,0:T(8,128)(2,1)S(1)}, bf16[448,512]{1,0:T(8,128)(2,1)}, u32[]{:S(2)}) copy-start(bf16[448,512]{1,0:T(8,128)(2,1)} %refs_5_.1) | copy-start | bytes 1376260
  25.6 7.1 %copy-start.9 = (s32[128,448]{0,1:T(8,128)S(1)}, s32[128,448]{0,1:T(8,128)}, u32[]{:S(2)}) copy-start(s32[128,448]{0,1:T(8,128)} %param.13) | copy-start | bytes 688132
  25.6 7.1 %copy-start.10 = (s32[128,448]{0,1:T(8,128)S(1)}, s32[128,448]{0,1:T(8,128)}, u32[]{:S(2)}) copy-start(s32[128,448]{0,1:T(8,128)} %param.14) | copy-start | bytes 688132
  25.6 7.1 %copy-start.11 = (s32[112,512]{1,0:T(8,128)S(1)}, s32[112,512]{1,0:T(8,128)}, u32[]{:S(2)}) copy-start(s32[112,512]{1,0:T(8,128)} %refs_2_) | copy-start | bytes 688132
  26.5 6.3 %copy-start.6 = (bf16[512,448]{0,1:T(8,128)(2,1)S(1)}, bf16[512,448]{0,1:T(8,128)(2,1)}, u32[]{:S(2)}) copy-start(bf16[512,448]{0,1:T(8,128)(2,1)} %param.10) | copy-start | bytes 1376260
  26.5 6.3 %copy-start.7 = (bf16[512,448]{0,1:T(8,128)(2,1)S(1)}, bf16[512,448]{0,1:T(8,128)(2,1)}, u32[]{:S(2)}) copy-start(bf16[512,448]{0,1:T(8,128)(2,1)} %param.11) | copy-start | bytes 1376260
  26.5 12.3 %all-to-all-start.1 = ((bf16[4,8,2,8,512]{4,3,2,1,0:T(8,128)(2,1)}), bf16[4,8,2,8,512]{4,3,2,1,0:T(8,128)(2,1)S(1)}, u32[]{:S(2)}, u32[]{:S(2)}) async-start(bf16[4,8,2,8,512]{4,3,2,1,0:T(8,128)(2,1)} %shard_map.111), calls=%async_computation.1 | async-start | bytes 1048576 | tf_op jit(solution)/shard_map/all_to_all | solution.py:232
  34.2 0.8 copy-start
  35.0 0.8 copy-start.2
  35.7 0.8 copy-start.4
  36.5 0.8 copy-start.14
  37.3 0.8 copy-start.17
  38.0 9.7 %copy-start.12 = (bf16[448,512]{1,0:T(8,128)(2,1)}, bf16[448,512]{1,0:T(8,128)(2,1)S(1)}, u32[]{:S(2)}) copy-start(bf16[448,512]{1,0:T(8,128)(2,1)S(1)} %get-tuple-element.36.gate_ref) | copy-start | bytes 1376260
  38.7 4.0 %copy-start.15 = (bf16[448,512]{1,0:T(8,128)(2,1)S(1)}, bf16[448,512]{1,0:T(8,128)(2,1)}, u32[]{:S(2)}) copy-start(bf16[448,512]{1,0:T(8,128)(2,1)} %copy-done.14) | copy-start | bytes 1376260
  38.8 4.0 %copy-start.18 = (bf16[448,512]{1,0:T(8,128)(2,1)S(1)}, bf16[448,512]{1,0:T(8,128)(2,1)}, u32[]{:S(2)}) copy-start(bf16[448,512]{1,0:T(8,128)(2,1)} %copy-done.17) | copy-start | bytes 1376260
  38.8 3.9 %collective-permute-start = (bf16[2,256,512]{2,1,0:T(8,128)(2,1)S(1)}, bf16[2,256,512]{2,1,0:T(8,128)(2,1)S(1)}, u32[]{:S(2)}, u32[]{:S(2)}) collective-permute-start(bf16[2,256,512]{2,1,0:T(8,128)(2,1)S(1)} %bitcast.49), channel_id=1, source_target_pairs={{0,1},{1,0},{2,3},{3,2},{4,5},{5,4},{6,7},{7,6},{8,9},{9,8},{10,11... | collective-permute-start | bytes 1572872 | tf_op jit(solution)/shard_map/ppermute | solution.py:245
  44.3 15.6 %all-to-all-start.2 = ((s16[4,352,256]{2,1,0:T(8,128)(2,1)}), s16[4,352,256]{2,1,0:T(8,128)(2,1)S(1)}, u32[]{:S(2)}, u32[]{:S(2)}) async-start(s16[4,352,256]{2,1,0:T(8,128)(2,1)} %shard_map.114), calls=%async_computation.2 | async-start | bytes 1441792 | tf_op jit(solution)/shard_map/all_to_all | solution.py:258
  47.8 1.0 copy-start.19
  60.2 35.7 %all-to-all-start.3 = ((s16[4,352,256]{2,1,0:T(8,128)(2,1)}), s16[4,352,256]{2,1,0:T(8,128)(2,1)S(1)}, u32[]{:S(2)}, u32[]{:S(2)}) async-start(s16[4,352,256]{2,1,0:T(8,128)(2,1)} %shard_map.113), calls=%async_computation.3 | async-start | bytes 1441792 | tf_op jit(solution)/shard_map/all_to_all | solution.py:262
  63.7 32.2 %collective-permute-start.1 = (s16[352,256]{1,0:T(8,128)(2,1)S(1)}, s16[352,256]{1,0:T(8,128)(2,1)S(1)}, u32[]{:S(2)}, u32[]{:S(2)}) collective-permute-start(s16[352,256]{1,0:T(8,128)(2,1)S(1)} %shard_map.115), channel_id=1, source_target_pairs={{0,256},{1,769},{256,0},{257,513},{512,768},{513,257},{768,512},{7... | collective-permute-start | bytes 540680 | tf_op jit(solution)/shard_map/ppermute | solution.py:39
  96.1 19.9 %collective-permute-start.2 = (s16[352,256]{1,0:T(8,128)(2,1)S(1)}, s16[352,256]{1,0:T(8,128)(2,1)S(1)}, u32[]{:S(2)}, u32[]{:S(2)}) collective-permute-start(s16[352,256]{1,0:T(8,128)(2,1)S(1)} %get-tuple-element.43), channel_id=1, source_target_pairs={{0,768},{1,257},{256,512},{257,1},{512,256},{513,769},{768,0},{769... | collective-permute-start | bytes 540680 | tf_op jit(solution)/shard_map/ppermute | solution.py:39
  117.0 26.0 %all-to-all-start.4 = ((bf16[4,336,256]{2,1,0:T(8,128)(2,1)}), bf16[4,336,256]{2,1,0:T(8,128)(2,1)S(1)}, u32[]{:S(2)}, u32[]{:S(2)}) async-start(bf16[4,336,256]{2,1,0:T(8,128)(2,1)} %get-tuple-element.44), calls=%async_computation.4 | async-start | bytes 1376256 | tf_op jit(solution)/shard_map/all_to_all | solution.py:270
  122.0 21.0 %collective-permute-start.3 = (bf16[336,256]{1,0:T(8,128)(2,1)S(1)}, bf16[336,256]{1,0:T(8,128)(2,1)S(1)}, u32[]{:S(2)}, u32[]{:S(2)}) collective-permute-start(bf16[336,256]{1,0:T(8,128)(2,1)S(1)} %get-tuple-element.45), channel_id=1, source_target_pairs={{0,256},{1,769},{256,0},{257,513},{512,768},{513,257},{768,512},{7... | collective-permute-start | bytes 516104 | tf_op jit(solution)/shard_map/ppermute | solution.py:39
  143.1 13.7 %copy-start.13 = (bf16[448,512]{1,0:T(8,128)(2,1)S(1)}, bf16[448,512]{1,0:T(8,128)(2,1)}, u32[]{:S(2)}) copy-start(bf16[448,512]{1,0:T(8,128)(2,1)} %copy-done.12) | copy-start | bytes 1376260
  143.1 13.7 %copy-start.16 = (bf16[448,512]{1,0:T(8,128)(2,1)S(1)}, bf16[448,512]{1,0:T(8,128)(2,1)}, u32[]{:S(2)}) copy-start(bf16[448,512]{1,0:T(8,128)(2,1)} %copy-done.14) | copy-start | bytes 1376260
  157.5 3.8 %collective-permute-start.4 = (f32[256,512]{1,0:T(8,128)S(1)}, f32[256,512]{1,0:T(8,128)S(1)}, u32[]{:S(2)}, u32[]{:S(2)}) collective-permute-start(f32[256,512]{1,0:T(8,128)S(1)} %get-tuple-element.47), channel_id=1, source_target_pairs={{0,1},{1,0},{2,3},{3,2},{4,5},{5,4},{6,7},{7,6},{8,9},{9,8},{10,11... | collective-permute-start | bytes 1572872 | tf_op jit(solution)/shard_map/ppermute | solution.py:280
  162.1 11.2 %all-to-all-start.6 = ((s16[4,80,512]{2,1,0:T(8,128)(2,1)}), s16[4,80,512]{2,1,0:T(8,128)(2,1)S(1)}, u32[]{:S(2)}, u32[]{:S(2)}) async-start(s16[4,80,512]{2,1,0:T(8,128)(2,1)} %shard_map.120), calls=%async_computation.6 | async-start | bytes 655360 | tf_op jit(solution)/shard_map/all_to_all | solution.py:283
  167.7 1.0 copy-start.22
  173.3 7.0 %copy-start.21 = (bf16[2,256,512]{2,1,0:T(8,128)(2,1)S(1)}, bf16[2,256,512]{2,1,0:T(8,128)(2,1)}, u32[]{:S(2)}) copy-start(bf16[2,256,512]{2,1,0:T(8,128)(2,1)} %get-tuple-element.54) | copy-start | bytes 1572868
  174.1 17.7 %all-to-all-start.7 = ((f32[8,8,512]{2,1,0:T(8,128)}), f32[8,8,512]{2,1,0:T(8,128)S(1)}, u32[]{:S(2)}, u32[]{:S(2)}) async-start(f32[8,8,512]{2,1,0:T(8,128)} %shard_map.121), calls=%async_computation.7 | async-start | bytes 262144 | tf_op jit(solution)/shard_map/all_to_all | solution.py:285
  180.2 1.2 copy-start.20
  180.2 1.3 copy-start.5
  181.5 1.1 copy-start.3
  182.6 1.1 copy-start.1

commit v10 on v9

--- a/solution.py
+++ b/solution.py
@@ -201,7 +201,7 @@
     out_ref[...] = total.astype(bf16)
 
 
-def call(kernel, outs, *args, scalars=0):
+def call(kernel, outs, *args, scalars=0, cost=COST):
     specs = [pl.BlockSpec(memory_space=pltpu.SMEM)] * scalars
     specs += [pl.BlockSpec()] * (len(args) - scalars)
     return pl.pallas_call(
@@ -209,7 +209,7 @@
         in_specs=specs,
         out_shape=[jax.ShapeDtypeStruct(shape, kind) for shape, kind in outs],
         compiler_params=pltpu.CompilerParams(vmem_limit_bytes=32 * 2**20),
-        cost_estimate=pl.CostEstimate(flops=COST, bytes_accessed=1024, transcendentals=0),
+        cost_estimate=pl.CostEstimate(flops=cost, bytes_accessed=1024, transcendentals=0),
     )(*args)
 
 
@@ -279,7 +279,9 @@
     )
     got = lax.ppermute(leaves, "core", swap)
     (back,) = call(core_sum_kernel, [((nx, half // nx + EXTRA, width), i16)], stays, got)
-    back, first, second = lax.optimization_barrier((back, first, second))
+    back, first, second, own, other = lax.optimization_barrier(
+        (back, first, second, own, other)
+    )
     back = lax.all_to_all(back, "x", 0, 0)
     (back,) = call(x_sum_kernel, [((nzlo, rows, width), f32)], back)
     back = lax.all_to_all(back, "zlo", 0, 0)

time: 194 us -> 195 us (level)
  no operation moved by 1% of the time
where the time goes in v10:
time: 195 us; the launch traced here: 193 us
  starting transfers between devices  70.3 us (36%)
  waiting for transfers between devices  60.7 us (31%)
  blocking collectives  37.9 us (19%)
  Pallas kernels  9.81 us (5%)
  local copies, waits for them, and re-layouts  6.98 us (4%)
  matrix products  4.94 us (3%)
    ppermute x3, waiting for transfers between devices, zhi_exchange(): return lax.ppermute(block, ('zhi', 'core'), pairs)  36.7 us
    ppermute x3, starting transfers between devices, zhi_exchange(): return lax.ppermute(block, ('zhi', 'core'), pairs)  36.3 us
    all_to_all x1, blocking collectives, body(): both = lax.all_to_all(both, 'zlo', 0, 0)  24.3 us
    all_to_all x1, blocking collectives, body(): second = lax.all_to_all(to_y, 'y', 0, 0)  13.6 us
    pallas_call x12, Pallas kernels, call(): pl.pallas_call(kernel, in_specs=specs, out_shape=[jax.ShapeDtypeStruct(sh...  9.81 us
    all_to_all x1, waiting for transfers between devices, body(): sent = lax.all_to_all(sent, 'y', 0, 0)  9.55 us
    all_to_all x1, waiting for transfers between devices, body(): back = lax.all_to_all(back, 'zlo', 0, 0)  7.03 us
    all_to_all x1, starting transfers between devices, body(): both = lax.all_to_all(both, 'x', 0, 0)  6.25 us
  transfers between devices with their start and end apart: 11, of which 9 were waited for; matrix products, arithmetic and copies ran while one was open for 3% of the time, Pallas kernels for 2%

profile of v10, /device:TPU:6, one launch (start us, length us, event | category | flops | bytes accessed | tf_op | source)
XLA Modules:
  0.0 193.1 jit_solution(11107058215403372731)
XLA Ops:
  0.6 0.7 pad_maximum_fusion
  1.4 24.3 %all_to_all.40.block_ref = bf16[8,2,8,512]{3,2,1,0:T(8,128)(2,1)S(1)} all-to-all(bf16[8,2,8,512]{3,2,1,0:T(8,128)(2,1)S(1)} %broadcast_in_dim.12), channel_id=1, replica_groups=mesh['zhi'=4,'y'=4,'zlo'=8,'x'=4,'core'=2] {'zlo'}, dimensions={0} | all-to-all | bytes 262144 | tf_op jit(solution)/shard_map/all_to_all | solution.py:227
  25.6 0.8 shard_map.111
  26.5 6.3 %all-to-all-start.1 = ((bf16[4,8,2,8,512]{4,3,2,1,0:T(8,128)(2,1)}), bf16[4,8,2,8,512]{4,3,2,1,0:T(8,128)(2,1)S(1)}, u32[]{:S(2)}, u32[]{:S(2)}) async-start(bf16[4,8,2,8,512]{4,3,2,1,0:T(8,128)(2,1)} %shard_map.111), calls=%async_computation.1 | async-start | bytes 1048576 | tf_op jit(solution)/shard_map/all_to_all | solution.py:232
  32.8 1.4 shard_map.112
  34.2 0.8 copy-done
  35.0 0.8 copy-done.2
  35.7 0.8 copy-done.4
  36.5 0.8 copy-done.14
  37.3 0.8 copy-done.17
  38.0 0.7 all-to-all-done.1
  38.8 2.1 %collective-permute-start = (bf16[2,256,512]{2,1,0:T(8,128)(2,1)S(1)}, bf16[2,256,512]{2,1,0:T(8,128)(2,1)S(1)}, u32[]{:S(2)}, u32[]{:S(2)}) collective-permute-start(bf16[2,256,512]{2,1,0:T(8,128)(2,1)S(1)} %bitcast.47), channel_id=1, source_target_pairs={{0,1},{1,0},{2,3},{3,2},{4,5},{5,4},{6,7},{7,6},{8,9},{9,8},{10,11... | collective-permute-start | bytes 1572872 | tf_op jit(solution)/shard_map/ppermute | solution.py:245
  40.9 1.9 collective-permute-done.other_ref
  42.7 1.6 shard_map.114
  44.3 3.5 %all-to-all-start.2 = ((s16[4,352,256]{2,1,0:T(8,128)(2,1)}), s16[4,352,256]{2,1,0:T(8,128)(2,1)S(1)}, u32[]{:S(2)}, u32[]{:S(2)}) async-start(s16[4,352,256]{2,1,0:T(8,128)(2,1)} %shard_map.114), calls=%async_computation.2 | async-start | bytes 1441792 | tf_op jit(solution)/shard_map/all_to_all | solution.py:258
  47.8 1.0 copy-done.19
  48.8 1.5 shard_map.113
  50.4 9.5 %all-to-all-done.2.block_ref = s16[4,352,256]{2,1,0:T(8,128)(2,1)S(1)} async-done(((s16[4,352,256]{2,1,0:T(8,128)(2,1)}), s16[4,352,256]{2,1,0:T(8,128)(2,1)S(1)}, u32[]{:S(2)}, u32[]{:S(2)}) %all-to-all-start.2) | async-done | bytes 720928 | tf_op jit(solution)/shard_map/all_to_all | solution.py:258
  60.2 3.5 %all-to-all-start.3 = ((s16[4,352,256]{2,1,0:T(8,128)(2,1)}), s16[4,352,256]{2,1,0:T(8,128)(2,1)S(1)}, u32[]{:S(2)}, u32[]{:S(2)}) async-start(s16[4,352,256]{2,1,0:T(8,128)(2,1)} %shard_map.113), calls=%async_computation.3 | async-start | bytes 1441792 | tf_op jit(solution)/shard_map/all_to_all | solution.py:262
  63.7 15.1 %collective-permute-start.1 = (s16[352,256]{1,0:T(8,128)(2,1)S(1)}, s16[352,256]{1,0:T(8,128)(2,1)S(1)}, u32[]{:S(2)}, u32[]{:S(2)}) collective-permute-start(s16[352,256]{1,0:T(8,128)(2,1)S(1)} %shard_map.115), channel_id=1, source_target_pairs={{0,256},{1,769},{256,0},{257,513},{512,768},{513,257},{768,512},{7... | collective-permute-start | bytes 540680 | tf_op jit(solution)/shard_map/ppermute | solution.py:39
  78.8 17.1 %collective-permute-done.1.got_ref = s16[352,256]{1,0:T(8,128)(2,1)S(1)} collective-permute-done((s16[352,256]{1,0:T(8,128)(2,1)S(1)}, s16[352,256]{1,0:T(8,128)(2,1)S(1)}, u32[]{:S(2)}, u32[]{:S(2)}) %collective-permute-start.1) | collective-permute-done | bytes 180256 | tf_op jit(solution)/shard_map/ppermute | solution.py:39
  95.8 0.3 shard_map.116
  96.1 11.2 %collective-permute-start.2 = (s16[352,256]{1,0:T(8,128)(2,1)S(1)}, s16[352,256]{1,0:T(8,128)(2,1)S(1)}, u32[]{:S(2)}, u32[]{:S(2)}) collective-permute-start(s16[352,256]{1,0:T(8,128)(2,1)S(1)} %get-tuple-element.45), channel_id=1, source_target_pairs={{0,768},{1,257},{256,512},{257,1},{512,256},{513,769},{768,0},{769... | collective-permute-start | bytes 540680 | tf_op jit(solution)/shard_map/ppermute | solution.py:39
  107.3 8.7 %collective-permute-done.2.got_ref = s16[352,256]{1,0:T(8,128)(2,1)S(1)} collective-permute-done((s16[352,256]{1,0:T(8,128)(2,1)S(1)}, s16[352,256]{1,0:T(8,128)(2,1)S(1)}, u32[]{:S(2)}, u32[]{:S(2)}) %collective-permute-start.2) | collective-permute-done | bytes 180256 | tf_op jit(solution)/shard_map/ppermute | solution.py:39
  116.0 1.0 shard_map.117
  117.0 5.0 %all-to-all-start.4 = ((bf16[4,336,256]{2,1,0:T(8,128)(2,1)}), bf16[4,336,256]{2,1,0:T(8,128)(2,1)S(1)}, u32[]{:S(2)}, u32[]{:S(2)}) async-start(bf16[4,336,256]{2,1,0:T(8,128)(2,1)} %get-tuple-element.46), calls=%async_computation.4 | async-start | bytes 1376256 | tf_op jit(solution)/shard_map/all_to_all | solution.py:270
  122.0 10.0 %collective-permute-start.3 = (bf16[336,256]{1,0:T(8,128)(2,1)S(1)}, bf16[336,256]{1,0:T(8,128)(2,1)S(1)}, u32[]{:S(2)}, u32[]{:S(2)}) collective-permute-start(bf16[336,256]{1,0:T(8,128)(2,1)S(1)} %get-tuple-element.47), channel_id=1, source_target_pairs={{0,256},{1,769},{256,0},{257,513},{512,768},{513,257},{768,512},{7... | collective-permute-start | bytes 516104 | tf_op jit(solution)/shard_map/ppermute | solution.py:39
  132.0 11.0 %collective-permute-done.3.block_ref = bf16[336,256]{1,0:T(8,128)(2,1)S(1)} collective-permute-done((bf16[336,256]{1,0:T(8,128)(2,1)S(1)}, bf16[336,256]{1,0:T(8,128)(2,1)S(1)}, u32[]{:S(2)}, u32[]{:S(2)}) %collective-permute-start.3) | collective-permute-done | bytes 172064 | tf_op jit(solution)/shard_map/ppermute | solution.py:39
  143.1 13.6 %all_to_all.41.second_ref = bf16[4,336,256]{2,1,0:T(8,128)(2,1)S(1)} all-to-all(bf16[4,336,256]{2,1,0:T(8,128)(2,1)S(1)} %shard_map.118), channel_id=1, replica_groups=mesh['zhi'=4,'y'=4,'zlo'=8,'x'=4,'core'=2] {'y'}, dimensions={0} | all-to-all | bytes 1376256 | tf_op jit(solution)/shard_map/all_to_all | solution.py:272
  156.7 0.7 shard_map.119
  157.5 1.9 collective-permute-start.4
  159.4 1.9 collective-permute-done.4.got_ref
  161.3 0.8 shard_map.120
  162.1 0.7 fusion.12
  162.9 5.5 %all-to-all-start.6 = ((s16[4,80,512]{2,1,0:T(8,128)(2,1)}), s16[4,80,512]{2,1,0:T(8,128)(2,1)S(1)}, u32[]{:S(2)}, u32[]{:S(2)}) async-start(s16[4,80,512]{2,1,0:T(8,128)(2,1)} %shard_map.120), calls=%async_computation.6 | async-start | bytes 655360 | tf_op jit(solution)/shard_map/all_to_all | solution.py:285
  168.4 0.9 broadcast_select_fusion
  169.3 1.2 fusion.9
  170.5 0.3 fusion.8
  170.7 0.3 fusion.10
  171.0 3.0 %all-to-all-done.6.block_ref = s16[4,80,512]{2,1,0:T(8,128)(2,1)S(1)} async-done(((s16[4,80,512]{2,1,0:T(8,128)(2,1)}), s16[4,80,512]{2,1,0:T(8,128)(2,1)S(1)}, u32[]{:S(2)}, u32[]{:S(2)}) %all-to-all-start.6) | async-done | bytes 327712 | tf_op jit(solution)/shard_map/all_to_all | solution.py:285
  174.1 0.7 shard_map.121
  174.8 6.2 %all-to-all-start.7 = ((f32[8,8,512]{2,1,0:T(8,128)}), f32[8,8,512]{2,1,0:T(8,128)S(1)}, u32[]{:S(2)}, u32[]{:S(2)}) async-start(f32[8,8,512]{2,1,0:T(8,128)} %shard_map.121), calls=%async_computation.7 | async-start | bytes 262144 | tf_op jit(solution)/shard_map/all_to_all | solution.py:287
  181.1 1.1 copy-done.20
  182.3 1.1 fusion.6
  183.3 1.1 fusion.5
  184.4 1.1 fusion.7
  185.5 7.0 %all-to-all-done.7.block_ref = f32[8,8,512]{2,1,0:T(8,128)S(1)} async-done(((f32[8,8,512]{2,1,0:T(8,128)}), f32[8,8,512]{2,1,0:T(8,128)S(1)}, u32[]{:S(2)}, u32[]{:S(2)}) %all-to-all-start.7) | async-done | bytes 131104 | tf_op jit(solution)/shard_map/all_to_all | solution.py:287
  192.5 0.6 shard_map.122
  (46 shorter events, 0.6 us)
Async XLA Ops:
  25.6 7.1 %copy-start.8 = (bf16[448,512]{1,0:T(8,128)(2,1)S(1)}, bf16[448,512]{1,0:T(8,128)(2,1)}, u32[]{:S(2)}) copy-start(bf16[448,512]{1,0:T(8,128)(2,1)} %refs_5_.1) | copy-start | bytes 1376260
  25.6 7.1 %copy-start.9 = (s32[128,448]{0,1:T(8,128)S(1)}, s32[128,448]{0,1:T(8,128)}, u32[]{:S(2)}) copy-start(s32[128,448]{0,1:T(8,128)} %param.13) | copy-start | bytes 688132
  25.6 7.1 %copy-start.10 = (s32[128,448]{0,1:T(8,128)S(1)}, s32[128,448]{0,1:T(8,128)}, u32[]{:S(2)}) copy-start(s32[128,448]{0,1:T(8,128)} %param.14) | copy-start | bytes 688132
  25.6 7.1 %copy-start.11 = (s32[112,512]{1,0:T(8,128)S(1)}, s32[112,512]{1,0:T(8,128)}, u32[]{:S(2)}) copy-start(s32[112,512]{1,0:T(8,128)} %refs_2_) | copy-start | bytes 688132
  26.5 6.3 %copy-start.6 = (bf16[512,448]{0,1:T(8,128)(2,1)S(1)}, bf16[512,448]{0,1:T(8,128)(2,1)}, u32[]{:S(2)}) copy-start(bf16[512,448]{0,1:T(8,128)(2,1)} %param.10) | copy-start | bytes 1376260
  26.5 6.3 %copy-start.7 = (bf16[512,448]{0,1:T(8,128)(2,1)S(1)}, bf16[512,448]{0,1:T(8,128)(2,1)}, u32[]{:S(2)}) copy-start(bf16[512,448]{0,1:T(8,128)(2,1)} %param.11) | copy-start | bytes 1376260
  26.5 12.3 %all-to-all-start.1 = ((bf16[4,8,2,8,512]{4,3,2,1,0:T(8,128)(2,1)}), bf16[4,8,2,8,512]{4,3,2,1,0:T(8,128)(2,1)S(1)}, u32[]{:S(2)}, u32[]{:S(2)}) async-start(bf16[4,8,2,8,512]{4,3,2,1,0:T(8,128)(2,1)} %shard_map.111), calls=%async_computation.1 | async-start | bytes 1048576 | tf_op jit(solution)/shard_map/all_to_all | solution.py:232
  34.2 0.8 copy-start
  35.0 0.8 copy-start.2
  35.7 0.8 copy-start.4
  36.5 0.8 copy-start.14
  37.3 0.8 copy-start.17
  38.0 9.7 %copy-start.12 = (bf16[448,512]{1,0:T(8,128)(2,1)}, bf16[448,512]{1,0:T(8,128)(2,1)S(1)}, u32[]{:S(2)}) copy-start(bf16[448,512]{1,0:T(8,128)(2,1)S(1)} %get-tuple-element.38.gate_ref) | copy-start | bytes 1376260
  38.7 4.0 %copy-start.15 = (bf16[448,512]{1,0:T(8,128)(2,1)S(1)}, bf16[448,512]{1,0:T(8,128)(2,1)}, u32[]{:S(2)}) copy-start(bf16[448,512]{1,0:T(8,128)(2,1)} %copy-done.14) | copy-start | bytes 1376260
  38.8 4.0 %copy-start.18 = (bf16[448,512]{1,0:T(8,128)(2,1)S(1)}, bf16[448,512]{1,0:T(8,128)(2,1)}, u32[]{:S(2)}) copy-start(bf16[448,512]{1,0:T(8,128)(2,1)} %copy-done.17) | copy-start | bytes 1376260
  38.8 3.9 %collective-permute-start = (bf16[2,256,512]{2,1,0:T(8,128)(2,1)S(1)}, bf16[2,256,512]{2,1,0:T(8,128)(2,1)S(1)}, u32[]{:S(2)}, u32[]{:S(2)}) collective-permute-start(bf16[2,256,512]{2,1,0:T(8,128)(2,1)S(1)} %bitcast.47), channel_id=1, source_target_pairs={{0,1},{1,0},{2,3},{3,2},{4,5},{5,4},{6,7},{7,6},{8,9},{9,8},{10,11... | collective-permute-start | bytes 1572872 | tf_op jit(solution)/shard_map/ppermute | solution.py:245
  44.3 15.6 %all-to-all-start.2 = ((s16[4,352,256]{2,1,0:T(8,128)(2,1)}), s16[4,352,256]{2,1,0:T(8,128)(2,1)S(1)}, u32[]{:S(2)}, u32[]{:S(2)}) async-start(s16[4,352,256]{2,1,0:T(8,128)(2,1)} %shard_map.114), calls=%async_computation.2 | async-start | bytes 1441792 | tf_op jit(solution)/shard_map/all_to_all | solution.py:258
  47.8 1.0 copy-start.19
  60.2 35.7 %all-to-all-start.3 = ((s16[4,352,256]{2,1,0:T(8,128)(2,1)}), s16[4,352,256]{2,1,0:T(8,128)(2,1)S(1)}, u32[]{:S(2)}, u32[]{:S(2)}) async-start(s16[4,352,256]{2,1,0:T(8,128)(2,1)} %shard_map.113), calls=%async_computation.3 | async-start | bytes 1441792 | tf_op jit(solution)/shard_map/all_to_all | solution.py:262
  63.7 32.2 %collective-permute-start.1 = (s16[352,256]{1,0:T(8,128)(2,1)S(1)}, s16[352,256]{1,0:T(8,128)(2,1)S(1)}, u32[]{:S(2)}, u32[]{:S(2)}) collective-permute-start(s16[352,256]{1,0:T(8,128)(2,1)S(1)} %shard_map.115), channel_id=1, source_target_pairs={{0,256},{1,769},{256,0},{257,513},{512,768},{513,257},{768,512},{7... | collective-permute-start | bytes 540680 | tf_op jit(solution)/shard_map/ppermute | solution.py:39
  96.1 19.9 %collective-permute-start.2 = (s16[352,256]{1,0:T(8,128)(2,1)S(1)}, s16[352,256]{1,0:T(8,128)(2,1)S(1)}, u32[]{:S(2)}, u32[]{:S(2)}) collective-permute-start(s16[352,256]{1,0:T(8,128)(2,1)S(1)} %get-tuple-element.45), channel_id=1, source_target_pairs={{0,768},{1,257},{256,512},{257,1},{512,256},{513,769},{768,0},{769... | collective-permute-start | bytes 540680 | tf_op jit(solution)/shard_map/ppermute | solution.py:39
  117.0 26.0 %all-to-all-start.4 = ((bf16[4,336,256]{2,1,0:T(8,128)(2,1)}), bf16[4,336,256]{2,1,0:T(8,128)(2,1)S(1)}, u32[]{:S(2)}, u32[]{:S(2)}) async-start(bf16[4,336,256]{2,1,0:T(8,128)(2,1)} %get-tuple-element.46), calls=%async_computation.4 | async-start | bytes 1376256 | tf_op jit(solution)/shard_map/all_to_all | solution.py:270
  122.0 21.0 %collective-permute-start.3 = (bf16[336,256]{1,0:T(8,128)(2,1)S(1)}, bf16[336,256]{1,0:T(8,128)(2,1)S(1)}, u32[]{:S(2)}, u32[]{:S(2)}) collective-permute-start(bf16[336,256]{1,0:T(8,128)(2,1)S(1)} %get-tuple-element.47), channel_id=1, source_target_pairs={{0,256},{1,769},{256,0},{257,513},{512,768},{513,257},{768,512},{7... | collective-permute-start | bytes 516104 | tf_op jit(solution)/shard_map/ppermute | solution.py:39
  143.1 13.7 %copy-start.13 = (bf16[448,512]{1,0:T(8,128)(2,1)S(1)}, bf16[448,512]{1,0:T(8,128)(2,1)}, u32[]{:S(2)}) copy-start(bf16[448,512]{1,0:T(8,128)(2,1)} %copy-done.12) | copy-start | bytes 1376260
  143.1 13.7 %copy-start.16 = (bf16[448,512]{1,0:T(8,128)(2,1)S(1)}, bf16[448,512]{1,0:T(8,128)(2,1)}, u32[]{:S(2)}) copy-start(bf16[448,512]{1,0:T(8,128)(2,1)} %copy-done.14) | copy-start | bytes 1376260
  157.5 3.8 %collective-permute-start.4 = (f32[256,512]{1,0:T(8,128)S(1)}, f32[256,512]{1,0:T(8,128)S(1)}, u32[]{:S(2)}, u32[]{:S(2)}) collective-permute-start(f32[256,512]{1,0:T(8,128)S(1)} %get-tuple-element.49), channel_id=1, source_target_pairs={{0,1},{1,0},{2,3},{3,2},{4,5},{5,4},{6,7},{7,6},{8,9},{9,8},{10,11... | collective-permute-start | bytes 1572872 | tf_op jit(solution)/shard_map/ppermute | solution.py:280
  162.9 11.2 %all-to-all-start.6 = ((s16[4,80,512]{2,1,0:T(8,128)(2,1)}), s16[4,80,512]{2,1,0:T(8,128)(2,1)S(1)}, u32[]{:S(2)}, u32[]{:S(2)}) async-start(s16[4,80,512]{2,1,0:T(8,128)(2,1)} %shard_map.120), calls=%async_computation.6 | async-start | bytes 655360 | tf_op jit(solution)/shard_map/all_to_all | solution.py:285
  169.3 1.2 copy-start.22
  174.1 7.0 %copy-start.21 = (bf16[2,256,512]{2,1,0:T(8,128)(2,1)S(1)}, bf16[2,256,512]{2,1,0:T(8,128)(2,1)}, u32[]{:S(2)}) copy-start(bf16[2,256,512]{2,1,0:T(8,128)(2,1)} %get-tuple-element.58) | copy-start | bytes 1572868
  174.8 17.7 %all-to-all-start.7 = ((f32[8,8,512]{2,1,0:T(8,128)}), f32[8,8,512]{2,1,0:T(8,128)S(1)}, u32[]{:S(2)}, u32[]{:S(2)}) async-start(f32[8,8,512]{2,1,0:T(8,128)} %shard_map.121), calls=%async_computation.7 | async-start | bytes 262144 | tf_op jit(solution)/shard_map/all_to_all | solution.py:287
  181.0 1.2 copy-start.20
  181.0 1.3 copy-start.5
  182.3 1.1 copy-start.3
  183.3 1.1 copy-start.1

commit v11 on v9

--- a/solution.py
+++ b/solution.py
@@ -40,7 +40,7 @@
 
 
 EXTRA = 16
-COST = 2 * 10**9
+COST = 2 * 10**10
 
 
 def pack(values):

time: 194 us -> 202 us (1.041)
  starting transfers between devices: 70.3 us -> 77.3 us
    all_to_all x1, starting transfers between devices: 6.19 us -> 12.9 us  [body(): back = lax.all_to_all(back, 'zlo', 0, 0)]
    all_to_all x1, waiting for transfers between devices: 0.01 us -> 2.51 us  [body(): first = lax.all_to_all(to_y, 'y', 0, 0)]
    ppermute x3, waiting for transfers between devices: 36.7 us -> 34.2 us  [zhi_exchange(): return lax.ppermute(block, ('zhi', 'core'), pairs)]
  transfers between devices with their start and end apart: 11 -> 11, of which waited for: 9 -> 10; matrix products, arithmetic and copies ran while one was open for 3% -> 3% of each run, Pallas kernels for 2% -> 1%
where the time goes in v11:
time: 202 us; the launch traced here: 200 us
  starting transfers between devices  77.3 us (38%)
  waiting for transfers between devices  59.5 us (29%)
  blocking collectives  38.9 us (19%)
  Pallas kernels  9.8 us (5%)
  local copies, waits for them, and re-layouts  7.27 us (4%)
  matrix products  4.95 us (2%)
    ppermute x3, starting transfers between devices, zhi_exchange(): return lax.ppermute(block, ('zhi', 'core'), pairs)  36.2 us
    ppermute x3, waiting for transfers between devices, zhi_exchange(): return lax.ppermute(block, ('zhi', 'core'), pairs)  34.2 us
    all_to_all x1, blocking collectives, body(): both = lax.all_to_all(both, 'zlo', 0, 0)  24.3 us
    all_to_all x1, blocking collectives, body(): second = lax.all_to_all(to_y, 'y', 0, 0)  14.6 us
    all_to_all x1, starting transfers between devices, body(): back = lax.all_to_all(back, 'zlo', 0, 0)  12.9 us
    pallas_call x12, Pallas kernels, call(): pl.pallas_call(kernel, in_specs=specs, out_shape=[jax.ShapeDtypeStruct(sh...  9.8 us
    all_to_all x1, waiting for transfers between devices, body(): sent = lax.all_to_all(sent, 'y', 0, 0)  9.55 us
    unnamed x46, local copies, waits for them, and re-layouts  7.13 us
  transfers between devices with their start and end apart: 11, of which 10 were waited for; matrix products, arithmetic and copies ran while one was open for 3% of the time, Pallas kernels for 1%

profile of v11, /device:TPU:6, one launch (start us, length us, event | category | flops | bytes accessed | tf_op | source)
XLA Modules:
  0.0 200.4 jit_solution(8091915552236200072)
XLA Ops:
  0.6 0.7 pad_maximum_fusion
  1.4 24.3 %all_to_all.40.block_ref = bf16[8,2,8,512]{3,2,1,0:T(8,128)(2,1)S(1)} all-to-all(bf16[8,2,8,512]{3,2,1,0:T(8,128)(2,1)S(1)} %broadcast_in_dim.12), channel_id=1, replica_groups=mesh['zhi'=4,'y'=4,'zlo'=8,'x'=4,'core'=2] {'zlo'}, dimensions={0} | all-to-all | bytes 262144 | tf_op jit(solution)/shard_map/all_to_all | solution.py:227
  25.6 0.8 shard_map.111
  26.5 6.3 %all-to-all-start.1 = ((bf16[4,8,2,8,512]{4,3,2,1,0:T(8,128)(2,1)}), bf16[4,8,2,8,512]{4,3,2,1,0:T(8,128)(2,1)S(1)}, u32[]{:S(2)}, u32[]{:S(2)}) async-start(bf16[4,8,2,8,512]{4,3,2,1,0:T(8,128)(2,1)} %shard_map.111), calls=%async_computation.1 | async-start | bytes 1048576 | tf_op jit(solution)/shard_map/all_to_all | solution.py:232
  32.8 1.4 shard_map.112
  34.2 0.8 copy-done
  35.0 0.8 copy-done.2
  35.7 0.8 copy-done.4
  36.5 0.8 copy-done.14
  37.3 0.8 copy-done.17
  38.0 0.7 all-to-all-done.1
  38.8 2.1 %collective-permute-start = (bf16[2,256,512]{2,1,0:T(8,128)(2,1)S(1)}, bf16[2,256,512]{2,1,0:T(8,128)(2,1)S(1)}, u32[]{:S(2)}, u32[]{:S(2)}) collective-permute-start(bf16[2,256,512]{2,1,0:T(8,128)(2,1)S(1)} %bitcast.49), channel_id=1, source_target_pairs={{0,1},{1,0},{2,3},{3,2},{4,5},{5,4},{6,7},{7,6},{8,9},{9,8},{10,11... | collective-permute-start | bytes 1572872 | tf_op jit(solution)/shard_map/ppermute | solution.py:245
  40.9 1.9 collective-permute-done.other_ref
  42.7 1.6 shard_map.114
  44.3 3.5 %all-to-all-start.2 = ((s16[4,352,256]{2,1,0:T(8,128)(2,1)}), s16[4,352,256]{2,1,0:T(8,128)(2,1)S(1)}, u32[]{:S(2)}, u32[]{:S(2)}) async-start(s16[4,352,256]{2,1,0:T(8,128)(2,1)} %shard_map.114), calls=%async_computation.2 | async-start | bytes 1441792 | tf_op jit(solution)/shard_map/all_to_all | solution.py:258
  47.8 1.0 copy-done.19
  48.8 1.5 shard_map.113
  50.4 9.5 %all-to-all-done.2.block_ref = s16[4,352,256]{2,1,0:T(8,128)(2,1)S(1)} async-done(((s16[4,352,256]{2,1,0:T(8,128)(2,1)}), s16[4,352,256]{2,1,0:T(8,128)(2,1)S(1)}, u32[]{:S(2)}, u32[]{:S(2)}) %all-to-all-start.2) | async-done | bytes 720928 | tf_op jit(solution)/shard_map/all_to_all | solution.py:258
  60.2 3.5 %all-to-all-start.3 = ((s16[4,352,256]{2,1,0:T(8,128)(2,1)}), s16[4,352,256]{2,1,0:T(8,128)(2,1)S(1)}, u32[]{:S(2)}, u32[]{:S(2)}) async-start(s16[4,352,256]{2,1,0:T(8,128)(2,1)} %shard_map.113), calls=%async_computation.3 | async-start | bytes 1441792 | tf_op jit(solution)/shard_map/all_to_all | solution.py:262
  63.7 15.1 %collective-permute-start.1 = (s16[352,256]{1,0:T(8,128)(2,1)S(1)}, s16[352,256]{1,0:T(8,128)(2,1)S(1)}, u32[]{:S(2)}, u32[]{:S(2)}) collective-permute-start(s16[352,256]{1,0:T(8,128)(2,1)S(1)} %shard_map.115), channel_id=1, source_target_pairs={{0,256},{1,769},{256,0},{257,513},{512,768},{513,257},{768,512},{7... | collective-permute-start | bytes 540680 | tf_op jit(solution)/shard_map/ppermute | solution.py:39
  78.8 17.1 %collective-permute-done.1.got_ref = s16[352,256]{1,0:T(8,128)(2,1)S(1)} collective-permute-done((s16[352,256]{1,0:T(8,128)(2,1)S(1)}, s16[352,256]{1,0:T(8,128)(2,1)S(1)}, u32[]{:S(2)}, u32[]{:S(2)}) %collective-permute-start.1) | collective-permute-done | bytes 180256 | tf_op jit(solution)/shard_map/ppermute | solution.py:39
  95.8 0.3 shard_map.116
  96.1 11.2 %collective-permute-start.2 = (s16[352,256]{1,0:T(8,128)(2,1)S(1)}, s16[352,256]{1,0:T(8,128)(2,1)S(1)}, u32[]{:S(2)}, u32[]{:S(2)}) collective-permute-start(s16[352,256]{1,0:T(8,128)(2,1)S(1)} %get-tuple-element.43), channel_id=1, source_target_pairs={{0,768},{1,257},{256,512},{257,1},{512,256},{513,769},{768,0},{769... | collective-permute-start | bytes 540680 | tf_op jit(solution)/shard_map/ppermute | solution.py:39
  107.3 8.8 %collective-permute-done.2.got_ref = s16[352,256]{1,0:T(8,128)(2,1)S(1)} collective-permute-done((s16[352,256]{1,0:T(8,128)(2,1)S(1)}, s16[352,256]{1,0:T(8,128)(2,1)S(1)}, u32[]{:S(2)}, u32[]{:S(2)}) %collective-permute-start.2) | collective-permute-done | bytes 180256 | tf_op jit(solution)/shard_map/ppermute | solution.py:39
  116.1 1.0 shard_map.117
  117.1 9.9 %collective-permute-start.3 = (bf16[336,256]{1,0:T(8,128)(2,1)S(1)}, bf16[336,256]{1,0:T(8,128)(2,1)S(1)}, u32[]{:S(2)}, u32[]{:S(2)}) collective-permute-start(bf16[336,256]{1,0:T(8,128)(2,1)S(1)} %get-tuple-element.45), channel_id=1, source_target_pairs={{0,256},{1,769},{256,0},{257,513},{512,768},{513,257},{768,512},{7... | collective-permute-start | bytes 516104 | tf_op jit(solution)/shard_map/ppermute | solution.py:39
  127.0 5.0 %all-to-all-start.4 = ((bf16[4,336,256]{2,1,0:T(8,128)(2,1)}), bf16[4,336,256]{2,1,0:T(8,128)(2,1)S(1)}, u32[]{:S(2)}, u32[]{:S(2)}) async-start(bf16[4,336,256]{2,1,0:T(8,128)(2,1)} %get-tuple-element.44), calls=%async_computation.4 | async-start | bytes 1376256 | tf_op jit(solution)/shard_map/all_to_all | solution.py:270
  132.1 8.4 %collective-permute-done.3.block_ref = bf16[336,256]{1,0:T(8,128)(2,1)S(1)} collective-permute-done((bf16[336,256]{1,0:T(8,128)(2,1)S(1)}, bf16[336,256]{1,0:T(8,128)(2,1)S(1)}, u32[]{:S(2)}, u32[]{:S(2)}) %collective-permute-start.3) | collective-permute-done | bytes 172064 | tf_op jit(solution)/shard_map/ppermute | solution.py:39
  140.5 2.5 %all-to-all-done.4.first_ref = bf16[4,336,256]{2,1,0:T(8,128)(2,1)S(1)} async-done(((bf16[4,336,256]{2,1,0:T(8,128)(2,1)}), bf16[4,336,256]{2,1,0:T(8,128)(2,1)S(1)}, u32[]{:S(2)}, u32[]{:S(2)}) %all-to-all-start.4) | async-done | bytes 688160 | tf_op jit(solution)/shard_map/all_to_all | solution.py:270
  143.0 14.6 %all_to_all.41.second_ref = bf16[4,336,256]{2,1,0:T(8,128)(2,1)S(1)} all-to-all(bf16[4,336,256]{2,1,0:T(8,128)(2,1)S(1)} %shard_map.118), channel_id=1, replica_groups=mesh['zhi'=4,'y'=4,'zlo'=8,'x'=4,'core'=2] {'y'}, dimensions={0} | all-to-all | bytes 1376256 | tf_op jit(solution)/shard_map/all_to_all | solution.py:272
  157.6 0.7 shard_map.119
  158.3 2.3 %collective-permute-start.4 = (f32[256,512]{1,0:T(8,128)S(1)}, f32[256,512]{1,0:T(8,128)S(1)}, u32[]{:S(2)}, u32[]{:S(2)}) collective-permute-start(f32[256,512]{1,0:T(8,128)S(1)} %get-tuple-element.47), channel_id=1, source_target_pairs={{0,1},{1,0},{2,3},{3,2},{4,5},{5,4},{6,7},{7,6},{8,9},{9,8},{10,11... | collective-permute-start | bytes 1572872 | tf_op jit(solution)/shard_map/ppermute | solution.py:280
  160.6 1.1 broadcast_select_fusion.1
  161.7 0.5 collective-permute-done.4.got_ref
  162.1 0.8 shard_map.120
  163.0 5.6 %all-to-all-start.6 = ((s16[4,80,512]{2,1,0:T(8,128)(2,1)}), s16[4,80,512]{2,1,0:T(8,128)(2,1)S(1)}, u32[]{:S(2)}, u32[]{:S(2)}) async-start(s16[4,80,512]{2,1,0:T(8,128)(2,1)} %shard_map.120), calls=%async_computation.6 | async-start | bytes 655360 | tf_op jit(solution)/shard_map/all_to_all | solution.py:283
  168.7 1.0 copy-done.22
  169.6 1.2 fusion.9
  170.9 0.3 fusion.8
  171.4 3.2 %all-to-all-done.6.block_ref = s16[4,80,512]{2,1,0:T(8,128)(2,1)S(1)} async-done(((s16[4,80,512]{2,1,0:T(8,128)(2,1)}), s16[4,80,512]{2,1,0:T(8,128)(2,1)S(1)}, u32[]{:S(2)}, u32[]{:S(2)}) %all-to-all-start.6) | async-done | bytes 327712 | tf_op jit(solution)/shard_map/all_to_all | solution.py:283
  174.6 0.7 shard_map.121
  175.4 12.9 %all-to-all-start.7 = ((f32[8,8,512]{2,1,0:T(8,128)}), f32[8,8,512]{2,1,0:T(8,128)S(1)}, u32[]{:S(2)}, u32[]{:S(2)}) async-start(f32[8,8,512]{2,1,0:T(8,128)} %shard_map.121), calls=%async_computation.7 | async-start | bytes 262144 | tf_op jit(solution)/shard_map/all_to_all | solution.py:285
  188.3 1.1 copy-done.20
  189.5 1.1 fusion.6
  190.6 1.1 fusion.5
  191.7 1.1 fusion.7
  192.7 7.0 %all-to-all-done.7.block_ref = f32[8,8,512]{2,1,0:T(8,128)S(1)} async-done(((f32[8,8,512]{2,1,0:T(8,128)}), f32[8,8,512]{2,1,0:T(8,128)S(1)}, u32[]{:S(2)}, u32[]{:S(2)}) %all-to-all-start.7) | async-done | bytes 131104 | tf_op jit(solution)/shard_map/all_to_all | solution.py:285
  199.8 0.6 shard_map.122
  (46 shorter events, 0.9 us)
Async XLA Ops:
  25.6 7.1 %copy-start.8 = (bf16[448,512]{1,0:T(8,128)(2,1)S(1)}, bf16[448,512]{1,0:T(8,128)(2,1)}, u32[]{:S(2)}) copy-start(bf16[448,512]{1,0:T(8,128)(2,1)} %refs_5_.1) | copy-start | bytes 1376260
  25.6 7.1 %copy-start.9 = (s32[128,448]{0,1:T(8,128)S(1)}, s32[128,448]{0,1:T(8,128)}, u32[]{:S(2)}) copy-start(s32[128,448]{0,1:T(8,128)} %param.13) | copy-start | bytes 688132
  25.6 7.1 %copy-start.10 = (s32[128,448]{0,1:T(8,128)S(1)}, s32[128,448]{0,1:T(8,128)}, u32[]{:S(2)}) copy-start(s32[128,448]{0,1:T(8,128)} %param.14) | copy-start | bytes 688132
  25.6 7.1 %copy-start.11 = (s32[112,512]{1,0:T(8,128)S(1)}, s32[112,512]{1,0:T(8,128)}, u32[]{:S(2)}) copy-start(s32[112,512]{1,0:T(8,128)} %refs_2_) | copy-start | bytes 688132
  26.5 6.3 %copy-start.6 = (bf16[512,448]{0,1:T(8,128)(2,1)S(1)}, bf16[512,448]{0,1:T(8,128)(2,1)}, u32[]{:S(2)}) copy-start(bf16[512,448]{0,1:T(8,128)(2,1)} %param.10) | copy-start | bytes 1376260
  26.5 6.3 %copy-start.7 = (bf16[512,448]{0,1:T(8,128)(2,1)S(1)}, bf16[512,448]{0,1:T(8,128)(2,1)}, u32[]{:S(2)}) copy-start(bf16[512,448]{0,1:T(8,128)(2,1)} %param.11) | copy-start | bytes 1376260
  26.5 12.3 %all-to-all-start.1 = ((bf16[4,8,2,8,512]{4,3,2,1,0:T(8,128)(2,1)}), bf16[4,8,2,8,512]{4,3,2,1,0:T(8,128)(2,1)S(1)}, u32[]{:S(2)}, u32[]{:S(2)}) async-start(bf16[4,8,2,8,512]{4,3,2,1,0:T(8,128)(2,1)} %shard_map.111), calls=%async_computation.1 | async-start | bytes 1048576 | tf_op jit(solution)/shard_map/all_to_all | solution.py:232
  34.2 0.8 copy-start
  35.0 0.8 copy-start.2
  35.7 0.8 copy-start.4
  36.5 0.8 copy-start.14
  37.3 0.8 copy-start.17
  38.0 9.7 %copy-start.12 = (bf16[448,512]{1,0:T(8,128)(2,1)}, bf16[448,512]{1,0:T(8,128)(2,1)S(1)}, u32[]{:S(2)}) copy-start(bf16[448,512]{1,0:T(8,128)(2,1)S(1)} %get-tuple-element.36.gate_ref) | copy-start | bytes 1376260
  38.7 4.0 %copy-start.15 = (bf16[448,512]{1,0:T(8,128)(2,1)S(1)}, bf16[448,512]{1,0:T(8,128)(2,1)}, u32[]{:S(2)}) copy-start(bf16[448,512]{1,0:T(8,128)(2,1)} %copy-done.14) | copy-start | bytes 1376260
  38.8 4.0 %copy-start.18 = (bf16[448,512]{1,0:T(8,128)(2,1)S(1)}, bf16[448,512]{1,0:T(8,128)(2,1)}, u32[]{:S(2)}) copy-start(bf16[448,512]{1,0:T(8,128)(2,1)} %copy-done.17) | copy-start | bytes 1376260
  38.8 3.9 %collective-permute-start = (bf16[2,256,512]{2,1,0:T(8,128)(2,1)S(1)}, bf16[2,256,512]{2,1,0:T(8,128)(2,1)S(1)}, u32[]{:S(2)}, u32[]{:S(2)}) collective-permute-start(bf16[2,256,512]{2,1,0:T(8,128)(2,1)S(1)} %bitcast.49), channel_id=1, source_target_pairs={{0,1},{1,0},{2,3},{3,2},{4,5},{5,4},{6,7},{7,6},{8,9},{9,8},{10,11... | collective-permute-start | bytes 1572872 | tf_op jit(solution)/shard_map/ppermute | solution.py:245
  44.3 15.6 %all-to-all-start.2 = ((s16[4,352,256]{2,1,0:T(8,128)(2,1)}), s16[4,352,256]{2,1,0:T(8,128)(2,1)S(1)}, u32[]{:S(2)}, u32[]{:S(2)}) async-start(s16[4,352,256]{2,1,0:T(8,128)(2,1)} %shard_map.114), calls=%async_computation.2 | async-start | bytes 1441792 | tf_op jit(solution)/shard_map/all_to_all | solution.py:258
  47.8 1.0 copy-start.19
  60.2 35.7 %all-to-all-start.3 = ((s16[4,352,256]{2,1,0:T(8,128)(2,1)}), s16[4,352,256]{2,1,0:T(8,128)(2,1)S(1)}, u32[]{:S(2)}, u32[]{:S(2)}) async-start(s16[4,352,256]{2,1,0:T(8,128)(2,1)} %shard_map.113), calls=%async_computation.3 | async-start | bytes 1441792 | tf_op jit(solution)/shard_map/all_to_all | solution.py:262
  63.7 32.2 %collective-permute-start.1 = (s16[352,256]{1,0:T(8,128)(2,1)S(1)}, s16[352,256]{1,0:T(8,128)(2,1)S(1)}, u32[]{:S(2)}, u32[]{:S(2)}) collective-permute-start(s16[352,256]{1,0:T(8,128)(2,1)S(1)} %shard_map.115), channel_id=1, source_target_pairs={{0,256},{1,769},{256,0},{257,513},{512,768},{513,257},{768,512},{7... | collective-permute-start | bytes 540680 | tf_op jit(solution)/shard_map/ppermute | solution.py:39
  96.1 20.0 %collective-permute-start.2 = (s16[352,256]{1,0:T(8,128)(2,1)S(1)}, s16[352,256]{1,0:T(8,128)(2,1)S(1)}, u32[]{:S(2)}, u32[]{:S(2)}) collective-permute-start(s16[352,256]{1,0:T(8,128)(2,1)S(1)} %get-tuple-element.43), channel_id=1, source_target_pairs={{0,768},{1,257},{256,512},{257,1},{512,256},{513,769},{768,0},{769... | collective-permute-start | bytes 540680 | tf_op jit(solution)/shard_map/ppermute | solution.py:39
  117.1 23.3 %collective-permute-start.3 = (bf16[336,256]{1,0:T(8,128)(2,1)S(1)}, bf16[336,256]{1,0:T(8,128)(2,1)S(1)}, u32[]{:S(2)}, u32[]{:S(2)}) collective-permute-start(bf16[336,256]{1,0:T(8,128)(2,1)S(1)} %get-tuple-element.45), channel_id=1, source_target_pairs={{0,256},{1,769},{256,0},{257,513},{512,768},{513,257},{768,512},{7... | collective-permute-start | bytes 516104 | tf_op jit(solution)/shard_map/ppermute | solution.py:39
  127.0 15.9 %all-to-all-start.4 = ((bf16[4,336,256]{2,1,0:T(8,128)(2,1)}), bf16[4,336,256]{2,1,0:T(8,128)(2,1)S(1)}, u32[]{:S(2)}, u32[]{:S(2)}) async-start(bf16[4,336,256]{2,1,0:T(8,128)(2,1)} %get-tuple-element.44), calls=%async_computation.4 | async-start | bytes 1376256 | tf_op jit(solution)/shard_map/all_to_all | solution.py:270
  143.0 14.6 %copy-start.13 = (bf16[448,512]{1,0:T(8,128)(2,1)S(1)}, bf16[448,512]{1,0:T(8,128)(2,1)}, u32[]{:S(2)}) copy-start(bf16[448,512]{1,0:T(8,128)(2,1)} %copy-done.12) | copy-start | bytes 1376260
  143.0 14.6 %copy-start.16 = (bf16[448,512]{1,0:T(8,128)(2,1)S(1)}, bf16[448,512]{1,0:T(8,128)(2,1)}, u32[]{:S(2)}) copy-start(bf16[448,512]{1,0:T(8,128)(2,1)} %copy-done.14) | copy-start | bytes 1376260
  158.3 3.8 %collective-permute-start.4 = (f32[256,512]{1,0:T(8,128)S(1)}, f32[256,512]{1,0:T(8,128)S(1)}, u32[]{:S(2)}, u32[]{:S(2)}) collective-permute-start(f32[256,512]{1,0:T(8,128)S(1)} %get-tuple-element.47), channel_id=1, source_target_pairs={{0,1},{1,0},{2,3},{3,2},{4,5},{5,4},{6,7},{7,6},{8,9},{9,8},{10,11... | collective-permute-start | bytes 1572872 | tf_op jit(solution)/shard_map/ppermute | solution.py:280
  163.0 11.6 %all-to-all-start.6 = ((s16[4,80,512]{2,1,0:T(8,128)(2,1)}), s16[4,80,512]{2,1,0:T(8,128)(2,1)S(1)}, u32[]{:S(2)}, u32[]{:S(2)}) async-start(s16[4,80,512]{2,1,0:T(8,128)(2,1)} %shard_map.120), calls=%async_computation.6 | async-start | bytes 655360 | tf_op jit(solution)/shard_map/all_to_all | solution.py:283
  168.6 1.0 copy-start.22
  174.6 13.7 %copy-start.21 = (bf16[2,256,512]{2,1,0:T(8,128)(2,1)S(1)}, bf16[2,256,512]{2,1,0:T(8,128)(2,1)}, u32[]{:S(2)}) copy-start(bf16[2,256,512]{2,1,0:T(8,128)(2,1)} %get-tuple-element.54) | copy-start | bytes 1572868
  175.4 24.4 %all-to-all-start.7 = ((f32[8,8,512]{2,1,0:T(8,128)}), f32[8,8,512]{2,1,0:T(8,128)S(1)}, u32[]{:S(2)}, u32[]{:S(2)}) async-start(f32[8,8,512]{2,1,0:T(8,128)} %shard_map.121), calls=%async_computation.7 | async-start | bytes 262144 | tf_op jit(solution)/shard_map/all_to_all | solution.py:285
  188.2 1.2 copy-start.20
  188.2 1.3 copy-start.5
  189.5 1.1 copy-start.3
  190.6 1.1 copy-start.1
